TPU v7x, 32 devices: a whole 2x2x4 slice. The times are simulated.
32 devices in a mesh: grp: 2 (over y), seq: 4 (over z), head: 2 (over x), sub: 2 (over core).
Axes of the slice: x: 2, y: 2, z: 4, core: 2. Of those that a mesh axis runs over, the one named last changes fastest.
Arguments:
- hidden: bfloat16 [2048, 4096], P(('grp', 'seq'), ('head', 'sub')), parts along dimension 0, may hold values from -6 to 6
- inner_values: bfloat16 [2048, 8192], P(('grp', 'seq'), ('head', 'sub')), parts along dimension 0, may hold values from -0.29882812 to 0.29882812
- log_decay: float32 [2048, 128], P(('grp', 'seq'), ('head', 'sub')), parts along dimension 0, may hold values from -2 to 0
- skip_gain: float32 [128], P(('head', 'sub')), may hold values from 0.1 to 10
- cotangent: bfloat16 [2048, 8192], P(('grp', 'seq'), ('head', 'sub')), parts along dimension 0, may hold values from -6 to 6
- master: float32 [4096, 2048], P('seq', ('head', 'sub')), may hold values from -0.4 to 0.4
- mask_now: int32 [1024, 2048], P('seq', ('head', 'sub')), may hold values from 0 to 5
- mask_next: int32 [1024, 2048], P('seq', ('head', 'sub')), may hold values from 0 to 5
Outputs:
- ssd_output: bfloat16 [2048, 8192], P(('grp', 'seq'), ('head', 'sub')), parts along dimension 0
- new_weight: float32 [8192, 2048], P(('grp', 'seq'), ('head', 'sub')), parts along dimension 0
- sparse_weight: bfloat16 [8192, 2048], P(('grp', 'seq'), ('head', 'sub')), parts along dimension 0
There are 2 independent parts, one for each index of `grp`. A program takes and returns all parts, laid end to end along the dimension named above; an argument that names none is the same for every part. Nothing has to cross between parts.
All inputs are finite; a program needn't handle non-finite values.
Results may differ from a plain program's by a relative error of at most 0.033.
Values may be sent and summed in bfloat16 or wider, within the bound.
No kernel may reach another device: no remote copies, remote signals or barrier semaphores. Data moves between devices by JAX's collectives and lax.ppermute only.
A program may use at most 128 MiB of HBM per device.

v0:
```python
import functools
import math

import jax
import jax.numpy as jnp
from jax import lax
from jax.experimental import pallas as pl
from jax.experimental.pallas import tpu as pltpu
from jax.sharding import PartitionSpec as P

D = 4096
STATE = 128
SPAN = 256
LEARN_RATE = 0.05
WEIGHT_DECAY = 10.0
WEIGHT_SCALE = 2.0 / math.sqrt(D)
KEEP_BITS = (0b000111, 0b011001, 0b101010, 0b110100)
OUT_OF_SIGHT = -1e30
MIB = 1024 * 1024

F32 = jnp.float32
BF16 = jnp.bfloat16
NT = (((1,), (1,)), ((), ()))


def call(kernel, out_shape, flops, moved, exps=0, vmem=16 * MIB, **more):
    return pl.pallas_call(
        kernel,
        out_shape=out_shape,
        compiler_params=pltpu.CompilerParams(vmem_limit_bytes=vmem),
        cost_estimate=pl.CostEstimate(flops=flops, bytes_accessed=moved, transcendentals=exps),
        **more,
    )


def dot(a, b):
    return jnp.dot(a, b, preferred_element_type=F32)


def dot_nt(a, b):
    return lax.dot_general(a, b, NT, preferred_element_type=F32)


def turned(a):
    return a.astype(F32).T.astype(BF16)


def expanded(codes, rows):
    spread = (
        lax.broadcasted_iota(jnp.int32, (rows, rows // 4), 0) // 4
        == lax.broadcasted_iota(jnp.int32, (rows, rows // 4), 1)
    ).astype(F32)
    code = dot(spread.astype(BF16), codes.astype(F32).astype(BF16)).astype(jnp.int32)
    place = lax.broadcasted_iota(jnp.int32, (rows, 1), 0) % 4
    bits = jnp.where(
        place < 2,
        jnp.where(place == 0, KEEP_BITS[0], KEEP_BITS[1]),
        jnp.where(place == 2, KEEP_BITS[2], KEEP_BITS[3]),
    )
    return lax.shift_right_logical(jnp.broadcast_to(bits, code.shape), code) & 1


def weights_kernel(master_ref, now_ref, next_ref, effective_ref, decayed_ref, keep_ref):
    rows = master_ref.shape[0]
    master = master_ref[...]
    kept = expanded(now_ref[...], rows) == 1
    effective_ref[...] = jnp.where(kept, master * WEIGHT_SCALE, 0.0).astype(BF16)
    decayed_ref[...] = jnp.where(kept, master, master * (1.0 - LEARN_RATE * WEIGHT_DECAY))
    keep_ref[...] = expanded(next_ref[...], rows).astype(F32).astype(BF16)


def weights(master, mask_now, mask_next):
    rows, columns = master.shape
    block = min(rows, 256)
    full = pl.BlockSpec((block, columns), lambda i: (i, 0))
    quarter = pl.BlockSpec((block // 4, columns), lambda i: (i, 0))
    return call(
        weights_kernel,
        (
            jax.ShapeDtypeStruct((rows, columns), BF16),
            jax.ShapeDtypeStruct((rows, columns), F32),
            jax.ShapeDtypeStruct((rows, columns), BF16),
        ),
        flops=rows * columns * 3000,
        moved=rows * columns * 14,
        grid=(rows // block,),
        in_specs=[full, quarter, quarter],
        out_specs=(full, full, full),
    )(master, mask_now, mask_next)


def effective_kernel(master_ref, now_ref, effective_ref):
    kept = expanded(now_ref[...], master_ref.shape[0]) == 1
    effective_ref[...] = jnp.where(kept, master_ref[...] * WEIGHT_SCALE, 0.0).astype(BF16)


def effective_of(master, mask_now):
    rows, columns = master.shape
    block = min(rows, 256)
    full = pl.BlockSpec((block, columns), lambda i: (i, 0))
    return call(
        effective_kernel,
        jax.ShapeDtypeStruct((rows, columns), BF16),
        flops=rows * columns * 3000,
        moved=rows * columns * 7,
        grid=(rows // block,),
        in_specs=[full, pl.BlockSpec((block // 4, columns), lambda i: (i, 0))],
        out_specs=full,
    )(master, mask_now)


def lanes_of(left, right, wide):
    lane = lax.broadcasted_iota(jnp.int32, (left.shape[0], wide), 1)
    return jnp.where(lane < wide // 2, left, right)


def decays_of(col, row):
    half = SPAN // 2
    causal = lax.broadcasted_iota(jnp.int32, (half, half), 0) >= lax.broadcasted_iota(
        jnp.int32, (half, half), 1
    )
    top = jnp.exp(jnp.where(causal, col[:half] - row[:, :half], OUT_OF_SIGHT))
    low = jnp.exp(col[half:] - row[:, :half])
    end = jnp.exp(jnp.where(causal, col[half:] - row[:, half:], OUT_OF_SIGHT))
    return top, low, end


def before_kernel(
    x_ref, dy_ref, logt_ref,
    xd_ref, yd_ref, mix_ref, mixt_ref, cum_ref, cumt_ref, end_ref, tall_ref,
):
    heads = cum_ref.shape[2]
    half = SPAN // 2
    wide = x_ref.shape[1] // heads * 2
    row = lax.broadcasted_iota(jnp.int32, (SPAN, SPAN), 0)
    col = lax.broadcasted_iota(jnp.int32, (SPAN, SPAN), 1)
    first = pl.multiple_of(pl.program_id(0) * heads, heads)
    cumt = jnp.dot(
        logt_ref[pl.ds(first, heads), :], (row <= col).astype(F32),
        precision=lax.Precision.HIGHEST, preferred_element_type=F32,
    )
    tall_ref[...] = jnp.zeros_like(tall_ref)
    tall_ref[:heads, :] = cumt
    cum = tall_ref[...].T[:, :heads]
    cum_ref[0] = cum
    cumt_ref[0] = cumt
    end = cum[SPAN - 1 :, :]
    from_start = jnp.exp(cum)
    to_end = jnp.exp(end - cum)
    whole = jnp.exp(end)
    mix = [jnp.zeros((half, half), F32) for _ in range(3)]
    lane = lax.broadcasted_iota(jnp.int32, (SPAN, wide), 1)
    for pair in range(heads // 2):
        a, b = 2 * pair, 2 * pair + 1
        cut = slice(pair * wide, (pair + 1) * wide)
        x = x_ref[:, cut]
        dy = dy_ref[:, cut]
        wide_dy = dy.astype(F32)
        xd_ref[:, cut] = (
            x.astype(F32) * lanes_of(to_end[:, a : a + 1], to_end[:, b : b + 1], wide)
        ).astype(BF16)
        yd_ref[:, cut] = (
            wide_dy * lanes_of(from_start[:, a : a + 1], from_start[:, b : b + 1], wide)
        ).astype(BF16)
        end_ref[0, :, cut] = lanes_of(whole[:, a : a + 1], whole[:, b : b + 1], wide)
        for head, mine in ((a, lane < wide // 2), (b, lane >= wide // 2)):
            one = jnp.where(mine, wide_dy, 0.0).astype(BF16)
            decays = decays_of(cum[:, head : head + 1], cumt[head : head + 1, :])
            mix[0] += dot_nt(one[:half], x[:half]) * decays[0]
            both = dot_nt(one[half:], x)
            mix[1] += both[:, :half] * decays[1]
            mix[2] += both[:, half:] * decays[2]
    nothing = jnp.zeros((half, half), BF16)
    top, low, end_mix = (m.astype(BF16) for m in mix)
    topt, lowt, end_mixt = (m.T.astype(BF16) for m in mix)
    mix_ref[0, :half, :half] = top
    mix_ref[0, :half, half:] = nothing
    mix_ref[0, half:, :half] = low
    mix_ref[0, half:, half:] = end_mix
    mixt_ref[0, :half, :half] = topt
    mixt_ref[0, :half, half:] = lowt
    mixt_ref[0, half:, :half] = nothing
    mixt_ref[0, half:, half:] = end_mixt


def wide_spec(width):
    return pl.BlockSpec((SPAN, width), lambda g: (0, g))


def lead_spec(*shape):
    return pl.BlockSpec((1, *shape), lambda g: (g, *(0 for _ in shape)))


def before(values, cotan, logs_t, groups):
    heads = logs_t.shape[0] // groups
    width = values.shape[1] // groups
    wide = wide_spec(width)
    return call(
        before_kernel,
        (
            jax.ShapeDtypeStruct(values.shape, BF16),
            jax.ShapeDtypeStruct(values.shape, BF16),
            jax.ShapeDtypeStruct((groups, SPAN, SPAN), BF16),
            jax.ShapeDtypeStruct((groups, SPAN, SPAN), BF16),
            jax.ShapeDtypeStruct((groups, SPAN, heads), F32),
            jax.ShapeDtypeStruct((groups, heads, SPAN), F32),
            jax.ShapeDtypeStruct((groups, 1, width), F32),
        ),
        flops=groups * heads * SPAN * SPAN * 2500,
        moved=values.size * 8,
        exps=groups * heads * SPAN * SPAN,
        grid=(groups,),
        in_specs=[wide, wide, pl.BlockSpec(logs_t.shape, lambda g: (0, 0))],
        out_specs=(
            wide, wide, lead_spec(SPAN, SPAN), lead_spec(SPAN, SPAN),
            lead_spec(SPAN, heads), lead_spec(heads, SPAN), lead_spec(1, width),
        ),
        scratch_shapes=[pltpu.VMEM((STATE, SPAN), F32)],
    )(values, cotan, logs_t)


def partial_kernel(spread, *refs):
    given = refs[:-1] if spread else refs
    (*pieces, weight_ref, sibling_weight_ref, out_ref, sibling_out_ref) = given
    pieces = [piece[...] for piece in pieces]
    if spread:
        refs[-1][...] = pieces[-2] + pieces[-1]
        pieces[-2:] = [refs[-1][...]]
    start = 0
    for piece in pieces:
        rows = slice(start, start + piece.shape[0])
        start += piece.shape[0]
        out_ref[rows, :] = dot(piece, weight_ref[...]).astype(BF16)
        sibling_out_ref[rows, :] = dot(piece, sibling_weight_ref[...]).astype(BF16)


def partials(pieces, effective, sibling_effective, spread=False):
    rows = sum(piece.shape[0] for piece in pieces[: -1 if spread else None])
    columns = effective.shape[1]
    whole = pl.BlockSpec(memory_space=pltpu.VMEM)
    shapes = [jax.ShapeDtypeStruct((rows, columns), BF16)] * 2
    if spread:
        shapes.append(jax.ShapeDtypeStruct(pieces[-1].shape, BF16))
    return call(
        functools.partial(partial_kernel, spread),
        tuple(shapes),
        flops=4 * rows * effective.size,
        moved=(rows * effective.shape[0] + 2 * effective.size + 2 * rows * columns) * 2,
        in_specs=[whole] * (len(pieces) + 2),
        out_specs=(whole,) * len(shapes),
    )(*pieces, effective, sibling_effective)


def turn_kernel(*refs):
    (*pieces, out_ref) = refs
    start = 0
    for piece in pieces:
        out_ref[:, start : start + piece.shape[0]] = turned(piece[...])
        start += piece.shape[0]


def turn(pieces):
    rows, features = sum(piece.shape[0] for piece in pieces), pieces[0].shape[1]
    whole = pl.BlockSpec(memory_space=pltpu.VMEM)
    return call(
        turn_kernel,
        jax.ShapeDtypeStruct((features, rows), BF16),
        flops=rows * features * 2000,
        moved=rows * features * 4,
        in_specs=[whole] * len(pieces),
        out_specs=whole,
    )(*pieces)


def either(ahead, first, second, body):
    if ahead:
        return body(first, second)
    lower = lax.axis_index("seq") < lax.axis_size("seq") // 2

    @pl.when(lower)
    def _():
        body(first, second)

    @pl.when(jnp.logical_not(lower))
    def _():
        body(second, first)


def states_kernel(both, *refs):
    (*terms, xd_ref, yd_ref, proj_ref, near_low_ref, near_ref, far_ref) = refs
    total = terms[0][...].astype(F32)
    for term in terms[1:]:
        total += term[...].astype(F32)
    low = total.astype(BF16)
    proj_ref[...] = low
    state = dot(turned(low[:, :STATE]), xd_ref[...])
    adjoint = dot(turned(low[:, STATE:]), yd_ref[...])

    def put(near, far):
        near_low_ref[0] = near.astype(BF16)
        near_ref[0] = near
        far_ref[0] = far

    either(both, state, adjoint, put)


def states(ahead, terms, xd, yd, first, groups, width):
    pair = pl.BlockSpec((SPAN, 2 * STATE), lambda g: (0, g))
    pair_from = pl.BlockSpec((SPAN, 2 * STATE), lambda g: (0, g + first))
    wide = pl.BlockSpec((SPAN, width), lambda g: (0, g + first))
    lead = lead_spec(STATE, width)
    shape = (groups, STATE, width)
    return call(
        functools.partial(states_kernel, ahead),
        (
            jax.ShapeDtypeStruct((SPAN, groups * 2 * STATE), BF16),
            jax.ShapeDtypeStruct(shape, BF16),
            jax.ShapeDtypeStruct(shape, F32),
            jax.ShapeDtypeStruct(shape, F32),
        ),
        flops=4 * SPAN * groups * width * STATE,
        moved=groups * SPAN * (width * 4 + 4 * STATE * 5),
        grid=(groups,),
        in_specs=[pair_from] * len(terms) + [wide, wide],
        out_specs=(pair, lead, lead, lead),
    )(*terms, xd, yd)


def added(refs):
    total = refs[0][0]
    for ref in refs[1:]:
        total += ref[0]
    return total


def message_kernel(decay_ref, arrived_ref, own_ref, out_ref):
    out_ref[0] = (decay_ref[0] * arrived_ref[0].astype(F32) + own_ref[0]).astype(BF16)


def handed_on(decay, arrived, own, first):
    groups, _, width = arrived.shape
    lead = lead_spec(STATE, width)
    return call(
        message_kernel,
        jax.ShapeDtypeStruct(arrived.shape, BF16),
        flops=2 * arrived.size,
        moved=8 * arrived.size,
        grid=(groups,),
        in_specs=[pl.BlockSpec((1, 1, width), lambda g: (g + first, 0, 0)), lead, lead],
        out_specs=lead,
    )(decay, arrived, own)


def grads_kernel(ahead, proj_ref, xd_ref, yd_ref, mix_ref, mixt_ref, near_ref, *refs):
    (*far_refs, out_ref) = refs

    def body(start, adjoint):
        write, read = proj_ref[:, :STATE], proj_ref[:, STATE:]
        grad_write = dot(mixt_ref[0], read) + dot_nt(xd_ref[...], added(adjoint))
        grad_read = dot(mix_ref[0], write) + dot_nt(yd_ref[...], added(start))
        out_ref[:, :STATE] = grad_write.astype(BF16)
        out_ref[:, STATE:] = grad_read.astype(BF16)

    either(ahead, [near_ref], far_refs, body)


def grads(ahead, proj, xd, yd, mix, mixt, near, far, first):
    groups, _, width = near.shape
    pair = pl.BlockSpec((SPAN, 2 * STATE), lambda g: (0, g))
    wide = pl.BlockSpec((SPAN, width), lambda g: (0, g + first))
    square = pl.BlockSpec((1, SPAN, SPAN), lambda g: (g + first, 0, 0))
    return call(
        functools.partial(grads_kernel, ahead),
        jax.ShapeDtypeStruct(proj.shape, BF16),
        flops=4 * SPAN * groups * (width + SPAN) * STATE,
        moved=groups * SPAN * width * 8,
        grid=(groups,),
        in_specs=[pair, wide, wide, square, square]
        + [lead_spec(STATE, width)] * (1 + len(far)),
        out_specs=pair,
    )(proj, xd, yd, mix, mixt, near, *far)


def output_kernel(parts, hops, ahead, skip_ref, x_ref, cum_ref, cumt_ref, *refs):
    (*refs, out_ref, proj_ref, start_ref) = refs
    projs, nears = refs[:parts], refs[parts : 2 * parts]
    fars = [refs[2 * parts + hops * p : 2 * parts + hops * (p + 1)] for p in range(parts)]
    each = projs[0].shape[1] // (2 * STATE)
    for group in range(parts * each):
        part, at = divmod(group, each)

        @pl.when(pl.program_id(0) == group)
        def _(part=part, at=at):
            proj_ref[...] = projs[part][:, at * 2 * STATE : (at + 1) * 2 * STATE]

            def put(start, _):
                start_ref[...] = added([ref.at[at : at + 1] for ref in start])

            either(ahead, [nears[part]], fars[part], put)

    heads = cum_ref.shape[2]
    half = SPAN // 2
    wide = x_ref.shape[1] // heads * 2
    write = proj_ref[:, :STATE]
    read = proj_ref[:, STATE:]
    cum = cum_ref[0]
    cumt = cumt_ref[0]
    from_start = jnp.exp(cum)
    scores = dot_nt(read, write)
    top, low, end = scores[:half, :half], scores[half:, :half], scores[half:, half:]
    lane = lax.broadcasted_iota(jnp.int32, (half, wide), 1)
    for pair in range(heads // 2):
        a, b = 2 * pair, 2 * pair + 1
        cut = slice(pair * wide, (pair + 1) * wide)
        x = x_ref[:, cut]
        upper, lower = [], []
        for head in (a, b):
            decays = decays_of(cum[:, head : head + 1], cumt[head : head + 1, :])
            upper.append(dot((top * decays[0]).astype(BF16), x[:half]))
            lower.append(
                dot((low * decays[1]).astype(BF16), x[:half])
                + dot((end * decays[2]).astype(BF16), x[half:])
            )
        carried = dot(read, start_ref[:, cut]) * lanes_of(
            from_start[:, a : a + 1], from_start[:, b : b + 1], wide
        )
        head = pl.program_id(0) * heads + a
        gain = jnp.where(
            lax.broadcasted_iota(jnp.int32, (1, wide), 1) < wide // 2,
            skip_ref[head], skip_ref[head + 1],
        )
        rest = carried + gain * x.astype(F32)
        out_ref[:half, cut] = (
            jnp.where(lane < wide // 2, upper[0], upper[1]) + rest[:half]
        ).astype(BF16)
        out_ref[half:, cut] = (
            jnp.where(lane < wide // 2, lower[0], lower[1]) + rest[half:]
        ).astype(BF16)


def output(ahead, values, cum, cumt, skip, projs, nears, fars):
    groups, _, heads = cum.shape
    width = values.shape[1] // groups
    wide = wide_spec(width)
    pieces = [*projs, *nears, *(ref for far in fars for ref in far)]
    return call(
        functools.partial(output_kernel, len(projs), len(fars[0]), ahead),
        jax.ShapeDtypeStruct(values.shape, BF16),
        flops=groups * heads * SPAN * SPAN * 2000,
        moved=values.size * 5,
        exps=groups * heads * SPAN * SPAN,
        grid=(groups,),
        in_specs=[
            pl.BlockSpec(memory_space=pltpu.SMEM), wide, lead_spec(SPAN, heads),
            lead_spec(heads, SPAN),
        ]
        + [pl.BlockSpec(memory_space=pltpu.VMEM)] * len(pieces),
        out_specs=wide,
        scratch_shapes=[
            pltpu.VMEM((SPAN, 2 * STATE), BF16), pltpu.VMEM((STATE, width), BF16)
        ],
    )(skip, values, cum, cumt, *pieces)


def spot_of(block, spots):
    if spots == 1:
        return 0
    other_x = (lax.axis_index("head") != block % 2).astype(jnp.int32)
    other_core = (lax.axis_index("sub") != block // 2).astype(jnp.int32)
    return 2 * other_x + other_core


def update_kernel(blocks, spots, part, *refs):
    turned_refs, pieces = refs[:spots], refs[spots : spots + blocks]
    decayed_ref, keep_ref = refs[spots + blocks : spots + blocks + 2]
    weight_ref, sparse_ref, grad_ref, weight_out, sparse_out, sems = refs[-6:]
    tokens, width = pieces[0].shape
    rows = decayed_ref.shape[0]
    step = min(rows, 256)
    columns = slice(part * width, (part + 1) * width)
    for block, piece in enumerate(pieces):
        start = pl.multiple_of(spot_of(block, spots) * tokens, tokens)
        grad_ref[pl.ds(start, tokens), :] = piece[...]
    copies = []
    for number in range(rows // step):
        here = slice(number * step, (number + 1) * step)
        total = dot(turned_refs[0][here, :], grad_ref[:tokens, :])
        for spot in range(1, spots):
            total += dot(
                turned_refs[spot][here, :], grad_ref[spot * tokens : (spot + 1) * tokens, :]
            )
        weight = decayed_ref[here, columns] - (LEARN_RATE * WEIGHT_SCALE) * total
        weight_out[here, :] = weight
        sparse_out[here, :] = (weight * keep_ref[here, columns].astype(F32)).astype(BF16)
        for place, (source, target) in enumerate(
            ((weight_out, weight_ref), (sparse_out, sparse_ref))
        ):
            copies.append(
                pltpu.make_async_copy(
                    source.at[here, :], target.at[here, columns], sems.at[place, number]
                )
            )
            copies[-1].start()
    for copy in copies:
        copy.wait()


def update(turned_hidden, grad_blocks, decayed, keep, part, earlier, vmem):
    rows, columns = decayed.shape
    width = grad_blocks[0].shape[1]
    tokens = turned_hidden[0].shape[1]
    spots, blocks = len(turned_hidden), len(grad_blocks)
    earlier = earlier or ()
    whole, anywhere = pl.BlockSpec(memory_space=pltpu.VMEM), pl.BlockSpec(memory_space=pl.ANY)
    return call(
        functools.partial(update_kernel, blocks, spots, part),
        (jax.ShapeDtypeStruct((rows, columns), F32), jax.ShapeDtypeStruct((rows, columns), BF16)),
        flops=2 * spots * tokens * rows * width,
        moved=rows * width * 12 + spots * tokens * (rows + width) * 2,
        vmem=vmem,
        in_specs=[whole] * (spots + blocks + 2) + [anywhere] * len(earlier),
        out_specs=(anywhere, anywhere),
        scratch_shapes=[
            pltpu.VMEM((spots * tokens, width), BF16),
            pltpu.VMEM((rows, width), F32),
            pltpu.VMEM((rows, width), BF16),
            pltpu.SemaphoreType.DMA((2, rows // min(rows, 256))),
        ],
        input_output_aliases={spots + blocks + 2 + i: i for i in range(len(earlier))},
    )(*turned_hidden, *grad_blocks, decayed, keep, *earlier)


def held(after, *before):
    return lax.optimization_barrier((after, *before))[0]


def to_all(seq, distance):
    return [(source, (source + distance) % seq) for source in range(seq)]


def block_pairs(seq, near, same_core):
    return [
        (
            (z * 2 + x) * 2 + core,
            ((z + (x if near else 1 - x) + 2 * core) % seq * 2 + x) * 2
            + (core if same_core else 1 - core),
        )
        for z in range(seq)
        for x in range(2)
        for core in range(2)
    ]


def transpose_pairs(seq):
    stays, crosses, beside, onward = [], [], [], []
    for z in range(seq):
        for x in range(2):
            for core in range(2):
                layer = 2 * x + core
                distance = (z - layer) % seq
                source, step = ((z * 2 + way) * 2 + core for way in (x, 1 - x))
                target = (layer * 2 + distance % 2) * 2 + distance // 2
                if distance % 2 == x:
                    stays.append((source, target))
                else:
                    crosses.append((source, target))
                    beside.append((source, step))
                    onward.append((step, target))
    return stays, crosses, beside, onward


SWAP = [(0, 1), (1, 0)]


def chain(own, own_low, decay, seq, step):
    arrived = jnp.zeros_like(own_low)
    message = own_low
    first = 0 if step > 0 else seq - 1
    for hop in range(seq - 1):
        source = first + hop * step
        if hop:
            message = handed_on(decay, arrived, own, 0)
        arrived = arrived + lax.ppermute(message, "seq", [(source, source + step)])
    return arrived


def on_device_general(
    seq, hidden, inner_values, log_decay, skip_gain, cotangent, master, mask_now, mask_next
):
    groups = master.shape[1] // (2 * STATE)
    effective, decayed, keep = weights(master, mask_now, mask_next)
    features = lax.all_gather(hidden, ("head", "sub"), axis=1, tiled=True)
    layer = lax.all_to_all(features, "seq", split_axis=1, concat_axis=0, tiled=True)
    xd, yd, mix, mixt, cum, cumt, decay = before(
        inner_values, cotangent, log_decay.T, groups
    )
    part = dot(layer, effective).astype(BF16)
    terms = [lax.psum_scatter(part, "seq", scatter_dimension=0, tiled=True)]
    proj, state_low, state, adjoint = states(True, terms, xd, yd, 0, groups, decay.shape[2])
    start = chain(state, state_low, decay, seq, 1)
    adjoint_in = chain(adjoint, adjoint.astype(BF16), decay, seq, -1)
    grad = grads(True, proj, xd, yd, mix, mixt, start, [adjoint_in], 0)
    blocks = [lax.all_gather(grad, "seq", axis=0, tiled=True)]
    ssd_output = output(
        True, inner_values, cum, cumt, skip_gain, [proj], [start], [[adjoint_in]]
    )
    return ssd_output, *update([layer.T], blocks, decayed, keep, 0, None, 40 * MIB)


def on_device(
    seq, hidden, inner_values, log_decay, skip_gain, cotangent, master, mask_now, mask_next
):
    groups = master.shape[1] // (2 * STATE)
    axes = ("seq", "head", "sub")
    rows = hidden.shape[0] // 2
    stays, crosses, beside, onward = transpose_pairs(seq)
    relayed = lax.ppermute(hidden[rows:], axes, beside)
    top = lax.ppermute(hidden[:rows], axes, stays + crosses)
    low = [lax.ppermute(hidden[rows:], axes, stays), lax.ppermute(relayed, axes, onward)]
    effective, decayed, keep = weights(master, mask_now, mask_next)
    sibling_effective = effective_of(
        lax.ppermute(master, "sub", SWAP), lax.ppermute(mask_now, "sub", SWAP)
    )
    top = held(top, effective, sibling_effective)

    other = [lax.ppermute(top, "head", SWAP)]
    same, cross, low = partials([top, *low], effective, sibling_effective, True)
    other.append(lax.ppermute(low, "head", SWAP))
    terms = [
        lax.ppermute(same, axes, block_pairs(seq, True, True)),
        lax.ppermute(cross, axes, block_pairs(seq, True, False)),
    ]
    same, cross = partials(other, effective, sibling_effective)
    terms += [
        lax.ppermute(same, axes, block_pairs(seq, False, True)),
        lax.ppermute(cross, axes, block_pairs(seq, False, False)),
    ]

    xd, yd, mix, mixt, cum, cumt, decay = before(
        held(inner_values, same), cotangent, log_decay.T, groups
    )

    each = groups // PARTS
    spans = range(PARTS)
    projs, messages, nears, fars = zip(
        *(
            states(None, terms, xd, yd, p * each, each, decay.shape[2])
            for p in spans
        )
    )
    turned_hidden = []
    for first, second in ((top, low), other):
        piece = turn([held(first, nears[0]), second])
        turned_hidden += [piece, lax.ppermute(piece, "sub", SWAP)]
    fars = [*fars[:-1], held(fars[-1], *turned_hidden)]
    arrived = [[] for _ in spans]
    hops = (([(0, 1), (3, 2)], nears), ([(1, 2), (2, 1)], fars), ([(1, 0), (2, 3)], None))
    messages = list(messages)
    for pairs, own_terms in hops:
        for p in spans:
            message = messages[p]
            if p and not arrived[p]:
                message = held(message, arrived[p - 1][-1])
            arrived[p].append(lax.ppermute(message, "seq", pairs))
        for p in spans:
            if own_terms:
                messages[p] = handed_on(decay, arrived[p][-1], own_terms[p], p * each)
    blocks = []
    for p in spans:
        grad = grads(
            None, projs[p], xd, yd, mix, mixt, arrived[p][0], arrived[p][1:], p * each
        )
        blocks.append([grad])
        for distance in range(1, seq):
            pairs = to_all(seq, seq - distance)
            blocks[p].append(lax.ppermute(grad, "seq", pairs))

    decayed = held(decayed, blocks[-1][0])
    updated = None
    for p in spans:
        updated = update(turned_hidden, blocks[p], decayed, keep, p, updated, 16 * MIB)
        if not p:
            cum = held(cum, *updated)
    ssd_output = output(
        None, inner_values, cum, cumt, skip_gain,
        projs, [a[0] for a in arrived], [a[1:] for a in arrived],
    )
    return ssd_output, *updated


PARTS = 2


def solution(mesh):
    by_position = P(("grp", "seq"), ("head", "sub"))
    by_row = P("seq", ("head", "sub"))
    seq, head, sub = (mesh.shape[name] for name in ("seq", "head", "sub"))
    body = on_device if (seq, head, sub) == (4, 2, 2) else on_device_general
    return jax.shard_map(
        functools.partial(body, seq),
        mesh=mesh,
        in_specs=(
            by_position, by_position, by_position, P(("head", "sub")), by_position,
            by_row, by_row, by_row,
        ),
        out_specs=(by_position, by_position, by_position),
        check_vma=False,
    )
```

profile of v0, /device:TPU:0, one launch (start us, length us, event | category | flops | bytes accessed | tf_op | source)
XLA Modules:
  0.0 116.0 jit_solution(3290169025259057658)
XLA Ops:
  0.6 0.5 collective-permute-start.1
  1.1 0.1 collective-permute-start.2
  1.2 1.1 fusion
  2.3 1.3 %collective-permute-start.5 = (bf16[128,1024]{1,0:T(8,128)(2,1)S(1)}, bf16[128,1024]{1,0:T(8,128)(2,1)S(1)}, u32[]{:S(2)}, u32[]{:S(2)}) collective-permute-start(bf16[128,1024]{1,0:T(8,128)(2,1)S(1)} %get-tuple-element.73), channel_id=1, source_target_pairs={{1,3},{2,0},{4,6},{7,5},{9,11},{10,8},{12,14},{15,13},{17,19},{18,... | collective-permute-start | bytes 786440 | tf_op jit(solution)/shard_map/ppermute | solution.py:617
  3.6 0.7 collective-permute-start.4
  4.3 0.7 collective-permute-start
  5.0 5.9 %collective-permute-done.5 = bf16[128,1024]{1,0:T(8,128)(2,1)S(1)} collective-permute-done((bf16[128,1024]{1,0:T(8,128)(2,1)S(1)}, bf16[128,1024]{1,0:T(8,128)(2,1)S(1)}, u32[]{:S(2)}, u32[]{:S(2)}) %collective-permute-start.5) | collective-permute-done | bytes 262176 | tf_op jit(solution)/shard_map/ppermute | solution.py:617
  10.8 4.9 %collective-permute-start.6 = (bf16[128,1024]{1,0:T(8,128)(2,1)S(1)}, bf16[128,1024]{1,0:T(8,128)(2,1)S(1)}, u32[]{:S(2)}, u32[]{:S(2)}) collective-permute-start(bf16[128,1024]{1,0:T(8,128)(2,1)S(1)} %collective-permute-done.5), channel_id=1, source_target_pairs={{3,7},{0,9},{6,2},{5,13},{11,6},{8,8},{14,3},{13,12},{19,23},{16,2... | collective-permute-start | bytes 786440 | tf_op jit(solution)/shard_map/ppermute | solution.py:619
  15.8 1.6 %copy-done = f32[1024,512]{1,0:T(8,128)S(1)} copy-done((f32[1024,512]{1,0:T(8,128)S(1)}, f32[1024,512]{1,0:T(8,128)}, u32[]{:S(2)}) %copy-start) | copy-done | bytes 2097176
  17.3 1.0 copy-done.3
  18.4 1.0 copy-done.4
  19.4 1.7 %shard_map.103 = (bf16[1024,512]{1,0:T(8,128)(2,1)S(1)}, f32[1024,512]{1,0:T(8,128)S(1)}, bf16[1024,512]{1,0:T(8,128)(2,1)S(1)}) custom-call(f32[1024,512]{1,0:T(8,128)S(1)} %copy-done, s32[256,512]{1,0:T(8,128)S(1)} %copy-done.4, s32[256,512]{1,0:T(8,128)S(1)} %copy-done.3), custom_call_target="tpu_custom_call" | custom-call | flops 1572864000 | bytes 7340032 | tf_op jit(solution)/shard_map/pallas_call | solution.py:77
  21.1 1.2 %shard_map.104.refs_4_.refs_3_ = bf16[1024,512]{1,0:T(8,128)(2,1)S(1)} custom-call(f32[1024,512]{1,0:T(8,128)S(1)} %collective-permute-done.1.master_ref, s32[256,512]{1,0:T(8,128)S(1)} %collective-permute-done.2.now_ref), custom_call_target="tpu_custom_call" | custom-call | flops 1572864000 | bytes 3670016 | tf_op jit(solution)/shard_map/pallas_call | solution.py:101
  22.5 0.7 shard_map.105
  23.2 2.1 %collective-permute-start.7 = (bf16[128,1024]{1,0:T(8,128)(2,1)S(1)}, bf16[128,1024]{1,0:T(8,128)(2,1)S(1)}, u32[]{:S(2)}, u32[]{:S(2)}) collective-permute-start(bf16[128,1024]{1,0:T(8,128)(2,1)S(1)} %get-tuple-element.40.refs_1_), channel_id=1, source_target_pairs={{0,2},{2,0},{1,3},{3,1},{4,6},{6,4},{5,7},{7,5},{8,10},{10,8},{9,1... | collective-permute-start | bytes 786440 | tf_op jit(solution)/shard_map/ppermute | solution.py:628
  25.2 0.7 collective-permute-start.8
  25.9 7.2 %collective-permute-start.9 = (bf16[256,512]{1,0:T(8,128)(2,1)S(1)}, bf16[256,512]{1,0:T(8,128)(2,1)S(1)}, u32[]{:S(2)}, u32[]{:S(2)}) collective-permute-start(bf16[256,512]{1,0:T(8,128)(2,1)S(1)} %get-tuple-element.45), channel_id=1, source_target_pairs={{0,1},{1,8},{2,7},{3,14},{4,5},{5,12},{6,11},{7,2},{8,9},{9,0},{10... | collective-permute-start | bytes 786440 | tf_op jit(solution)/shard_map/ppermute | solution.py:631
  33.1 0.7 shard_map.106
  33.9 9.2 %collective-permute-start.10 = (bf16[256,512]{1,0:T(8,128)(2,1)S(1)}, bf16[256,512]{1,0:T(8,128)(2,1)S(1)}, u32[]{:S(2)}, u32[]{:S(2)}) collective-permute-start(bf16[256,512]{1,0:T(8,128)(2,1)S(1)} %get-tuple-element.41), channel_id=1, source_target_pairs={{0,4},{1,13},{2,2},{3,11},{4,8},{5,1},{6,6},{7,15},{8,12},{9,5},{1... | collective-permute-start | bytes 786440 | tf_op jit(solution)/shard_map/ppermute | solution.py:635
  43.1 5.2 %shard_map.107 = (bf16[256,2048]{1,0:T(8,128)(2,1)S(1)}, bf16[256,2048]{1,0:T(8,128)(2,1)S(1)}, bf16[2,256,256]{2,1,0:T(8,128)(2,1)S(1)}, bf16[2,256,256]{2,1,0:...) custom-call(bf16[256,2048]{1,0:T(8,128)(2,1)S(1)} %copy-done.2, ...), custom_call_target="tpu_custom_call" | custom-call | flops 5242880000 | bytes 4194304 | tf_op jit(solution)/shard_map/pallas_call | solution.py:198
  48.3 2.2 %collective-permute-done.9.refs_1_ = bf16[256,512]{1,0:T(8,128)(2,1)S(1)} collective-permute-done((bf16[256,512]{1,0:T(8,128)(2,1)S(1)}, bf16[256,512]{1,0:T(8,128)(2,1)S(1)}, u32[]{:S(2)}, u32[]{:S(2)}) %collective-permute-start.9) | collective-permute-done | bytes 262176 | tf_op jit(solution)/shard_map/ppermute | solution.py:631
  50.5 7.2 %collective-permute-done.11.refs_3_ = bf16[256,512]{1,0:T(8,128)(2,1)S(1)} collective-permute-done((bf16[256,512]{1,0:T(8,128)(2,1)S(1)}, bf16[256,512]{1,0:T(8,128)(2,1)S(1)}, u32[]{:S(2)}, u32[]{:S(2)}) %collective-permute-start.11) | collective-permute-done | bytes 262176 | tf_op jit(solution)/shard_map/ppermute | solution.py:636
  57.7 0.4 shard_map.108
  58.2 2.5 %collective-permute-start.14 = (bf16[1,128,1024]{2,1,0:T(8,128)(2,1)S(1)}, bf16[1,128,1024]{2,1,0:T(8,128)(2,1)S(1)}, u32[]{:S(2)}, u32[]{:S(2)}) collective-permute-start(bf16[1,128,1024]{2,1,0:T(8,128)(2,1)S(1)} %get-tuple-element.55), channel_id=1, source_target_pairs={{0,4},{12,8},{1,5},{13,9},{2,6},{14,10},{3,7},{15,11},{16,20},{28,... | collective-permute-start | bytes 786440 | tf_op jit(solution)/shard_map/ppermute | solution.py:664
  60.7 0.2 shard_map.109.refs_0_
  61.0 0.2 shard_map.110.refs_2_
  61.2 0.6 collective-permute-start.13
  61.8 0.4 shard_map.114
  62.2 3.3 %collective-permute-done.14.arrived_ref.near_ref.refs_2_ = bf16[1,128,1024]{2,1,0:T(8,128)(2,1)S(1)} collective-permute-done((bf16[1,128,1024]{2,1,0:T(8,128)(2,1)S(1)}, bf16[1,128,1024]{2,1,0:T(8,128)(2,1)S(1)}, u32[]{:S(2)}, u32[]{:S(2)}) %collective-permute-start.14) | collective-permute-done | bytes 262176 | tf_op jit(solution)/shard_map/ppermute | solution.py:664
  65.5 4.4 %collective-permute-start.20 = (bf16[1,128,1024]{2,1,0:T(8,128)(2,1)S(1)}, bf16[1,128,1024]{2,1,0:T(8,128)(2,1)S(1)}, u32[]{:S(2)}, u32[]{:S(2)}) collective-permute-start(bf16[1,128,1024]{2,1,0:T(8,128)(2,1)S(1)} %get-tuple-element.61), channel_id=1, source_target_pairs={{0,4},{12,8},{1,5},{13,9},{2,6},{14,10},{3,7},{15,11},{16,20},{28,... | collective-permute-start | bytes 786440 | tf_op jit(solution)/shard_map/ppermute | solution.py:664
  70.0 0.7 collective-permute-start.15
  70.7 3.1 %collective-permute-done.20.arrived_ref.near_ref.refs_3_ = bf16[1,128,1024]{2,1,0:T(8,128)(2,1)S(1)} collective-permute-done((bf16[1,128,1024]{2,1,0:T(8,128)(2,1)S(1)}, bf16[1,128,1024]{2,1,0:T(8,128)(2,1)S(1)}, u32[]{:S(2)}, u32[]{:S(2)}) %collective-permute-start.20) | collective-permute-done | bytes 262176 | tf_op jit(solution)/shard_map/ppermute | solution.py:664
  73.9 0.7 collective-permute-start.21
  74.7 1.3 %collective-permute-start.16 = (bf16[1,128,1024]{2,1,0:T(8,128)(2,1)S(1)}, bf16[1,128,1024]{2,1,0:T(8,128)(2,1)S(1)}, u32[]{:S(2)}, u32[]{:S(2)}) collective-permute-start(bf16[1,128,1024]{2,1,0:T(8,128)(2,1)S(1)} %shard_map.112), channel_id=1, source_target_pairs={{4,0},{8,12},{5,1},{9,13},{6,2},{10,14},{7,3},{11,15},{20,16},{24,... | collective-permute-start | bytes 786440 | tf_op jit(solution)/shard_map/ppermute | solution.py:664
  76.1 1.3 %collective-permute-start.22 = (bf16[1,128,1024]{2,1,0:T(8,128)(2,1)S(1)}, bf16[1,128,1024]{2,1,0:T(8,128)(2,1)S(1)}, u32[]{:S(2)}, u32[]{:S(2)}) collective-permute-start(bf16[1,128,1024]{2,1,0:T(8,128)(2,1)S(1)} %shard_map.116), channel_id=1, source_target_pairs={{4,0},{8,12},{5,1},{9,13},{6,2},{10,14},{7,3},{11,15},{20,16},{24,... | collective-permute-start | bytes 786440 | tf_op jit(solution)/shard_map/ppermute | solution.py:664
  77.4 12.0 %collective-permute-done.16.refs_1_.refs_5_ = bf16[1,128,1024]{2,1,0:T(8,128)(2,1)S(1)} collective-permute-done((bf16[1,128,1024]{2,1,0:T(8,128)(2,1)S(1)}, bf16[1,128,1024]{2,1,0:T(8,128)(2,1)S(1)}, u32[]{:S(2)}, u32[]{:S(2)}) %collective-permute-start.16) | collective-permute-done | bytes 262176 | tf_op jit(solution)/shard_map/ppermute | solution.py:664
  89.4 0.6 shard_map.113.refs_4_
  90.0 0.9 collective-permute-start.17
  90.8 0.6 collective-permute-start.18
  91.4 1.7 %collective-permute-start.19 = (bf16[256,256]{1,0:T(8,128)(2,1)S(1)}, bf16[256,256]{1,0:T(8,128)(2,1)S(1)}, u32[]{:S(2)}, u32[]{:S(2)}) collective-permute-start(bf16[256,256]{1,0:T(8,128)(2,1)S(1)} %shard_map.113.refs_4_), channel_id=1, source_target_pairs={{0,4},{4,8},{8,12},{12,0},{1,5},{5,9},{9,13},{13,1},{2,6},{6,10},{... | collective-permute-start | bytes 393224 | tf_op jit(solution)/shard_map/ppermute | solution.py:676
  93.1 6.1 %collective-permute-done.22.refs_1_.refs_7_ = bf16[1,128,1024]{2,1,0:T(8,128)(2,1)S(1)} collective-permute-done((bf16[1,128,1024]{2,1,0:T(8,128)(2,1)S(1)}, bf16[1,128,1024]{2,1,0:T(8,128)(2,1)S(1)}, u32[]{:S(2)}, u32[]{:S(2)}) %collective-permute-start.22) | collective-permute-done | bytes 262176 | tf_op jit(solution)/shard_map/ppermute | solution.py:664
  99.3 0.6 shard_map.117.refs_4_
  99.9 6.9 %collective-permute-start.23 = (bf16[256,256]{1,0:T(8,128)(2,1)S(1)}, bf16[256,256]{1,0:T(8,128)(2,1)S(1)}, u32[]{:S(2)}, u32[]{:S(2)}) collective-permute-start(bf16[256,256]{1,0:T(8,128)(2,1)S(1)} %shard_map.117.refs_4_), channel_id=1, source_target_pairs={{0,12},{4,0},{8,4},{12,8},{1,13},{5,1},{9,5},{13,9},{2,14},{6,2},{... | collective-permute-start | bytes 393224 | tf_op jit(solution)/shard_map/ppermute | solution.py:676
  106.8 0.6 collective-permute-start.25
  107.4 1.8 %shard_map.118 = (f32[1024,512]{1,0:T(8,128)}, bf16[1024,512]{1,0:T(8,128)(2,1)}) custom-call(bf16[1024,256]{1,0:T(8,128)(2,1)S(1)} %shard_map.109.refs_0_, bf16[1024,256]{1,0:T(8,128)(2,1)S(1)} %collective-permute-done.12.refs_1_, bf16[1024,256]{1,0:T(8,128)(2,1)S(1)} %shard_map.110.refs_2_, bf16[1024,256]{1,0:T(8,128)(2,1)S(1)} %collective-permute-done.13.refs_3_, ...), custom_call_target="tpu_custom_call" | custom-call | flops 536870912 | bytes 5767168 | tf_op jit(solution)/shard_map/pallas_call | solution.py:515
  109.2 4.5 %shard_map.119 = bf16[256,2048]{1,0:T(8,128)(2,1)} custom-call(f32[32]{0:T(128)S(1)} %copy-done.6, bf16[256,2048]{1,0:T(8,128)(2,1)S(1)} %copy-done.2, f32[2,256,16]{2,1,0:T(8,128)S(1)} %get-tuple-element.69.cum_ref, f32[2,16,256]{2,1,0:T(8,128)S(1)} %get-tuple-element.70.cumt_ref, bf16[256,256]{1,0:T(8,128)(2,1)S(1)} %get-tuple-element.52.proj_ref.refs_0_, ...), custom_call_target="tpu_custom_call" | custom-call | flops 4194304000 | bytes 2621440 | tf_op jit(solution)/shard_map/pallas_call | solution.py:446
  113.7 0.3 collective-permute-done.24.refs_6_
  114.0 1.8 %shard_map.120 = (f32[1024,512]{1,0:T(8,128)}, bf16[1024,512]{1,0:T(8,128)(2,1)}) custom-call(bf16[1024,256]{1,0:T(8,128)(2,1)S(1)} %shard_map.109.refs_0_, bf16[1024,256]{1,0:T(8,128)(2,1)S(1)} %collective-permute-done.12.refs_1_, bf16[1024,256]{1,0:T(8,128)(2,1)S(1)} %shard_map.110.refs_2_, ...), custom_call_target="tpu_custom_call", output_to_operand_aliasing={{0}: (10, {}), {1}: (11, {})} | custom-call | flops 536870912 | bytes 5767168 | tf_op jit(solution)/shard_map/pallas_call | solution.py:515
  (37 shorter events, 0.5 us)
Async XLA Ops:
  0.6 20.5 %collective-permute-start.1 = (f32[1024,512]{1,0:T(8,128)}, f32[1024,512]{1,0:T(8,128)S(1)}, u32[]{:S(2)}, u32[]{:S(2)}) collective-permute-start(f32[1024,512]{1,0:T(8,128)} %master_ref.1), channel_id=1, source_target_pairs={{0,1},{1,0},{2,3},{3,2},{4,5},{5,4},{6,7},{7,6},{8,9},{9,8},{10,11... | collective-permute-start | bytes 6291464 | tf_op jit(solution)/shard_map/ppermute | solution.py:622
  1.1 20.0 %collective-permute-start.2 = (s32[256,512]{1,0:T(8,128)}, s32[256,512]{1,0:T(8,128)S(1)}, u32[]{:S(2)}, u32[]{:S(2)}) collective-permute-start(s32[256,512]{1,0:T(8,128)} %now_ref.1), channel_id=1, source_target_pairs={{0,1},{1,0},{2,3},{3,2},{4,5},{5,4},{6,7},{7,6},{8,9},{9,8},{10,11... | collective-permute-start | bytes 1572872 | tf_op jit(solution)/shard_map/ppermute | solution.py:622
  2.3 8.5 %collective-permute-start.5 = (bf16[128,1024]{1,0:T(8,128)(2,1)S(1)}, bf16[128,1024]{1,0:T(8,128)(2,1)S(1)}, u32[]{:S(2)}, u32[]{:S(2)}) collective-permute-start(bf16[128,1024]{1,0:T(8,128)(2,1)S(1)} %get-tuple-element.73), channel_id=1, source_target_pairs={{1,3},{2,0},{4,6},{7,5},{9,11},{10,8},{12,14},{15,13},{17,19},{18,... | collective-permute-start | bytes 786440 | tf_op jit(solution)/shard_map/ppermute | solution.py:617
  3.6 18.8 %collective-permute-start.4 = (bf16[128,1024]{1,0:T(8,128)(2,1)S(1)}, bf16[128,1024]{1,0:T(8,128)(2,1)S(1)}, u32[]{:S(2)}, u32[]{:S(2)}) collective-permute-start(bf16[128,1024]{1,0:T(8,128)(2,1)S(1)} %get-tuple-element.73), channel_id=1, source_target_pairs={{0,0},{3,14},{5,4},{6,11},{8,1},{11,15},{13,5},{14,10},{16,16},{19... | collective-permute-start | bytes 786440 | tf_op jit(solution)/shard_map/ppermute | solution.py:619
  4.3 18.0 %collective-permute-start = (bf16[128,1024]{1,0:T(8,128)(2,1)S(1)}, bf16[128,1024]{1,0:T(8,128)(2,1)S(1)}, u32[]{:S(2)}, u32[]{:S(2)}) collective-permute-start(bf16[128,1024]{1,0:T(8,128)(2,1)S(1)} %get-tuple-element.74), channel_id=1, source_target_pairs={{0,0},{3,14},{5,4},{6,11},{8,1},{11,15},{13,5},{14,10},{1,7},{2,9}... | collective-permute-start | bytes 786440 | tf_op jit(solution)/shard_map/ppermute | solution.py:618
  10.8 11.6 %collective-permute-start.6 = (bf16[128,1024]{1,0:T(8,128)(2,1)S(1)}, bf16[128,1024]{1,0:T(8,128)(2,1)S(1)}, u32[]{:S(2)}, u32[]{:S(2)}) collective-permute-start(bf16[128,1024]{1,0:T(8,128)(2,1)S(1)} %collective-permute-done.5), channel_id=1, source_target_pairs={{3,7},{0,9},{6,2},{5,13},{11,6},{8,8},{14,3},{13,12},{19,23},{16,2... | collective-permute-start | bytes 786440 | tf_op jit(solution)/shard_map/ppermute | solution.py:619
  15.7 1.6 %copy-start = (f32[1024,512]{1,0:T(8,128)S(1)}, f32[1024,512]{1,0:T(8,128)}, u32[]{:S(2)}) copy-start(f32[1024,512]{1,0:T(8,128)} %master_ref.1) | copy-start | bytes 6291460
  17.3 1.0 copy-start.3
  18.4 1.0 copy-start.4
  22.3 20.8 %copy-start.1 = (bf16[256,2048]{1,0:T(8,128)(2,1)S(1)}, bf16[256,2048]{1,0:T(8,128)(2,1)}, u32[]{:S(2)}) copy-start(bf16[256,2048]{1,0:T(8,128)(2,1)} %dy_ref.1) | copy-start | bytes 3145732
  22.3 20.8 %copy-start.2 = (bf16[256,2048]{1,0:T(8,128)(2,1)S(1)}, bf16[256,2048]{1,0:T(8,128)(2,1)}, u32[]{:S(2)}) copy-start(bf16[256,2048]{1,0:T(8,128)(2,1)} %x_ref.2) | copy-start | bytes 3145732
  22.3 20.8 %copy-start.5 = (f32[256,32]{0,1:T(8,128)S(1)}, f32[256,32]{0,1:T(8,128)}, u32[]{:S(2)}) copy-start(f32[256,32]{0,1:T(8,128)} %param.10) | copy-start | bytes 98308
  22.4 10.8 %collective-permute-start.3 = (bf16[128,1024]{1,0:T(8,128)(2,1)S(1)}, bf16[128,1024]{1,0:T(8,128)(2,1)S(1)}, u32[]{:S(2)}, u32[]{:S(2)}) collective-permute-start(bf16[128,1024]{1,0:T(8,128)(2,1)S(1)} %collective-permute-done.refs_0_), channel_id=1, source_target_pairs={{0,2},{2,0},{1,3},{3,1},{4,6},{6,4},{5,7},{7,5},{8,10},{10,8},{9,1... | collective-permute-start | bytes 786440 | tf_op jit(solution)/shard_map/ppermute | solution.py:626
  23.2 10.0 %collective-permute-start.7 = (bf16[128,1024]{1,0:T(8,128)(2,1)S(1)}, bf16[128,1024]{1,0:T(8,128)(2,1)S(1)}, u32[]{:S(2)}, u32[]{:S(2)}) collective-permute-start(bf16[128,1024]{1,0:T(8,128)(2,1)S(1)} %get-tuple-element.40.refs_1_), channel_id=1, source_target_pairs={{0,2},{2,0},{1,3},{3,1},{4,6},{6,4},{5,7},{7,5},{8,10},{10,8},{9,1... | collective-permute-start | bytes 786440 | tf_op jit(solution)/shard_map/ppermute | solution.py:628
  25.2 23.1 %collective-permute-start.8 = (bf16[256,512]{1,0:T(8,128)(2,1)S(1)}, bf16[256,512]{1,0:T(8,128)(2,1)S(1)}, u32[]{:S(2)}, u32[]{:S(2)}) collective-permute-start(bf16[256,512]{1,0:T(8,128)(2,1)S(1)} %get-tuple-element.44), channel_id=1, source_target_pairs={{0,0},{1,9},{2,6},{3,15},{4,4},{5,13},{6,10},{7,3},{8,8},{9,1},{10... | collective-permute-start | bytes 786440 | tf_op jit(solution)/shard_map/ppermute | solution.py:630
  25.9 24.6 %collective-permute-start.9 = (bf16[256,512]{1,0:T(8,128)(2,1)S(1)}, bf16[256,512]{1,0:T(8,128)(2,1)S(1)}, u32[]{:S(2)}, u32[]{:S(2)}) collective-permute-start(bf16[256,512]{1,0:T(8,128)(2,1)S(1)} %get-tuple-element.45), channel_id=1, source_target_pairs={{0,1},{1,8},{2,7},{3,14},{4,5},{5,12},{6,11},{7,2},{8,9},{9,0},{10... | collective-permute-start | bytes 786440 | tf_op jit(solution)/shard_map/ppermute | solution.py:631
  33.9 16.6 %collective-permute-start.10 = (bf16[256,512]{1,0:T(8,128)(2,1)S(1)}, bf16[256,512]{1,0:T(8,128)(2,1)S(1)}, u32[]{:S(2)}, u32[]{:S(2)}) collective-permute-start(bf16[256,512]{1,0:T(8,128)(2,1)S(1)} %get-tuple-element.41), channel_id=1, source_target_pairs={{0,4},{1,13},{2,2},{3,11},{4,8},{5,1},{6,6},{7,15},{8,12},{9,5},{1... | collective-permute-start | bytes 786440 | tf_op jit(solution)/shard_map/ppermute | solution.py:635
  43.0 14.7 %collective-permute-start.11 = (bf16[256,512]{1,0:T(8,128)(2,1)S(1)}, bf16[256,512]{1,0:T(8,128)(2,1)S(1)}, u32[]{:S(2)}, u32[]{:S(2)}) collective-permute-start(bf16[256,512]{1,0:T(8,128)(2,1)S(1)} %get-tuple-element.46), channel_id=1, source_target_pairs={{0,5},{1,12},{2,3},{3,10},{4,9},{5,0},{6,7},{7,14},{8,13},{9,4},{1... | collective-permute-start | bytes 786440 | tf_op jit(solution)/shard_map/ppermute | solution.py:636
  58.2 7.4 %collective-permute-start.14 = (bf16[1,128,1024]{2,1,0:T(8,128)(2,1)S(1)}, bf16[1,128,1024]{2,1,0:T(8,128)(2,1)S(1)}, u32[]{:S(2)}, u32[]{:S(2)}) collective-permute-start(bf16[1,128,1024]{2,1,0:T(8,128)(2,1)S(1)} %get-tuple-element.55), channel_id=1, source_target_pairs={{0,4},{12,8},{1,5},{13,9},{2,6},{14,10},{3,7},{15,11},{16,20},{28,... | collective-permute-start | bytes 786440 | tf_op jit(solution)/shard_map/ppermute | solution.py:664
  60.9 15.0 %collective-permute-start.12 = (bf16[1024,256]{1,0:T(8,128)(2,1)S(1)}, bf16[1024,256]{1,0:T(8,128)(2,1)S(1)}, u32[]{:S(2)}, u32[]{:S(2)}) collective-permute-start(bf16[1024,256]{1,0:T(8,128)(2,1)S(1)} %shard_map.109.refs_0_), channel_id=1, source_target_pairs={{0,1},{1,0},{2,3},{3,2},{4,5},{5,4},{6,7},{7,6},{8,9},{9,8},{10,11... | collective-permute-start | bytes 1572872 | tf_op jit(solution)/shard_map/ppermute | solution.py:654
  61.2 14.8 %collective-permute-start.13 = (bf16[1024,256]{1,0:T(8,128)(2,1)S(1)}, bf16[1024,256]{1,0:T(8,128)(2,1)S(1)}, u32[]{:S(2)}, u32[]{:S(2)}) collective-permute-start(bf16[1024,256]{1,0:T(8,128)(2,1)S(1)} %shard_map.110.refs_2_), channel_id=1, source_target_pairs={{0,1},{1,0},{2,3},{3,2},{4,5},{5,4},{6,7},{7,6},{8,9},{9,8},{10,11... | collective-permute-start | bytes 1572872 | tf_op jit(solution)/shard_map/ppermute | solution.py:654
  65.5 8.3 %collective-permute-start.20 = (bf16[1,128,1024]{2,1,0:T(8,128)(2,1)S(1)}, bf16[1,128,1024]{2,1,0:T(8,128)(2,1)S(1)}, u32[]{:S(2)}, u32[]{:S(2)}) collective-permute-start(bf16[1,128,1024]{2,1,0:T(8,128)(2,1)S(1)} %get-tuple-element.61), channel_id=1, source_target_pairs={{0,4},{12,8},{1,5},{13,9},{2,6},{14,10},{3,7},{15,11},{16,20},{28,... | collective-permute-start | bytes 786440 | tf_op jit(solution)/shard_map/ppermute | solution.py:664
  70.0 4.6 %collective-permute-start.15 = (bf16[1,128,1024]{2,1,0:T(8,128)(2,1)S(1)}, bf16[1,128,1024]{2,1,0:T(8,128)(2,1)S(1)}, u32[]{:S(2)}, u32[]{:S(2)}) collective-permute-start(bf16[1,128,1024]{2,1,0:T(8,128)(2,1)S(1)} %shard_map.111), channel_id=1, source_target_pairs={{4,8},{8,4},{5,9},{9,5},{6,10},{10,6},{7,11},{11,7},{20,24},{24,20... | collective-permute-start | bytes 786440 | tf_op jit(solution)/shard_map/ppermute | solution.py:664
  73.9 2.1 %collective-permute-start.21 = (bf16[1,128,1024]{2,1,0:T(8,128)(2,1)S(1)}, bf16[1,128,1024]{2,1,0:T(8,128)(2,1)S(1)}, u32[]{:S(2)}, u32[]{:S(2)}) collective-permute-start(bf16[1,128,1024]{2,1,0:T(8,128)(2,1)S(1)} %shard_map.115), channel_id=1, source_target_pairs={{4,8},{8,4},{5,9},{9,5},{6,10},{10,6},{7,11},{11,7},{20,24},{24,20... | collective-permute-start | bytes 786440 | tf_op jit(solution)/shard_map/ppermute | solution.py:664
  74.7 14.7 %collective-permute-start.16 = (bf16[1,128,1024]{2,1,0:T(8,128)(2,1)S(1)}, bf16[1,128,1024]{2,1,0:T(8,128)(2,1)S(1)}, u32[]{:S(2)}, u32[]{:S(2)}) collective-permute-start(bf16[1,128,1024]{2,1,0:T(8,128)(2,1)S(1)} %shard_map.112), channel_id=1, source_target_pairs={{4,0},{8,12},{5,1},{9,13},{6,2},{10,14},{7,3},{11,15},{20,16},{24,... | collective-permute-start | bytes 786440 | tf_op jit(solution)/shard_map/ppermute | solution.py:664
  76.1 23.2 %collective-permute-start.22 = (bf16[1,128,1024]{2,1,0:T(8,128)(2,1)S(1)}, bf16[1,128,1024]{2,1,0:T(8,128)(2,1)S(1)}, u32[]{:S(2)}, u32[]{:S(2)}) collective-permute-start(bf16[1,128,1024]{2,1,0:T(8,128)(2,1)S(1)} %shard_map.116), channel_id=1, source_target_pairs={{4,0},{8,12},{5,1},{9,13},{6,2},{10,14},{7,3},{11,15},{20,16},{24,... | collective-permute-start | bytes 786440 | tf_op jit(solution)/shard_map/ppermute | solution.py:664
  90.0 16.8 %collective-permute-start.17 = (bf16[256,256]{1,0:T(8,128)(2,1)S(1)}, bf16[256,256]{1,0:T(8,128)(2,1)S(1)}, u32[]{:S(2)}, u32[]{:S(2)}) collective-permute-start(bf16[256,256]{1,0:T(8,128)(2,1)S(1)} %shard_map.113.refs_4_), channel_id=1, source_target_pairs={{0,12},{4,0},{8,4},{12,8},{1,13},{5,1},{9,5},{13,9},{2,14},{6,2},{... | collective-permute-start | bytes 393224 | tf_op jit(solution)/shard_map/ppermute | solution.py:676
  90.8 16.6 %collective-permute-start.18 = (bf16[256,256]{1,0:T(8,128)(2,1)S(1)}, bf16[256,256]{1,0:T(8,128)(2,1)S(1)}, u32[]{:S(2)}, u32[]{:S(2)}) collective-permute-start(bf16[256,256]{1,0:T(8,128)(2,1)S(1)} %shard_map.113.refs_4_), channel_id=1, source_target_pairs={{0,8},{4,12},{8,0},{12,4},{1,9},{5,13},{9,1},{13,5},{2,10},{6,14},... | collective-permute-start | bytes 393224 | tf_op jit(solution)/shard_map/ppermute | solution.py:676
  91.4 16.0 %collective-permute-start.19 = (bf16[256,256]{1,0:T(8,128)(2,1)S(1)}, bf16[256,256]{1,0:T(8,128)(2,1)S(1)}, u32[]{:S(2)}, u32[]{:S(2)}) collective-permute-start(bf16[256,256]{1,0:T(8,128)(2,1)S(1)} %shard_map.113.refs_4_), channel_id=1, source_target_pairs={{0,4},{4,8},{8,12},{12,0},{1,5},{5,9},{9,13},{13,1},{2,6},{6,10},{... | collective-permute-start | bytes 393224 | tf_op jit(solution)/shard_map/ppermute | solution.py:676
  99.9 13.8 %collective-permute-start.23 = (bf16[256,256]{1,0:T(8,128)(2,1)S(1)}, bf16[256,256]{1,0:T(8,128)(2,1)S(1)}, u32[]{:S(2)}, u32[]{:S(2)}) collective-permute-start(bf16[256,256]{1,0:T(8,128)(2,1)S(1)} %shard_map.117.refs_4_), channel_id=1, source_target_pairs={{0,12},{4,0},{8,4},{12,8},{1,13},{5,1},{9,5},{13,9},{2,14},{6,2},{... | collective-permute-start | bytes 393224 | tf_op jit(solution)/shard_map/ppermute | solution.py:676
  106.8 7.3 %collective-permute-start.24 = (bf16[256,256]{1,0:T(8,128)(2,1)S(1)}, bf16[256,256]{1,0:T(8,128)(2,1)S(1)}, u32[]{:S(2)}, u32[]{:S(2)}) collective-permute-start(bf16[256,256]{1,0:T(8,128)(2,1)S(1)} %shard_map.117.refs_4_), channel_id=1, source_target_pairs={{0,8},{4,12},{8,0},{12,4},{1,9},{5,13},{9,1},{13,5},{2,10},{6,14},... | collective-permute-start | bytes 393224 | tf_op jit(solution)/shard_map/ppermute | solution.py:676
  106.8 7.3 %collective-permute-start.25 = (bf16[256,256]{1,0:T(8,128)(2,1)S(1)}, bf16[256,256]{1,0:T(8,128)(2,1)S(1)}, u32[]{:S(2)}, u32[]{:S(2)}) collective-permute-start(bf16[256,256]{1,0:T(8,128)(2,1)S(1)} %shard_map.117.refs_4_), channel_id=1, source_target_pairs={{0,4},{4,8},{8,12},{12,0},{1,5},{5,9},{9,13},{13,1},{2,6},{6,10},{... | collective-permute-start | bytes 393224 | tf_op jit(solution)/shard_map/ppermute | solution.py:676
  107.4 1.8 %copy-start.6 = (f32[32]{0:T(128)S(1)}, f32[32]{0:T(128)}, u32[]{:S(2)}) copy-start(f32[32]{0:T(128)} %skip_ref.1) | copy-start | bytes 388
where the time goes:
time: 116 us
  starting transfers between devices  49.6 us (43%)
  waiting for transfers between devices  40.3 us (35%)
  Pallas kernels  20.2 us (17%)
  local copies, waits for them, and re-layouts  4.75 us (4%)
  between operations  1.19 us (1%)
    ppermute x6, waiting for transfers between devices, on_device(): arrived[p].append(lax.ppermute(message, 'seq', pairs))  24.6 us
    ppermute x6, starting transfers between devices, on_device(): arrived[p].append(lax.ppermute(message, 'seq', pairs))  10.9 us
    ppermute x6, starting transfers between devices, on_device(): blocks[p].append(lax.ppermute(grad, 'seq', pairs))  10.7 us
    ppermute x1, starting transfers between devices, on_device(): lax.ppermute(same, axes, block_pairs(seq, False, True))  9.16 us
    ppermute x1, waiting for transfers between devices, on_device(): lax.ppermute(cross, axes, block_pairs(seq, False, False))  7.25 us
    ppermute x1, starting transfers between devices, on_device(): lax.ppermute(cross, axes, block_pairs(seq, True, False))  7.22 us
    ppermute x1, waiting for transfers between devices, on_device(): relayed = lax.ppermute(hidden[rows:], axes, beside)  5.87 us
    pallas_call x1, Pallas kernels, before(): call(before_kernel, (jax.ShapeDtypeStruct(values.shape, BF16), jax.ShapeD...  5.18 us
  transfers between devices with their start and end apart: 26, of which 8 were waited for; matrix products, arithmetic and copies ran while one was open for 1% of the time, Pallas kernels for 15%

commit v1 on v0

--- a/solution.py
+++ b/solution.py
@@ -381,6 +381,73 @@
     )(proj, xd, yd, mix, mixt, near, *far)
 
 
+def write_grad(proj_ref, xd, mixt, adjoint):
+    return (dot(mixt, proj_ref[:, STATE:]) + dot_nt(xd, adjoint)).astype(BF16)
+
+
+def read_grad(proj_ref, yd, mix, start):
+    return (dot(mix, proj_ref[:, :STATE]) + dot_nt(yd, start)).astype(BF16)
+
+
+def first_grads_kernel(
+    proj_ref, next_proj_ref, xd_ref, yd_ref, mix_ref, mixt_ref, near_ref, *refs
+):
+    (*far_refs, next_near_ref, out_ref) = refs
+    width = near_ref.shape[2]
+    here, after = slice(0, width), slice(width, 2 * width)
+    rest = slice(2 * STATE, 3 * STATE)
+    next_near = next_near_ref[0]
+
+    def body(start, adjoint):
+        out_ref[:, :STATE] = write_grad(proj_ref, xd_ref[:, here], mixt_ref[0], added(adjoint))
+        out_ref[:, STATE : 2 * STATE] = read_grad(
+            proj_ref, yd_ref[:, here], mix_ref[0], added(start)
+        )
+        if start[0] is near_ref:
+            out_ref[:, rest] = read_grad(next_proj_ref, yd_ref[:, after], mix_ref[1], next_near)
+        else:
+            out_ref[:, rest] = write_grad(next_proj_ref, xd_ref[:, after], mixt_ref[1], next_near)
+
+    either(None, [near_ref], far_refs, body)
+
+
+def last_grads_kernel(proj_ref, xd_ref, yd_ref, mix_ref, mixt_ref, *refs):
+    (*far_refs, out_ref) = refs
+    width = far_refs[0].shape[2]
+    after = slice(width, 2 * width)
+
+    def body(start, adjoint):
+        if start:
+            out_ref[...] = read_grad(proj_ref, yd_ref[:, after], mix_ref[1], added(start))
+        else:
+            out_ref[...] = write_grad(proj_ref, xd_ref[:, after], mixt_ref[1], added(adjoint))
+
+    either(None, [], far_refs, body)
+
+
+def some_grads(kernel, columns, *operands):
+    whole = pl.BlockSpec(memory_space=pltpu.VMEM)
+    return call(
+        kernel,
+        jax.ShapeDtypeStruct((SPAN, columns), BF16),
+        flops=8 * SPAN * columns * (SPAN + operands[-1].shape[2]),
+        moved=2 * sum(operand.size for operand in operands),
+        in_specs=[whole] * len(operands),
+        out_specs=whole,
+    )(*operands)
+
+
+def first_grads(proj, next_proj, xd, yd, mix, mixt, near, far, next_near):
+    return some_grads(
+        first_grads_kernel, 3 * STATE,
+        proj, next_proj, xd, yd, mix, mixt, near, *far, next_near,
+    )
+
+
+def last_grads(proj, xd, yd, mix, mixt, far):
+    return some_grads(last_grads_kernel, STATE, proj, xd, yd, mix, mixt, *far)
+
+
 def output_kernel(parts, hops, ahead, skip_ref, x_ref, cum_ref, cumt_ref, *refs):
     (*refs, out_ref, proj_ref, start_ref) = refs
     projs, nears = refs[:parts], refs[parts : 2 * parts]
@@ -470,17 +537,35 @@
     return 2 * other_x + other_core
 
 
-def update_kernel(blocks, spots, part, *refs):
-    turned_refs, pieces = refs[:spots], refs[spots : spots + blocks]
-    decayed_ref, keep_ref = refs[spots + blocks : spots + blocks + 2]
+def update_kernel(blocks, spots, part, split, *refs):
+    turned_refs, refs = refs[:spots], refs[spots:]
+    firsts, refs = refs[:blocks], refs[blocks:]
+    lasts = refs[:blocks] if split == 1 else ()
+    decayed_ref, keep_ref = refs[len(lasts) : len(lasts) + 2]
     weight_ref, sparse_ref, grad_ref, weight_out, sparse_out, sems = refs[-6:]
-    tokens, width = pieces[0].shape
+    tokens, width = firsts[0].shape[0], grad_ref.shape[1]
     rows = decayed_ref.shape[0]
     step = min(rows, 256)
     columns = slice(part * width, (part + 1) * width)
-    for block, piece in enumerate(pieces):
+    for block, first in enumerate(firsts):
         start = pl.multiple_of(spot_of(block, spots) * tokens, tokens)
-        grad_ref[pl.ds(start, tokens), :] = piece[...]
+        here = pl.ds(start, tokens)
+        if split != 1:
+            grad_ref[here, :] = first[:, :width]
+            continue
+        last = lasts[block]
+        lower = (lax.axis_index("seq") + block) % blocks < blocks // 2
+
+        @pl.when(lower)
+        def _(here=here, first=first, last=last):
+            grad_ref[here, :STATE] = last[...]
+            grad_ref[here, STATE:] = first[:, width:]
+
+        @pl.when(jnp.logical_not(lower))
+        def _(here=here, first=first, last=last):
+            grad_ref[here, :STATE] = first[:, width:]
+            grad_ref[here, STATE:] = last[...]
+
     copies = []
     for number in range(rows // step):
         here = slice(number * step, (number + 1) * step)
@@ -505,20 +590,20 @@
         copy.wait()
 
 
-def update(turned_hidden, grad_blocks, decayed, keep, part, earlier, vmem):
+def update(turned_hidden, firsts, lasts, decayed, keep, width, part, split, earlier, vmem):
     rows, columns = decayed.shape
-    width = grad_blocks[0].shape[1]
     tokens = turned_hidden[0].shape[1]
-    spots, blocks = len(turned_hidden), len(grad_blocks)
+    spots, blocks = len(turned_hidden), len(firsts)
+    pieces = [*turned_hidden, *firsts, *lasts, decayed, keep]
     earlier = earlier or ()
     whole, anywhere = pl.BlockSpec(memory_space=pltpu.VMEM), pl.BlockSpec(memory_space=pl.ANY)
     return call(
-        functools.partial(update_kernel, blocks, spots, part),
+        functools.partial(update_kernel, blocks, spots, part, split),
         (jax.ShapeDtypeStruct((rows, columns), F32), jax.ShapeDtypeStruct((rows, columns), BF16)),
         flops=2 * spots * tokens * rows * width,
         moved=rows * width * 12 + spots * tokens * (rows + width) * 2,
         vmem=vmem,
-        in_specs=[whole] * (spots + blocks + 2) + [anywhere] * len(earlier),
+        in_specs=[whole] * len(pieces) + [anywhere] * len(earlier),
         out_specs=(anywhere, anywhere),
         scratch_shapes=[
             pltpu.VMEM((spots * tokens, width), BF16),
@@ -526,8 +611,8 @@
             pltpu.VMEM((rows, width), BF16),
             pltpu.SemaphoreType.DMA((2, rows // min(rows, 256))),
         ],
-        input_output_aliases={spots + blocks + 2 + i: i for i in range(len(earlier))},
-    )(*turned_hidden, *grad_blocks, decayed, keep, *earlier)
+        input_output_aliases={len(pieces) + i: i for i in range(len(earlier))},
+    )(*pieces, *earlier)
 
 
 def held(after, *before):
@@ -604,7 +689,9 @@
     ssd_output = output(
         True, inner_values, cum, cumt, skip_gain, [proj], [start], [[adjoint_in]]
     )
-    return ssd_output, *update([layer.T], blocks, decayed, keep, 0, None, 40 * MIB)
+    return ssd_output, *update(
+        [layer.T], blocks, [], decayed, keep, grad.shape[1], 0, None, None, 40 * MIB
+    )
 
 
 def on_device(
@@ -665,20 +752,23 @@
         for p in spans:
             if own_terms:
                 messages[p] = handed_on(decay, arrived[p][-1], own_terms[p], p * each)
-    blocks = []
-    for p in spans:
-        grad = grads(
-            None, projs[p], xd, yd, mix, mixt, arrived[p][0], arrived[p][1:], p * each
-        )
-        blocks.append([grad])
-        for distance in range(1, seq):
-            pairs = to_all(seq, seq - distance)
-            blocks[p].append(lax.ppermute(grad, "seq", pairs))
-
-    decayed = held(decayed, blocks[-1][0])
+    (near, *far), (next_near, *next_far) = arrived
+    first = first_grads(*projs, xd, yd, mix, mixt, near, far, next_near)
+    last = last_grads(projs[1], xd, yd, mix, mixt, next_far)
+    firsts, lasts = (
+        [grad]
+        + [
+            lax.ppermute(grad, "seq", to_all(seq, seq - distance)) for distance in range(1, seq)
+        ]
+        for grad in (first, last)
+    )
+    decayed = held(decayed, last)
     updated = None
     for p in spans:
-        updated = update(turned_hidden, blocks[p], decayed, keep, p, updated, 16 * MIB)
+        updated = update(
+            turned_hidden, firsts, lasts if p else [], decayed, keep, 2 * STATE, p, p, updated,
+            16 * MIB,
+        )
         if not p:
             cum = held(cum, *updated)
     ssd_output = output(

time: 116 us -> 119 us (1.026)
  starting transfers between devices: 49.6 us -> 51.7 us
    ppermute x6, starting transfers between devices: 10.7 us -> 12.8 us  [on_device(): lax.ppermute(grad, 'seq', to_all(seq, seq - distance))]
where the time goes in v1:
time: 119 us
  starting transfers between devices  51.7 us (43%)
  waiting for transfers between devices  40.7 us (34%)
  Pallas kernels  20.2 us (17%)
  local copies, waits for them, and re-layouts  4.75 us (4%)
  between operations  1.19 us (1%)
    ppermute x6, waiting for transfers between devices, on_device(): arrived[p].append(lax.ppermute(message, 'seq', pairs))  24.4 us
    ppermute x6, starting transfers between devices, on_device(): lax.ppermute(grad, 'seq', to_all(seq, seq - distance))  12.8 us
    ppermute x6, starting transfers between devices, on_device(): arrived[p].append(lax.ppermute(message, 'seq', pairs))  10.9 us
    ppermute x1, starting transfers between devices, on_device(): lax.ppermute(same, axes, block_pairs(seq, False, True))  9.16 us
    ppermute x1, waiting for transfers between devices, on_device(): lax.ppermute(cross, axes, block_pairs(seq, False, False))  7.25 us
    ppermute x1, starting transfers between devices, on_device(): lax.ppermute(cross, axes, block_pairs(seq, True, False))  7.22 us
    ppermute x1, waiting for transfers between devices, on_device(): relayed = lax.ppermute(hidden[rows:], axes, beside)  5.87 us
    pallas_call x1, Pallas kernels, before(): call(before_kernel, (jax.ShapeDtypeStruct(values.shape, BF16), jax.ShapeD...  5.17 us
  transfers between devices with their start and end apart: 26, of which 8 were waited for; matrix products, arithmetic and copies ran while one was open for 1% of the time, Pallas kernels for 15%

profile of v1, /device:TPU:0, one launch (start us, length us, event | category | flops | bytes accessed | tf_op | source)
XLA Modules:
  0.0 118.6 jit_solution(15349991910765670199)
XLA Ops:
  0.6 0.5 collective-permute-start.1
  1.1 0.1 collective-permute-start.2
  1.2 1.1 fusion
  2.3 1.3 %collective-permute-start.5 = (bf16[128,1024]{1,0:T(8,128)(2,1)S(1)}, bf16[128,1024]{1,0:T(8,128)(2,1)S(1)}, u32[]{:S(2)}, u32[]{:S(2)}) collective-permute-start(bf16[128,1024]{1,0:T(8,128)(2,1)S(1)} %get-tuple-element.73), channel_id=1, source_target_pairs={{1,3},{2,0},{4,6},{7,5},{9,11},{10,8},{12,14},{15,13},{17,19},{18,... | collective-permute-start | bytes 786440 | tf_op jit(solution)/shard_map/ppermute | solution.py:704
  3.6 0.7 collective-permute-start.4
  4.3 0.7 collective-permute-start
  5.0 5.9 %collective-permute-done.5 = bf16[128,1024]{1,0:T(8,128)(2,1)S(1)} collective-permute-done((bf16[128,1024]{1,0:T(8,128)(2,1)S(1)}, bf16[128,1024]{1,0:T(8,128)(2,1)S(1)}, u32[]{:S(2)}, u32[]{:S(2)}) %collective-permute-start.5) | collective-permute-done | bytes 262176 | tf_op jit(solution)/shard_map/ppermute | solution.py:704
  10.8 4.9 %collective-permute-start.6 = (bf16[128,1024]{1,0:T(8,128)(2,1)S(1)}, bf16[128,1024]{1,0:T(8,128)(2,1)S(1)}, u32[]{:S(2)}, u32[]{:S(2)}) collective-permute-start(bf16[128,1024]{1,0:T(8,128)(2,1)S(1)} %collective-permute-done.5), channel_id=1, source_target_pairs={{3,7},{0,9},{6,2},{5,13},{11,6},{8,8},{14,3},{13,12},{19,23},{16,2... | collective-permute-start | bytes 786440 | tf_op jit(solution)/shard_map/ppermute | solution.py:706
  15.8 1.6 %copy-done = f32[1024,512]{1,0:T(8,128)S(1)} copy-done((f32[1024,512]{1,0:T(8,128)S(1)}, f32[1024,512]{1,0:T(8,128)}, u32[]{:S(2)}) %copy-start) | copy-done | bytes 2097176
  17.3 1.0 copy-done.3
  18.4 1.0 copy-done.4
  19.4 1.7 %shard_map.103 = (bf16[1024,512]{1,0:T(8,128)(2,1)S(1)}, f32[1024,512]{1,0:T(8,128)S(1)}, bf16[1024,512]{1,0:T(8,128)(2,1)S(1)}) custom-call(f32[1024,512]{1,0:T(8,128)S(1)} %copy-done, s32[256,512]{1,0:T(8,128)S(1)} %copy-done.4, s32[256,512]{1,0:T(8,128)S(1)} %copy-done.3), custom_call_target="tpu_custom_call" | custom-call | flops 1572864000 | bytes 7340032 | tf_op jit(solution)/shard_map/pallas_call | solution.py:77
  21.1 1.2 %shard_map.104.refs_4_.refs_3_ = bf16[1024,512]{1,0:T(8,128)(2,1)S(1)} custom-call(f32[1024,512]{1,0:T(8,128)S(1)} %collective-permute-done.1.master_ref, s32[256,512]{1,0:T(8,128)S(1)} %collective-permute-done.2.now_ref), custom_call_target="tpu_custom_call" | custom-call | flops 1572864000 | bytes 3670016 | tf_op jit(solution)/shard_map/pallas_call | solution.py:101
  22.5 0.7 shard_map.105
  23.2 2.1 %collective-permute-start.7 = (bf16[128,1024]{1,0:T(8,128)(2,1)S(1)}, bf16[128,1024]{1,0:T(8,128)(2,1)S(1)}, u32[]{:S(2)}, u32[]{:S(2)}) collective-permute-start(bf16[128,1024]{1,0:T(8,128)(2,1)S(1)} %get-tuple-element.40.refs_1_), channel_id=1, source_target_pairs={{0,2},{2,0},{1,3},{3,1},{4,6},{6,4},{5,7},{7,5},{8,10},{10,8},{9,1... | collective-permute-start | bytes 786440 | tf_op jit(solution)/shard_map/ppermute | solution.py:715
  25.2 0.7 collective-permute-start.8
  25.9 7.2 %collective-permute-start.9 = (bf16[256,512]{1,0:T(8,128)(2,1)S(1)}, bf16[256,512]{1,0:T(8,128)(2,1)S(1)}, u32[]{:S(2)}, u32[]{:S(2)}) collective-permute-start(bf16[256,512]{1,0:T(8,128)(2,1)S(1)} %get-tuple-element.45), channel_id=1, source_target_pairs={{0,1},{1,8},{2,7},{3,14},{4,5},{5,12},{6,11},{7,2},{8,9},{9,0},{10... | collective-permute-start | bytes 786440 | tf_op jit(solution)/shard_map/ppermute | solution.py:718
  33.1 0.7 shard_map.106
  33.9 9.2 %collective-permute-start.10 = (bf16[256,512]{1,0:T(8,128)(2,1)S(1)}, bf16[256,512]{1,0:T(8,128)(2,1)S(1)}, u32[]{:S(2)}, u32[]{:S(2)}) collective-permute-start(bf16[256,512]{1,0:T(8,128)(2,1)S(1)} %get-tuple-element.41), channel_id=1, source_target_pairs={{0,4},{1,13},{2,2},{3,11},{4,8},{5,1},{6,6},{7,15},{8,12},{9,5},{1... | collective-permute-start | bytes 786440 | tf_op jit(solution)/shard_map/ppermute | solution.py:722
  43.1 5.2 %shard_map.107 = (bf16[256,2048]{1,0:T(8,128)(2,1)S(1)}, bf16[256,2048]{1,0:T(8,128)(2,1)S(1)}, bf16[2,256,256]{2,1,0:T(8,128)(2,1)S(1)}, bf16[2,256,256]{2,1,0:...) custom-call(bf16[256,2048]{1,0:T(8,128)(2,1)S(1)} %copy-done.2, ...), custom_call_target="tpu_custom_call" | custom-call | flops 5242880000 | bytes 4194304 | tf_op jit(solution)/shard_map/pallas_call | solution.py:198
  48.3 2.2 %collective-permute-done.9.refs_1_ = bf16[256,512]{1,0:T(8,128)(2,1)S(1)} collective-permute-done((bf16[256,512]{1,0:T(8,128)(2,1)S(1)}, bf16[256,512]{1,0:T(8,128)(2,1)S(1)}, u32[]{:S(2)}, u32[]{:S(2)}) %collective-permute-start.9) | collective-permute-done | bytes 262176 | tf_op jit(solution)/shard_map/ppermute | solution.py:718
  50.5 7.2 %collective-permute-done.11.refs_3_ = bf16[256,512]{1,0:T(8,128)(2,1)S(1)} collective-permute-done((bf16[256,512]{1,0:T(8,128)(2,1)S(1)}, bf16[256,512]{1,0:T(8,128)(2,1)S(1)}, u32[]{:S(2)}, u32[]{:S(2)}) %collective-permute-start.11) | collective-permute-done | bytes 262176 | tf_op jit(solution)/shard_map/ppermute | solution.py:723
  57.7 0.4 shard_map.108
  58.2 2.5 %collective-permute-start.14 = (bf16[1,128,1024]{2,1,0:T(8,128)(2,1)S(1)}, bf16[1,128,1024]{2,1,0:T(8,128)(2,1)S(1)}, u32[]{:S(2)}, u32[]{:S(2)}) collective-permute-start(bf16[1,128,1024]{2,1,0:T(8,128)(2,1)S(1)} %get-tuple-element.56), channel_id=1, source_target_pairs={{0,4},{12,8},{1,5},{13,9},{2,6},{14,10},{3,7},{15,11},{16,20},{28,... | collective-permute-start | bytes 786440 | tf_op jit(solution)/shard_map/ppermute | solution.py:751
  60.7 0.2 shard_map.109.refs_0_
  61.0 0.2 shard_map.110.refs_2_
  61.2 0.6 collective-permute-start.13
  61.8 0.5 shard_map.111
  62.3 3.3 %collective-permute-done.14.arrived_ref.near_ref.refs_2_ = bf16[1,128,1024]{2,1,0:T(8,128)(2,1)S(1)} collective-permute-done((bf16[1,128,1024]{2,1,0:T(8,128)(2,1)S(1)}, bf16[1,128,1024]{2,1,0:T(8,128)(2,1)S(1)}, u32[]{:S(2)}, u32[]{:S(2)}) %collective-permute-start.14) | collective-permute-done | bytes 262176 | tf_op jit(solution)/shard_map/ppermute | solution.py:751
  65.5 4.4 %collective-permute-start.17 = (bf16[1,128,1024]{2,1,0:T(8,128)(2,1)S(1)}, bf16[1,128,1024]{2,1,0:T(8,128)(2,1)S(1)}, u32[]{:S(2)}, u32[]{:S(2)}) collective-permute-start(bf16[1,128,1024]{2,1,0:T(8,128)(2,1)S(1)} %get-tuple-element.60), channel_id=1, source_target_pairs={{0,4},{12,8},{1,5},{13,9},{2,6},{14,10},{3,7},{15,11},{16,20},{28,... | collective-permute-start | bytes 786440 | tf_op jit(solution)/shard_map/ppermute | solution.py:751
  70.0 0.7 collective-permute-start.15
  70.7 3.1 %collective-permute-done.17.refs_2_.arrived_ref.refs_3_ = bf16[1,128,1024]{2,1,0:T(8,128)(2,1)S(1)} collective-permute-done((bf16[1,128,1024]{2,1,0:T(8,128)(2,1)S(1)}, bf16[1,128,1024]{2,1,0:T(8,128)(2,1)S(1)}, u32[]{:S(2)}, u32[]{:S(2)}) %collective-permute-start.17) | collective-permute-done | bytes 262176 | tf_op jit(solution)/shard_map/ppermute | solution.py:751
  73.9 0.7 collective-permute-start.21
  74.7 1.3 %collective-permute-start.16 = (bf16[1,128,1024]{2,1,0:T(8,128)(2,1)S(1)}, bf16[1,128,1024]{2,1,0:T(8,128)(2,1)S(1)}, u32[]{:S(2)}, u32[]{:S(2)}) collective-permute-start(bf16[1,128,1024]{2,1,0:T(8,128)(2,1)S(1)} %shard_map.113), channel_id=1, source_target_pairs={{4,0},{8,12},{5,1},{9,13},{6,2},{10,14},{7,3},{11,15},{20,16},{24,... | collective-permute-start | bytes 786440 | tf_op jit(solution)/shard_map/ppermute | solution.py:751
  76.1 1.3 %collective-permute-start.22 = (bf16[1,128,1024]{2,1,0:T(8,128)(2,1)S(1)}, bf16[1,128,1024]{2,1,0:T(8,128)(2,1)S(1)}, u32[]{:S(2)}, u32[]{:S(2)}) collective-permute-start(bf16[1,128,1024]{2,1,0:T(8,128)(2,1)S(1)} %shard_map.116), channel_id=1, source_target_pairs={{4,0},{8,12},{5,1},{9,13},{6,2},{10,14},{7,3},{11,15},{20,16},{24,... | collective-permute-start | bytes 786440 | tf_op jit(solution)/shard_map/ppermute | solution.py:751
  77.4 12.0 %collective-permute-done.16.refs_1_.refs_5_ = bf16[1,128,1024]{2,1,0:T(8,128)(2,1)S(1)} collective-permute-done((bf16[1,128,1024]{2,1,0:T(8,128)(2,1)S(1)}, bf16[1,128,1024]{2,1,0:T(8,128)(2,1)S(1)}, u32[]{:S(2)}, u32[]{:S(2)}) %collective-permute-start.16) | collective-permute-done | bytes 262176 | tf_op jit(solution)/shard_map/ppermute | solution.py:751
  89.4 0.7 shard_map.114.refs_4_
  90.1 0.9 collective-permute-start.18
  91.0 0.6 collective-permute-start.19
  91.5 1.7 %collective-permute-start.20 = (bf16[256,384]{1,0:T(8,128)(2,1)S(1)}, bf16[256,384]{1,0:T(8,128)(2,1)S(1)}, u32[]{:S(2)}, u32[]{:S(2)}) collective-permute-start(bf16[256,384]{1,0:T(8,128)(2,1)S(1)} %shard_map.114.refs_4_), channel_id=1, source_target_pairs={{0,4},{4,8},{8,12},{12,0},{1,5},{5,9},{9,13},{13,1},{2,6},{6,10},{... | collective-permute-start | bytes 589832 | tf_op jit(solution)/shard_map/ppermute | solution.py:761
  93.3 6.0 %collective-permute-done.22.refs_1_.refs_7_ = bf16[1,128,1024]{2,1,0:T(8,128)(2,1)S(1)} collective-permute-done((bf16[1,128,1024]{2,1,0:T(8,128)(2,1)S(1)}, bf16[1,128,1024]{2,1,0:T(8,128)(2,1)S(1)}, u32[]{:S(2)}, u32[]{:S(2)}) %collective-permute-start.22) | collective-permute-done | bytes 262176 | tf_op jit(solution)/shard_map/ppermute | solution.py:751
  99.3 0.3 shard_map.117.refs_8_
  99.7 9.0 %collective-permute-start.23 = (bf16[256,128]{1,0:T(8,128)(2,1)S(1)}, bf16[256,128]{1,0:T(8,128)(2,1)S(1)}, u32[]{:S(2)}, u32[]{:S(2)}) collective-permute-start(bf16[256,128]{1,0:T(8,128)(2,1)S(1)} %shard_map.117.refs_8_), channel_id=1, source_target_pairs={{0,12},{4,0},{8,4},{12,8},{1,13},{5,1},{9,5},{13,9},{2,14},{6,2},{... | collective-permute-start | bytes 196616 | tf_op jit(solution)/shard_map/ppermute | solution.py:761
  108.7 0.6 collective-permute-start.25
  109.3 1.0 collective-permute-done.19.refs_6_
  110.3 1.8 %shard_map.118 = (f32[1024,512]{1,0:T(8,128)}, bf16[1024,512]{1,0:T(8,128)(2,1)}) custom-call(bf16[1024,256]{1,0:T(8,128)(2,1)S(1)} %shard_map.109.refs_0_, bf16[1024,256]{1,0:T(8,128)(2,1)S(1)} %collective-permute-done.12.refs_1_, bf16[1024,256]{1,0:T(8,128)(2,1)S(1)} %shard_map.110.refs_2_, bf16[1024,256]{1,0:T(8,128)(2,1)S(1)} %collective-permute-done.13.refs_3_, ...), custom_call_target="tpu_custom_call" | custom-call | flops 536870912 | bytes 5767168 | tf_op jit(solution)/shard_map/pallas_call | solution.py:600
  112.0 4.5 %shard_map.119 = bf16[256,2048]{1,0:T(8,128)(2,1)} custom-call(f32[32]{0:T(128)S(1)} %copy-done.6, bf16[256,2048]{1,0:T(8,128)(2,1)S(1)} %copy-done.2, f32[2,256,16]{2,1,0:T(8,128)S(1)} %get-tuple-element.69.cum_ref, f32[2,16,256]{2,1,0:T(8,128)S(1)} %get-tuple-element.70.cumt_ref, bf16[256,256]{1,0:T(8,128)(2,1)S(1)} %get-tuple-element.52.proj_ref.refs_0_, ...), custom_call_target="tpu_custom_call" | custom-call | flops 4194304000 | bytes 2621440 | tf_op jit(solution)/shard_map/pallas_call | solution.py:513
  116.5 1.9 %shard_map.120 = (f32[1024,512]{1,0:T(8,128)}, bf16[1024,512]{1,0:T(8,128)(2,1)}) custom-call(bf16[1024,256]{1,0:T(8,128)(2,1)S(1)} %shard_map.109.refs_0_, bf16[1024,256]{1,0:T(8,128)(2,1)S(1)} %collective-permute-done.12.refs_1_, bf16[1024,256]{1,0:T(8,128)(2,1)S(1)} %shard_map.110.refs_2_, ...), custom_call_target="tpu_custom_call", output_to_operand_aliasing={{0}: (14, {}), {1}: (15, {})} | custom-call | flops 536870912 | bytes 5767168 | tf_op jit(solution)/shard_map/pallas_call | solution.py:600
  (37 shorter events, 0.5 us)
Async XLA Ops:
  0.6 20.5 %collective-permute-start.1 = (f32[1024,512]{1,0:T(8,128)}, f32[1024,512]{1,0:T(8,128)S(1)}, u32[]{:S(2)}, u32[]{:S(2)}) collective-permute-start(f32[1024,512]{1,0:T(8,128)} %master_ref.1), channel_id=1, source_target_pairs={{0,1},{1,0},{2,3},{3,2},{4,5},{5,4},{6,7},{7,6},{8,9},{9,8},{10,11... | collective-permute-start | bytes 6291464 | tf_op jit(solution)/shard_map/ppermute | solution.py:709
  1.1 20.0 %collective-permute-start.2 = (s32[256,512]{1,0:T(8,128)}, s32[256,512]{1,0:T(8,128)S(1)}, u32[]{:S(2)}, u32[]{:S(2)}) collective-permute-start(s32[256,512]{1,0:T(8,128)} %now_ref.1), channel_id=1, source_target_pairs={{0,1},{1,0},{2,3},{3,2},{4,5},{5,4},{6,7},{7,6},{8,9},{9,8},{10,11... | collective-permute-start | bytes 1572872 | tf_op jit(solution)/shard_map/ppermute | solution.py:709
  2.3 8.5 %collective-permute-start.5 = (bf16[128,1024]{1,0:T(8,128)(2,1)S(1)}, bf16[128,1024]{1,0:T(8,128)(2,1)S(1)}, u32[]{:S(2)}, u32[]{:S(2)}) collective-permute-start(bf16[128,1024]{1,0:T(8,128)(2,1)S(1)} %get-tuple-element.73), channel_id=1, source_target_pairs={{1,3},{2,0},{4,6},{7,5},{9,11},{10,8},{12,14},{15,13},{17,19},{18,... | collective-permute-start | bytes 786440 | tf_op jit(solution)/shard_map/ppermute | solution.py:704
  3.6 18.8 %collective-permute-start.4 = (bf16[128,1024]{1,0:T(8,128)(2,1)S(1)}, bf16[128,1024]{1,0:T(8,128)(2,1)S(1)}, u32[]{:S(2)}, u32[]{:S(2)}) collective-permute-start(bf16[128,1024]{1,0:T(8,128)(2,1)S(1)} %get-tuple-element.73), channel_id=1, source_target_pairs={{0,0},{3,14},{5,4},{6,11},{8,1},{11,15},{13,5},{14,10},{16,16},{19... | collective-permute-start | bytes 786440 | tf_op jit(solution)/shard_map/ppermute | solution.py:706
  4.3 18.0 %collective-permute-start = (bf16[128,1024]{1,0:T(8,128)(2,1)S(1)}, bf16[128,1024]{1,0:T(8,128)(2,1)S(1)}, u32[]{:S(2)}, u32[]{:S(2)}) collective-permute-start(bf16[128,1024]{1,0:T(8,128)(2,1)S(1)} %get-tuple-element.74), channel_id=1, source_target_pairs={{0,0},{3,14},{5,4},{6,11},{8,1},{11,15},{13,5},{14,10},{1,7},{2,9}... | collective-permute-start | bytes 786440 | tf_op jit(solution)/shard_map/ppermute | solution.py:705
  10.8 11.6 %collective-permute-start.6 = (bf16[128,1024]{1,0:T(8,128)(2,1)S(1)}, bf16[128,1024]{1,0:T(8,128)(2,1)S(1)}, u32[]{:S(2)}, u32[]{:S(2)}) collective-permute-start(bf16[128,1024]{1,0:T(8,128)(2,1)S(1)} %collective-permute-done.5), channel_id=1, source_target_pairs={{3,7},{0,9},{6,2},{5,13},{11,6},{8,8},{14,3},{13,12},{19,23},{16,2... | collective-permute-start | bytes 786440 | tf_op jit(solution)/shard_map/ppermute | solution.py:706
  15.7 1.6 %copy-start = (f32[1024,512]{1,0:T(8,128)S(1)}, f32[1024,512]{1,0:T(8,128)}, u32[]{:S(2)}) copy-start(f32[1024,512]{1,0:T(8,128)} %master_ref.1) | copy-start | bytes 6291460
  17.3 1.0 copy-start.3
  18.4 1.0 copy-start.4
  22.3 20.8 %copy-start.1 = (bf16[256,2048]{1,0:T(8,128)(2,1)S(1)}, bf16[256,2048]{1,0:T(8,128)(2,1)}, u32[]{:S(2)}) copy-start(bf16[256,2048]{1,0:T(8,128)(2,1)} %dy_ref.1) | copy-start | bytes 3145732
  22.3 20.8 %copy-start.2 = (bf16[256,2048]{1,0:T(8,128)(2,1)S(1)}, bf16[256,2048]{1,0:T(8,128)(2,1)}, u32[]{:S(2)}) copy-start(bf16[256,2048]{1,0:T(8,128)(2,1)} %x_ref.2) | copy-start | bytes 3145732
  22.3 20.8 %copy-start.5 = (f32[256,32]{0,1:T(8,128)S(1)}, f32[256,32]{0,1:T(8,128)}, u32[]{:S(2)}) copy-start(f32[256,32]{0,1:T(8,128)} %param.10) | copy-start | bytes 98308
  22.4 10.8 %collective-permute-start.3 = (bf16[128,1024]{1,0:T(8,128)(2,1)S(1)}, bf16[128,1024]{1,0:T(8,128)(2,1)S(1)}, u32[]{:S(2)}, u32[]{:S(2)}) collective-permute-start(bf16[128,1024]{1,0:T(8,128)(2,1)S(1)} %collective-permute-done.refs_0_), channel_id=1, source_target_pairs={{0,2},{2,0},{1,3},{3,1},{4,6},{6,4},{5,7},{7,5},{8,10},{10,8},{9,1... | collective-permute-start | bytes 786440 | tf_op jit(solution)/shard_map/ppermute | solution.py:713
  23.2 10.0 %collective-permute-start.7 = (bf16[128,1024]{1,0:T(8,128)(2,1)S(1)}, bf16[128,1024]{1,0:T(8,128)(2,1)S(1)}, u32[]{:S(2)}, u32[]{:S(2)}) collective-permute-start(bf16[128,1024]{1,0:T(8,128)(2,1)S(1)} %get-tuple-element.40.refs_1_), channel_id=1, source_target_pairs={{0,2},{2,0},{1,3},{3,1},{4,6},{6,4},{5,7},{7,5},{8,10},{10,8},{9,1... | collective-permute-start | bytes 786440 | tf_op jit(solution)/shard_map/ppermute | solution.py:715
  25.2 23.1 %collective-permute-start.8 = (bf16[256,512]{1,0:T(8,128)(2,1)S(1)}, bf16[256,512]{1,0:T(8,128)(2,1)S(1)}, u32[]{:S(2)}, u32[]{:S(2)}) collective-permute-start(bf16[256,512]{1,0:T(8,128)(2,1)S(1)} %get-tuple-element.44), channel_id=1, source_target_pairs={{0,0},{1,9},{2,6},{3,15},{4,4},{5,13},{6,10},{7,3},{8,8},{9,1},{10... | collective-permute-start | bytes 786440 | tf_op jit(solution)/shard_map/ppermute | solution.py:717
  25.9 24.6 %collective-permute-start.9 = (bf16[256,512]{1,0:T(8,128)(2,1)S(1)}, bf16[256,512]{1,0:T(8,128)(2,1)S(1)}, u32[]{:S(2)}, u32[]{:S(2)}) collective-permute-start(bf16[256,512]{1,0:T(8,128)(2,1)S(1)} %get-tuple-element.45), channel_id=1, source_target_pairs={{0,1},{1,8},{2,7},{3,14},{4,5},{5,12},{6,11},{7,2},{8,9},{9,0},{10... | collective-permute-start | bytes 786440 | tf_op jit(solution)/shard_map/ppermute | solution.py:718
  33.9 16.6 %collective-permute-start.10 = (bf16[256,512]{1,0:T(8,128)(2,1)S(1)}, bf16[256,512]{1,0:T(8,128)(2,1)S(1)}, u32[]{:S(2)}, u32[]{:S(2)}) collective-permute-start(bf16[256,512]{1,0:T(8,128)(2,1)S(1)} %get-tuple-element.41), channel_id=1, source_target_pairs={{0,4},{1,13},{2,2},{3,11},{4,8},{5,1},{6,6},{7,15},{8,12},{9,5},{1... | collective-permute-start | bytes 786440 | tf_op jit(solution)/shard_map/ppermute | solution.py:722
  43.0 14.7 %collective-permute-start.11 = (bf16[256,512]{1,0:T(8,128)(2,1)S(1)}, bf16[256,512]{1,0:T(8,128)(2,1)S(1)}, u32[]{:S(2)}, u32[]{:S(2)}) collective-permute-start(bf16[256,512]{1,0:T(8,128)(2,1)S(1)} %get-tuple-element.46), channel_id=1, source_target_pairs={{0,5},{1,12},{2,3},{3,10},{4,9},{5,0},{6,7},{7,14},{8,13},{9,4},{1... | collective-permute-start | bytes 786440 | tf_op jit(solution)/shard_map/ppermute | solution.py:723
  58.2 7.4 %collective-permute-start.14 = (bf16[1,128,1024]{2,1,0:T(8,128)(2,1)S(1)}, bf16[1,128,1024]{2,1,0:T(8,128)(2,1)S(1)}, u32[]{:S(2)}, u32[]{:S(2)}) collective-permute-start(bf16[1,128,1024]{2,1,0:T(8,128)(2,1)S(1)} %get-tuple-element.56), channel_id=1, source_target_pairs={{0,4},{12,8},{1,5},{13,9},{2,6},{14,10},{3,7},{15,11},{16,20},{28,... | collective-permute-start | bytes 786440 | tf_op jit(solution)/shard_map/ppermute | solution.py:751
  60.9 15.0 %collective-permute-start.12 = (bf16[1024,256]{1,0:T(8,128)(2,1)S(1)}, bf16[1024,256]{1,0:T(8,128)(2,1)S(1)}, u32[]{:S(2)}, u32[]{:S(2)}) collective-permute-start(bf16[1024,256]{1,0:T(8,128)(2,1)S(1)} %shard_map.109.refs_0_), channel_id=1, source_target_pairs={{0,1},{1,0},{2,3},{3,2},{4,5},{5,4},{6,7},{7,6},{8,9},{9,8},{10,11... | collective-permute-start | bytes 1572872 | tf_op jit(solution)/shard_map/ppermute | solution.py:741
  61.2 14.8 %collective-permute-start.13 = (bf16[1024,256]{1,0:T(8,128)(2,1)S(1)}, bf16[1024,256]{1,0:T(8,128)(2,1)S(1)}, u32[]{:S(2)}, u32[]{:S(2)}) collective-permute-start(bf16[1024,256]{1,0:T(8,128)(2,1)S(1)} %shard_map.110.refs_2_), channel_id=1, source_target_pairs={{0,1},{1,0},{2,3},{3,2},{4,5},{5,4},{6,7},{7,6},{8,9},{9,8},{10,11... | collective-permute-start | bytes 1572872 | tf_op jit(solution)/shard_map/ppermute | solution.py:741
  65.5 8.3 %collective-permute-start.17 = (bf16[1,128,1024]{2,1,0:T(8,128)(2,1)S(1)}, bf16[1,128,1024]{2,1,0:T(8,128)(2,1)S(1)}, u32[]{:S(2)}, u32[]{:S(2)}) collective-permute-start(bf16[1,128,1024]{2,1,0:T(8,128)(2,1)S(1)} %get-tuple-element.60), channel_id=1, source_target_pairs={{0,4},{12,8},{1,5},{13,9},{2,6},{14,10},{3,7},{15,11},{16,20},{28,... | collective-permute-start | bytes 786440 | tf_op jit(solution)/shard_map/ppermute | solution.py:751
  70.0 4.6 %collective-permute-start.15 = (bf16[1,128,1024]{2,1,0:T(8,128)(2,1)S(1)}, bf16[1,128,1024]{2,1,0:T(8,128)(2,1)S(1)}, u32[]{:S(2)}, u32[]{:S(2)}) collective-permute-start(bf16[1,128,1024]{2,1,0:T(8,128)(2,1)S(1)} %shard_map.112), channel_id=1, source_target_pairs={{4,8},{8,4},{5,9},{9,5},{6,10},{10,6},{7,11},{11,7},{20,24},{24,20... | collective-permute-start | bytes 786440 | tf_op jit(solution)/shard_map/ppermute | solution.py:751
  73.9 2.1 %collective-permute-start.21 = (bf16[1,128,1024]{2,1,0:T(8,128)(2,1)S(1)}, bf16[1,128,1024]{2,1,0:T(8,128)(2,1)S(1)}, u32[]{:S(2)}, u32[]{:S(2)}) collective-permute-start(bf16[1,128,1024]{2,1,0:T(8,128)(2,1)S(1)} %shard_map.115), channel_id=1, source_target_pairs={{4,8},{8,4},{5,9},{9,5},{6,10},{10,6},{7,11},{11,7},{20,24},{24,20... | collective-permute-start | bytes 786440 | tf_op jit(solution)/shard_map/ppermute | solution.py:751
  74.7 14.7 %collective-permute-start.16 = (bf16[1,128,1024]{2,1,0:T(8,128)(2,1)S(1)}, bf16[1,128,1024]{2,1,0:T(8,128)(2,1)S(1)}, u32[]{:S(2)}, u32[]{:S(2)}) collective-permute-start(bf16[1,128,1024]{2,1,0:T(8,128)(2,1)S(1)} %shard_map.113), channel_id=1, source_target_pairs={{4,0},{8,12},{5,1},{9,13},{6,2},{10,14},{7,3},{11,15},{20,16},{24,... | collective-permute-start | bytes 786440 | tf_op jit(solution)/shard_map/ppermute | solution.py:751
  76.1 23.2 %collective-permute-start.22 = (bf16[1,128,1024]{2,1,0:T(8,128)(2,1)S(1)}, bf16[1,128,1024]{2,1,0:T(8,128)(2,1)S(1)}, u32[]{:S(2)}, u32[]{:S(2)}) collective-permute-start(bf16[1,128,1024]{2,1,0:T(8,128)(2,1)S(1)} %shard_map.116), channel_id=1, source_target_pairs={{4,0},{8,12},{5,1},{9,13},{6,2},{10,14},{7,3},{11,15},{20,16},{24,... | collective-permute-start | bytes 786440 | tf_op jit(solution)/shard_map/ppermute | solution.py:751
  90.1 18.6 %collective-permute-start.18 = (bf16[256,384]{1,0:T(8,128)(2,1)S(1)}, bf16[256,384]{1,0:T(8,128)(2,1)S(1)}, u32[]{:S(2)}, u32[]{:S(2)}) collective-permute-start(bf16[256,384]{1,0:T(8,128)(2,1)S(1)} %shard_map.114.refs_4_), channel_id=1, source_target_pairs={{0,12},{4,0},{8,4},{12,8},{1,13},{5,1},{9,5},{13,9},{2,14},{6,2},{... | collective-permute-start | bytes 589832 | tf_op jit(solution)/shard_map/ppermute | solution.py:761
  91.0 19.3 %collective-permute-start.19 = (bf16[256,384]{1,0:T(8,128)(2,1)S(1)}, bf16[256,384]{1,0:T(8,128)(2,1)S(1)}, u32[]{:S(2)}, u32[]{:S(2)}) collective-permute-start(bf16[256,384]{1,0:T(8,128)(2,1)S(1)} %shard_map.114.refs_4_), channel_id=1, source_target_pairs={{0,8},{4,12},{8,0},{12,4},{1,9},{5,13},{9,1},{13,5},{2,10},{6,14},... | collective-permute-start | bytes 589832 | tf_op jit(solution)/shard_map/ppermute | solution.py:761
  91.5 18.7 %collective-permute-start.20 = (bf16[256,384]{1,0:T(8,128)(2,1)S(1)}, bf16[256,384]{1,0:T(8,128)(2,1)S(1)}, u32[]{:S(2)}, u32[]{:S(2)}) collective-permute-start(bf16[256,384]{1,0:T(8,128)(2,1)S(1)} %shard_map.114.refs_4_), channel_id=1, source_target_pairs={{0,4},{4,8},{8,12},{12,0},{1,5},{5,9},{9,13},{13,1},{2,6},{6,10},{... | collective-permute-start | bytes 589832 | tf_op jit(solution)/shard_map/ppermute | solution.py:761
  99.7 16.9 %collective-permute-start.23 = (bf16[256,128]{1,0:T(8,128)(2,1)S(1)}, bf16[256,128]{1,0:T(8,128)(2,1)S(1)}, u32[]{:S(2)}, u32[]{:S(2)}) collective-permute-start(bf16[256,128]{1,0:T(8,128)(2,1)S(1)} %shard_map.117.refs_8_), channel_id=1, source_target_pairs={{0,12},{4,0},{8,4},{12,8},{1,13},{5,1},{9,5},{13,9},{2,14},{6,2},{... | collective-permute-start | bytes 196616 | tf_op jit(solution)/shard_map/ppermute | solution.py:761
  108.7 7.9 %collective-permute-start.24 = (bf16[256,128]{1,0:T(8,128)(2,1)S(1)}, bf16[256,128]{1,0:T(8,128)(2,1)S(1)}, u32[]{:S(2)}, u32[]{:S(2)}) collective-permute-start(bf16[256,128]{1,0:T(8,128)(2,1)S(1)} %shard_map.117.refs_8_), channel_id=1, source_target_pairs={{0,8},{4,12},{8,0},{12,4},{1,9},{5,13},{9,1},{13,5},{2,10},{6,14},... | collective-permute-start | bytes 196616 | tf_op jit(solution)/shard_map/ppermute | solution.py:761
  108.7 7.9 %collective-permute-start.25 = (bf16[256,128]{1,0:T(8,128)(2,1)S(1)}, bf16[256,128]{1,0:T(8,128)(2,1)S(1)}, u32[]{:S(2)}, u32[]{:S(2)}) collective-permute-start(bf16[256,128]{1,0:T(8,128)(2,1)S(1)} %shard_map.117.refs_8_), channel_id=1, source_target_pairs={{0,4},{4,8},{8,12},{12,0},{1,5},{5,9},{9,13},{13,1},{2,6},{6,10},{... | collective-permute-start | bytes 196616 | tf_op jit(solution)/shard_map/ppermute | solution.py:761
  110.3 1.8 %copy-start.6 = (f32[32]{0:T(128)S(1)}, f32[32]{0:T(128)}, u32[]{:S(2)}) copy-start(f32[32]{0:T(128)} %skip_ref.1) | copy-start | bytes 388

commit v2 on v1

--- a/solution.py
+++ b/solution.py
@@ -762,19 +762,17 @@
         ]
         for grad in (first, last)
     )
-    decayed = held(decayed, last)
+    ssd_output = output(
+        None, inner_values, held(cum, last), cumt, skip_gain,
+        projs, [a[0] for a in arrived], [a[1:] for a in arrived],
+    )
+    decayed = held(decayed, ssd_output)
     updated = None
     for p in spans:
         updated = update(
             turned_hidden, firsts, lasts if p else [], decayed, keep, 2 * STATE, p, p, updated,
             16 * MIB,
         )
-        if not p:
-            cum = held(cum, *updated)
-    ssd_output = output(
-        None, inner_values, cum, cumt, skip_gain,
-        projs, [a[0] for a in arrived], [a[1:] for a in arrived],
-    )
     return ssd_output, *updated
 
 

time: 119 us -> 117 us (0.983)
  starting transfers between devices: 51.7 us -> 47.6 us
  waiting for transfers between devices: 40.7 us -> 43.1 us
    ppermute x6, starting transfers between devices: 12.8 us -> 7.95 us  [on_device(): lax.ppermute(grad, 'seq', to_all(seq, seq - distance))]
    ppermute x6, waiting for transfers between devices: 24.4 us -> 28.5 us  [on_device(): arrived[p].append(lax.ppermute(message, 'seq', pairs))]
    ppermute x1, starting transfers between devices: 2.06 us -> 0.07 us  [on_device(): other.append(lax.ppermute(low, 'head', SWAP))]
    ppermute x1, starting transfers between devices: 0.07 us -> 2.01 us  [on_device(): other = [lax.ppermute(top, 'head', SWAP)]]
  transfers between devices with their start and end apart: 26 -> 26, of which waited for: 8 -> 7; matrix products, arithmetic and copies ran while one was open for 1% -> 1% of each run, Pallas kernels for 15% -> 15%
where the time goes in v2:
time: 117 us
  starting transfers between devices  47.6 us (41%)
  waiting for transfers between devices  43.1 us (37%)
  Pallas kernels  20.2 us (17%)
  local copies, waits for them, and re-layouts  4.76 us (4%)
  between operations  1.24 us (1%)
    ppermute x6, waiting for transfers between devices, on_device(): arrived[p].append(lax.ppermute(message, 'seq', pairs))  28.5 us
    ppermute x6, starting transfers between devices, on_device(): arrived[p].append(lax.ppermute(message, 'seq', pairs))  10.9 us
    ppermute x1, starting transfers between devices, on_device(): lax.ppermute(same, axes, block_pairs(seq, False, True))  9.9 us
    ppermute x6, starting transfers between devices, on_device(): lax.ppermute(grad, 'seq', to_all(seq, seq - distance))  7.95 us
    ppermute x1, waiting for transfers between devices, on_device(): lax.ppermute(cross, axes, block_pairs(seq, False, False))  7.58 us
    ppermute x1, starting transfers between devices, on_device(): lax.ppermute(cross, axes, block_pairs(seq, True, False))  7.34 us
    ppermute x1, waiting for transfers between devices, on_device(): relayed = lax.ppermute(hidden[rows:], axes, beside)  5.87 us
    pallas_call x1, Pallas kernels, before(): call(before_kernel, (jax.ShapeDtypeStruct(values.shape, BF16), jax.ShapeD...  5.17 us
  transfers between devices with their start and end apart: 26, of which 7 were waited for; matrix products, arithmetic and copies ran while one was open for 1% of the time, Pallas kernels for 15%

profile of v2, /device:TPU:0, one launch (start us, length us, event | category | flops | bytes accessed | tf_op | source)
XLA Modules:
  0.0 116.9 jit_solution(9771830395072639968)
XLA Ops:
  0.6 0.5 collective-permute-start.1
  1.1 0.1 collective-permute-start.2
  1.2 1.1 fusion
  2.3 1.3 %collective-permute-start.5 = (bf16[128,1024]{1,0:T(8,128)(2,1)S(1)}, bf16[128,1024]{1,0:T(8,128)(2,1)S(1)}, u32[]{:S(2)}, u32[]{:S(2)}) collective-permute-start(bf16[128,1024]{1,0:T(8,128)(2,1)S(1)} %get-tuple-element.73), channel_id=1, source_target_pairs={{1,3},{2,0},{4,6},{7,5},{9,11},{10,8},{12,14},{15,13},{17,19},{18,... | collective-permute-start | bytes 786440 | tf_op jit(solution)/shard_map/ppermute | solution.py:704
  3.6 0.7 collective-permute-start.4
  4.3 0.7 collective-permute-start
  5.0 5.9 %collective-permute-done.5 = bf16[128,1024]{1,0:T(8,128)(2,1)S(1)} collective-permute-done((bf16[128,1024]{1,0:T(8,128)(2,1)S(1)}, bf16[128,1024]{1,0:T(8,128)(2,1)S(1)}, u32[]{:S(2)}, u32[]{:S(2)}) %collective-permute-start.5) | collective-permute-done | bytes 262176 | tf_op jit(solution)/shard_map/ppermute | solution.py:704
  10.8 4.9 %collective-permute-start.6 = (bf16[128,1024]{1,0:T(8,128)(2,1)S(1)}, bf16[128,1024]{1,0:T(8,128)(2,1)S(1)}, u32[]{:S(2)}, u32[]{:S(2)}) collective-permute-start(bf16[128,1024]{1,0:T(8,128)(2,1)S(1)} %collective-permute-done.5), channel_id=1, source_target_pairs={{3,7},{0,9},{6,2},{5,13},{11,6},{8,8},{14,3},{13,12},{19,23},{16,2... | collective-permute-start | bytes 786440 | tf_op jit(solution)/shard_map/ppermute | solution.py:706
  15.8 1.6 %copy-done = f32[1024,512]{1,0:T(8,128)S(1)} copy-done((f32[1024,512]{1,0:T(8,128)S(1)}, f32[1024,512]{1,0:T(8,128)}, u32[]{:S(2)}) %copy-start) | copy-done | bytes 2097176
  17.3 1.0 copy-done.3
  18.4 1.0 copy-done.4
  19.4 1.7 %shard_map.103 = (bf16[1024,512]{1,0:T(8,128)(2,1)S(1)}, f32[1024,512]{1,0:T(8,128)S(1)}, bf16[1024,512]{1,0:T(8,128)(2,1)S(1)}) custom-call(f32[1024,512]{1,0:T(8,128)S(1)} %copy-done, s32[256,512]{1,0:T(8,128)S(1)} %copy-done.4, s32[256,512]{1,0:T(8,128)S(1)} %copy-done.3), custom_call_target="tpu_custom_call" | custom-call | flops 1572864000 | bytes 7340032 | tf_op jit(solution)/shard_map/pallas_call | solution.py:77
  21.1 1.2 %shard_map.104.refs_4_.refs_3_ = bf16[1024,512]{1,0:T(8,128)(2,1)S(1)} custom-call(f32[1024,512]{1,0:T(8,128)S(1)} %collective-permute-done.1.master_ref, s32[256,512]{1,0:T(8,128)S(1)} %collective-permute-done.2.now_ref), custom_call_target="tpu_custom_call" | custom-call | flops 1572864000 | bytes 3670016 | tf_op jit(solution)/shard_map/pallas_call | solution.py:101
  22.4 0.7 shard_map.105
  23.1 0.1 collective-permute-start.7
  23.2 2.0 %collective-permute-start.3 = (bf16[128,1024]{1,0:T(8,128)(2,1)S(1)}, bf16[128,1024]{1,0:T(8,128)(2,1)S(1)}, u32[]{:S(2)}, u32[]{:S(2)}) collective-permute-start(bf16[128,1024]{1,0:T(8,128)(2,1)S(1)} %collective-permute-done.refs_0_), channel_id=1, source_target_pairs={{0,2},{2,0},{1,3},{3,1},{4,6},{6,4},{5,7},{7,5},{8,10},{10,8},{9,1... | collective-permute-start | bytes 786440 | tf_op jit(solution)/shard_map/ppermute | solution.py:713
  25.2 0.7 collective-permute-start.8
  25.9 7.3 %collective-permute-start.9 = (bf16[256,512]{1,0:T(8,128)(2,1)S(1)}, bf16[256,512]{1,0:T(8,128)(2,1)S(1)}, u32[]{:S(2)}, u32[]{:S(2)}) collective-permute-start(bf16[256,512]{1,0:T(8,128)(2,1)S(1)} %get-tuple-element.45), channel_id=1, source_target_pairs={{0,1},{1,8},{2,7},{3,14},{4,5},{5,12},{6,11},{7,2},{8,9},{9,0},{10... | collective-permute-start | bytes 786440 | tf_op jit(solution)/shard_map/ppermute | solution.py:718
  33.2 0.7 shard_map.106
  33.9 9.9 %collective-permute-start.10 = (bf16[256,512]{1,0:T(8,128)(2,1)S(1)}, bf16[256,512]{1,0:T(8,128)(2,1)S(1)}, u32[]{:S(2)}, u32[]{:S(2)}) collective-permute-start(bf16[256,512]{1,0:T(8,128)(2,1)S(1)} %get-tuple-element.41), channel_id=1, source_target_pairs={{0,4},{1,13},{2,2},{3,11},{4,8},{5,1},{6,6},{7,15},{8,12},{9,5},{1... | collective-permute-start | bytes 786440 | tf_op jit(solution)/shard_map/ppermute | solution.py:722
  43.9 5.2 %shard_map.107 = (bf16[256,2048]{1,0:T(8,128)(2,1)S(1)}, bf16[256,2048]{1,0:T(8,128)(2,1)S(1)}, bf16[2,256,256]{2,1,0:T(8,128)(2,1)S(1)}, bf16[2,256,256]{2,1,0:...) custom-call(bf16[256,2048]{1,0:T(8,128)(2,1)S(1)} %copy-done.2, ...), custom_call_target="tpu_custom_call" | custom-call | flops 5242880000 | bytes 4194304 | tf_op jit(solution)/shard_map/pallas_call | solution.py:198
  49.1 1.0 collective-permute-done.9.refs_1_
  50.2 7.6 %collective-permute-done.11.refs_3_ = bf16[256,512]{1,0:T(8,128)(2,1)S(1)} collective-permute-done((bf16[256,512]{1,0:T(8,128)(2,1)S(1)}, bf16[256,512]{1,0:T(8,128)(2,1)S(1)}, u32[]{:S(2)}, u32[]{:S(2)}) %collective-permute-start.11) | collective-permute-done | bytes 262176 | tf_op jit(solution)/shard_map/ppermute | solution.py:723
  57.7 0.5 shard_map.109
  58.2 2.5 %collective-permute-start.12 = (bf16[1,128,1024]{2,1,0:T(8,128)(2,1)S(1)}, bf16[1,128,1024]{2,1,0:T(8,128)(2,1)S(1)}, u32[]{:S(2)}, u32[]{:S(2)}) collective-permute-start(bf16[1,128,1024]{2,1,0:T(8,128)(2,1)S(1)} %get-tuple-element.54), channel_id=1, source_target_pairs={{0,4},{12,8},{1,5},{13,9},{2,6},{14,10},{3,7},{15,11},{16,20},{28,... | collective-permute-start | bytes 786440 | tf_op jit(solution)/shard_map/ppermute | solution.py:751
  60.7 0.2 shard_map.111.refs_0_
  61.0 0.2 shard_map.112.refs_2_
  61.3 0.6 collective-permute-start.16
  61.8 0.5 shard_map.108
  62.3 3.7 %collective-permute-done.12.arrived_ref.refs_2_.near_ref = bf16[1,128,1024]{2,1,0:T(8,128)(2,1)S(1)} collective-permute-done((bf16[1,128,1024]{2,1,0:T(8,128)(2,1)S(1)}, bf16[1,128,1024]{2,1,0:T(8,128)(2,1)S(1)}, u32[]{:S(2)}, u32[]{:S(2)}) %collective-permute-start.12) | collective-permute-done | bytes 262176 | tf_op jit(solution)/shard_map/ppermute | solution.py:751
  65.9 4.4 %collective-permute-start.13 = (bf16[1,128,1024]{2,1,0:T(8,128)(2,1)S(1)}, bf16[1,128,1024]{2,1,0:T(8,128)(2,1)S(1)}, u32[]{:S(2)}, u32[]{:S(2)}) collective-permute-start(bf16[1,128,1024]{2,1,0:T(8,128)(2,1)S(1)} %get-tuple-element.55), channel_id=1, source_target_pairs={{0,4},{12,8},{1,5},{13,9},{2,6},{14,10},{3,7},{15,11},{16,20},{28,... | collective-permute-start | bytes 786440 | tf_op jit(solution)/shard_map/ppermute | solution.py:751
  70.4 0.7 collective-permute-start.18
  71.1 3.5 %collective-permute-done.13.arrived_ref.refs_3_.refs_2_ = bf16[1,128,1024]{2,1,0:T(8,128)(2,1)S(1)} collective-permute-done((bf16[1,128,1024]{2,1,0:T(8,128)(2,1)S(1)}, bf16[1,128,1024]{2,1,0:T(8,128)(2,1)S(1)}, u32[]{:S(2)}, u32[]{:S(2)}) %collective-permute-start.13) | collective-permute-done | bytes 262176 | tf_op jit(solution)/shard_map/ppermute | solution.py:751
  74.7 0.7 collective-permute-start.14
  75.4 0.1 shard_map.116
  75.4 1.3 %collective-permute-start.19 = (bf16[1,128,1024]{2,1,0:T(8,128)(2,1)S(1)}, bf16[1,128,1024]{2,1,0:T(8,128)(2,1)S(1)}, u32[]{:S(2)}, u32[]{:S(2)}) collective-permute-start(bf16[1,128,1024]{2,1,0:T(8,128)(2,1)S(1)} %shard_map.116), channel_id=1, source_target_pairs={{4,0},{8,12},{5,1},{9,13},{6,2},{10,14},{7,3},{11,15},{20,16},{24,... | collective-permute-start | bytes 786440 | tf_op jit(solution)/shard_map/ppermute | solution.py:751
  76.8 1.3 %collective-permute-start.17 = (bf16[1,128,1024]{2,1,0:T(8,128)(2,1)S(1)}, bf16[1,128,1024]{2,1,0:T(8,128)(2,1)S(1)}, u32[]{:S(2)}, u32[]{:S(2)}) collective-permute-start(bf16[1,128,1024]{2,1,0:T(8,128)(2,1)S(1)} %shard_map.113), channel_id=1, source_target_pairs={{4,0},{8,12},{5,1},{9,13},{6,2},{10,14},{7,3},{11,15},{20,16},{24,... | collective-permute-start | bytes 786440 | tf_op jit(solution)/shard_map/ppermute | solution.py:751
  78.1 11.3 %collective-permute-done.19.refs_5_.refs_1_ = bf16[1,128,1024]{2,1,0:T(8,128)(2,1)S(1)} collective-permute-done((bf16[1,128,1024]{2,1,0:T(8,128)(2,1)S(1)}, bf16[1,128,1024]{2,1,0:T(8,128)(2,1)S(1)}, u32[]{:S(2)}, u32[]{:S(2)}) %collective-permute-start.19) | collective-permute-done | bytes 262176 | tf_op jit(solution)/shard_map/ppermute | solution.py:751
  89.4 0.7 shard_map.118.refs_4_
  90.2 1.4 %collective-permute-start.21 = (bf16[256,384]{1,0:T(8,128)(2,1)S(1)}, bf16[256,384]{1,0:T(8,128)(2,1)S(1)}, u32[]{:S(2)}, u32[]{:S(2)}) collective-permute-start(bf16[256,384]{1,0:T(8,128)(2,1)S(1)} %shard_map.118.refs_4_), channel_id=1, source_target_pairs={{0,8},{4,12},{8,0},{12,4},{1,9},{5,13},{9,1},{13,5},{2,10},{6,14},... | collective-permute-start | bytes 589832 | tf_op jit(solution)/shard_map/ppermute | solution.py:761
  91.6 2.6 %collective-permute-start.20 = (bf16[256,384]{1,0:T(8,128)(2,1)S(1)}, bf16[256,384]{1,0:T(8,128)(2,1)S(1)}, u32[]{:S(2)}, u32[]{:S(2)}) collective-permute-start(bf16[256,384]{1,0:T(8,128)(2,1)S(1)} %shard_map.118.refs_4_), channel_id=1, source_target_pairs={{0,12},{4,0},{8,4},{12,8},{1,13},{5,1},{9,5},{13,9},{2,14},{6,2},{... | collective-permute-start | bytes 589832 | tf_op jit(solution)/shard_map/ppermute | solution.py:761
  94.3 10.1 %collective-permute-done.17.refs_1_.refs_7_ = bf16[1,128,1024]{2,1,0:T(8,128)(2,1)S(1)} collective-permute-done((bf16[1,128,1024]{2,1,0:T(8,128)(2,1)S(1)}, bf16[1,128,1024]{2,1,0:T(8,128)(2,1)S(1)}, u32[]{:S(2)}, u32[]{:S(2)}) %collective-permute-start.17) | collective-permute-done | bytes 262176 | tf_op jit(solution)/shard_map/ppermute | solution.py:751
  104.3 0.3 shard_map.114.refs_8_
  104.7 0.1 collective-permute-start.24
  104.8 3.7 %collective-permute-start.23 = (bf16[256,128]{1,0:T(8,128)(2,1)S(1)}, bf16[256,128]{1,0:T(8,128)(2,1)S(1)}, u32[]{:S(2)}, u32[]{:S(2)}) collective-permute-start(bf16[256,128]{1,0:T(8,128)(2,1)S(1)} %shard_map.114.refs_8_), channel_id=1, source_target_pairs={{0,12},{4,0},{8,4},{12,8},{1,13},{5,1},{9,5},{13,9},{2,14},{6,2},{... | collective-permute-start | bytes 196616 | tf_op jit(solution)/shard_map/ppermute | solution.py:761
  108.6 4.5 %shard_map.117 = bf16[256,2048]{1,0:T(8,128)(2,1)} custom-call(f32[32]{0:T(128)S(1)} %copy-done.6, bf16[256,2048]{1,0:T(8,128)(2,1)S(1)} %copy-done.2, f32[2,256,16]{2,1,0:T(8,128)S(1)} %get-tuple-element.62.cum_ref, f32[2,16,256]{2,1,0:T(8,128)S(1)} %get-tuple-element.63.cumt_ref, bf16[256,256]{1,0:T(8,128)(2,1)S(1)} %get-tuple-element.64.refs_0_.proj_ref, ...), custom_call_target="tpu_custom_call" | custom-call | flops 4194304000 | bytes 2621440 | tf_op jit(solution)/shard_map/pallas_call | solution.py:513
  113.0 1.8 %shard_map.119 = (f32[1024,512]{1,0:T(8,128)}, bf16[1024,512]{1,0:T(8,128)(2,1)}) custom-call(bf16[1024,256]{1,0:T(8,128)(2,1)S(1)} %shard_map.111.refs_0_, bf16[1024,256]{1,0:T(8,128)(2,1)S(1)} %collective-permute-done.15.refs_1_, bf16[1024,256]{1,0:T(8,128)(2,1)S(1)} %shard_map.112.refs_2_, bf16[1024,256]{1,0:T(8,128)(2,1)S(1)} %collective-permute-done.16.refs_3_, ...), custom_call_target="tpu_custom_call" | custom-call | flops 536870912 | bytes 5767168 | tf_op jit(solution)/shard_map/pallas_call | solution.py:600
  114.8 1.9 %shard_map.120 = (f32[1024,512]{1,0:T(8,128)}, bf16[1024,512]{1,0:T(8,128)(2,1)}) custom-call(bf16[1024,256]{1,0:T(8,128)(2,1)S(1)} %shard_map.111.refs_0_, bf16[1024,256]{1,0:T(8,128)(2,1)S(1)} %collective-permute-done.15.refs_1_, bf16[1024,256]{1,0:T(8,128)(2,1)S(1)} %shard_map.112.refs_2_, ...), custom_call_target="tpu_custom_call", output_to_operand_aliasing={{0}: (14, {}), {1}: (15, {})} | custom-call | flops 536870912 | bytes 5767168 | tf_op jit(solution)/shard_map/pallas_call | solution.py:600
  (37 shorter events, 0.5 us)
Async XLA Ops:
  0.6 20.5 %collective-permute-start.1 = (f32[1024,512]{1,0:T(8,128)}, f32[1024,512]{1,0:T(8,128)S(1)}, u32[]{:S(2)}, u32[]{:S(2)}) collective-permute-start(f32[1024,512]{1,0:T(8,128)} %master_ref.1), channel_id=1, source_target_pairs={{0,1},{1,0},{2,3},{3,2},{4,5},{5,4},{6,7},{7,6},{8,9},{9,8},{10,11... | collective-permute-start | bytes 6291464 | tf_op jit(solution)/shard_map/ppermute | solution.py:709
  1.1 20.0 %collective-permute-start.2 = (s32[256,512]{1,0:T(8,128)}, s32[256,512]{1,0:T(8,128)S(1)}, u32[]{:S(2)}, u32[]{:S(2)}) collective-permute-start(s32[256,512]{1,0:T(8,128)} %now_ref.1), channel_id=1, source_target_pairs={{0,1},{1,0},{2,3},{3,2},{4,5},{5,4},{6,7},{7,6},{8,9},{9,8},{10,11... | collective-permute-start | bytes 1572872 | tf_op jit(solution)/shard_map/ppermute | solution.py:709
  2.3 8.5 %collective-permute-start.5 = (bf16[128,1024]{1,0:T(8,128)(2,1)S(1)}, bf16[128,1024]{1,0:T(8,128)(2,1)S(1)}, u32[]{:S(2)}, u32[]{:S(2)}) collective-permute-start(bf16[128,1024]{1,0:T(8,128)(2,1)S(1)} %get-tuple-element.73), channel_id=1, source_target_pairs={{1,3},{2,0},{4,6},{7,5},{9,11},{10,8},{12,14},{15,13},{17,19},{18,... | collective-permute-start | bytes 786440 | tf_op jit(solution)/shard_map/ppermute | solution.py:704
  3.6 18.8 %collective-permute-start.4 = (bf16[128,1024]{1,0:T(8,128)(2,1)S(1)}, bf16[128,1024]{1,0:T(8,128)(2,1)S(1)}, u32[]{:S(2)}, u32[]{:S(2)}) collective-permute-start(bf16[128,1024]{1,0:T(8,128)(2,1)S(1)} %get-tuple-element.73), channel_id=1, source_target_pairs={{0,0},{3,14},{5,4},{6,11},{8,1},{11,15},{13,5},{14,10},{16,16},{19... | collective-permute-start | bytes 786440 | tf_op jit(solution)/shard_map/ppermute | solution.py:706
  4.3 18.0 %collective-permute-start = (bf16[128,1024]{1,0:T(8,128)(2,1)S(1)}, bf16[128,1024]{1,0:T(8,128)(2,1)S(1)}, u32[]{:S(2)}, u32[]{:S(2)}) collective-permute-start(bf16[128,1024]{1,0:T(8,128)(2,1)S(1)} %get-tuple-element.74), channel_id=1, source_target_pairs={{0,0},{3,14},{5,4},{6,11},{8,1},{11,15},{13,5},{14,10},{1,7},{2,9}... | collective-permute-start | bytes 786440 | tf_op jit(solution)/shard_map/ppermute | solution.py:705
  10.8 11.5 %collective-permute-start.6 = (bf16[128,1024]{1,0:T(8,128)(2,1)S(1)}, bf16[128,1024]{1,0:T(8,128)(2,1)S(1)}, u32[]{:S(2)}, u32[]{:S(2)}) collective-permute-start(bf16[128,1024]{1,0:T(8,128)(2,1)S(1)} %collective-permute-done.5), channel_id=1, source_target_pairs={{3,7},{0,9},{6,2},{5,13},{11,6},{8,8},{14,3},{13,12},{19,23},{16,2... | collective-permute-start | bytes 786440 | tf_op jit(solution)/shard_map/ppermute | solution.py:706
  15.7 1.6 %copy-start = (f32[1024,512]{1,0:T(8,128)S(1)}, f32[1024,512]{1,0:T(8,128)}, u32[]{:S(2)}) copy-start(f32[1024,512]{1,0:T(8,128)} %master_ref.1) | copy-start | bytes 6291460
  17.3 1.0 copy-start.3
  18.4 1.0 copy-start.4
  22.3 21.6 %copy-start.1 = (bf16[256,2048]{1,0:T(8,128)(2,1)S(1)}, bf16[256,2048]{1,0:T(8,128)(2,1)}, u32[]{:S(2)}) copy-start(bf16[256,2048]{1,0:T(8,128)(2,1)} %dy_ref.1) | copy-start | bytes 3145732
  22.3 21.6 %copy-start.2 = (bf16[256,2048]{1,0:T(8,128)(2,1)S(1)}, bf16[256,2048]{1,0:T(8,128)(2,1)}, u32[]{:S(2)}) copy-start(bf16[256,2048]{1,0:T(8,128)(2,1)} %x_ref.2) | copy-start | bytes 3145732
  22.3 21.6 %copy-start.5 = (f32[256,32]{0,1:T(8,128)S(1)}, f32[256,32]{0,1:T(8,128)}, u32[]{:S(2)}) copy-start(f32[256,32]{0,1:T(8,128)} %param.10) | copy-start | bytes 98308
  23.1 10.1 %collective-permute-start.7 = (bf16[128,1024]{1,0:T(8,128)(2,1)S(1)}, bf16[128,1024]{1,0:T(8,128)(2,1)S(1)}, u32[]{:S(2)}, u32[]{:S(2)}) collective-permute-start(bf16[128,1024]{1,0:T(8,128)(2,1)S(1)} %get-tuple-element.40.refs_1_), channel_id=1, source_target_pairs={{0,2},{2,0},{1,3},{3,1},{4,6},{6,4},{5,7},{7,5},{8,10},{10,8},{9,1... | collective-permute-start | bytes 786440 | tf_op jit(solution)/shard_map/ppermute | solution.py:715
  23.2 10.0 %collective-permute-start.3 = (bf16[128,1024]{1,0:T(8,128)(2,1)S(1)}, bf16[128,1024]{1,0:T(8,128)(2,1)S(1)}, u32[]{:S(2)}, u32[]{:S(2)}) collective-permute-start(bf16[128,1024]{1,0:T(8,128)(2,1)S(1)} %collective-permute-done.refs_0_), channel_id=1, source_target_pairs={{0,2},{2,0},{1,3},{3,1},{4,6},{6,4},{5,7},{7,5},{8,10},{10,8},{9,1... | collective-permute-start | bytes 786440 | tf_op jit(solution)/shard_map/ppermute | solution.py:713
  25.2 23.9 %collective-permute-start.8 = (bf16[256,512]{1,0:T(8,128)(2,1)S(1)}, bf16[256,512]{1,0:T(8,128)(2,1)S(1)}, u32[]{:S(2)}, u32[]{:S(2)}) collective-permute-start(bf16[256,512]{1,0:T(8,128)(2,1)S(1)} %get-tuple-element.44), channel_id=1, source_target_pairs={{0,0},{1,9},{2,6},{3,15},{4,4},{5,13},{6,10},{7,3},{8,8},{9,1},{10... | collective-permute-start | bytes 786440 | tf_op jit(solution)/shard_map/ppermute | solution.py:717
  25.9 24.3 %collective-permute-start.9 = (bf16[256,512]{1,0:T(8,128)(2,1)S(1)}, bf16[256,512]{1,0:T(8,128)(2,1)S(1)}, u32[]{:S(2)}, u32[]{:S(2)}) collective-permute-start(bf16[256,512]{1,0:T(8,128)(2,1)S(1)} %get-tuple-element.45), channel_id=1, source_target_pairs={{0,1},{1,8},{2,7},{3,14},{4,5},{5,12},{6,11},{7,2},{8,9},{9,0},{10... | collective-permute-start | bytes 786440 | tf_op jit(solution)/shard_map/ppermute | solution.py:718
  33.9 23.8 %collective-permute-start.10 = (bf16[256,512]{1,0:T(8,128)(2,1)S(1)}, bf16[256,512]{1,0:T(8,128)(2,1)S(1)}, u32[]{:S(2)}, u32[]{:S(2)}) collective-permute-start(bf16[256,512]{1,0:T(8,128)(2,1)S(1)} %get-tuple-element.41), channel_id=1, source_target_pairs={{0,4},{1,13},{2,2},{3,11},{4,8},{5,1},{6,6},{7,15},{8,12},{9,5},{1... | collective-permute-start | bytes 786440 | tf_op jit(solution)/shard_map/ppermute | solution.py:722
  43.8 13.9 %collective-permute-start.11 = (bf16[256,512]{1,0:T(8,128)(2,1)S(1)}, bf16[256,512]{1,0:T(8,128)(2,1)S(1)}, u32[]{:S(2)}, u32[]{:S(2)}) collective-permute-start(bf16[256,512]{1,0:T(8,128)(2,1)S(1)} %get-tuple-element.46), channel_id=1, source_target_pairs={{0,5},{1,12},{2,3},{3,10},{4,9},{5,0},{6,7},{7,14},{8,13},{9,4},{1... | collective-permute-start | bytes 786440 | tf_op jit(solution)/shard_map/ppermute | solution.py:723
  58.2 7.7 %collective-permute-start.12 = (bf16[1,128,1024]{2,1,0:T(8,128)(2,1)S(1)}, bf16[1,128,1024]{2,1,0:T(8,128)(2,1)S(1)}, u32[]{:S(2)}, u32[]{:S(2)}) collective-permute-start(bf16[1,128,1024]{2,1,0:T(8,128)(2,1)S(1)} %get-tuple-element.54), channel_id=1, source_target_pairs={{0,4},{12,8},{1,5},{13,9},{2,6},{14,10},{3,7},{15,11},{16,20},{28,... | collective-permute-start | bytes 786440 | tf_op jit(solution)/shard_map/ppermute | solution.py:751
  61.0 15.8 %collective-permute-start.15 = (bf16[1024,256]{1,0:T(8,128)(2,1)S(1)}, bf16[1024,256]{1,0:T(8,128)(2,1)S(1)}, u32[]{:S(2)}, u32[]{:S(2)}) collective-permute-start(bf16[1024,256]{1,0:T(8,128)(2,1)S(1)} %shard_map.111.refs_0_), channel_id=1, source_target_pairs={{0,1},{1,0},{2,3},{3,2},{4,5},{5,4},{6,7},{7,6},{8,9},{9,8},{10,11... | collective-permute-start | bytes 1572872 | tf_op jit(solution)/shard_map/ppermute | solution.py:741
  61.3 15.5 %collective-permute-start.16 = (bf16[1024,256]{1,0:T(8,128)(2,1)S(1)}, bf16[1024,256]{1,0:T(8,128)(2,1)S(1)}, u32[]{:S(2)}, u32[]{:S(2)}) collective-permute-start(bf16[1024,256]{1,0:T(8,128)(2,1)S(1)} %shard_map.112.refs_2_), channel_id=1, source_target_pairs={{0,1},{1,0},{2,3},{3,2},{4,5},{5,4},{6,7},{7,6},{8,9},{9,8},{10,11... | collective-permute-start | bytes 1572872 | tf_op jit(solution)/shard_map/ppermute | solution.py:741
  65.9 8.7 %collective-permute-start.13 = (bf16[1,128,1024]{2,1,0:T(8,128)(2,1)S(1)}, bf16[1,128,1024]{2,1,0:T(8,128)(2,1)S(1)}, u32[]{:S(2)}, u32[]{:S(2)}) collective-permute-start(bf16[1,128,1024]{2,1,0:T(8,128)(2,1)S(1)} %get-tuple-element.55), channel_id=1, source_target_pairs={{0,4},{12,8},{1,5},{13,9},{2,6},{14,10},{3,7},{15,11},{16,20},{28,... | collective-permute-start | bytes 786440 | tf_op jit(solution)/shard_map/ppermute | solution.py:751
  70.4 4.9 %collective-permute-start.18 = (bf16[1,128,1024]{2,1,0:T(8,128)(2,1)S(1)}, bf16[1,128,1024]{2,1,0:T(8,128)(2,1)S(1)}, u32[]{:S(2)}, u32[]{:S(2)}) collective-permute-start(bf16[1,128,1024]{2,1,0:T(8,128)(2,1)S(1)} %shard_map.115), channel_id=1, source_target_pairs={{4,8},{8,4},{5,9},{9,5},{6,10},{10,6},{7,11},{11,7},{20,24},{24,20... | collective-permute-start | bytes 786440 | tf_op jit(solution)/shard_map/ppermute | solution.py:751
  74.7 2.1 %collective-permute-start.14 = (bf16[1,128,1024]{2,1,0:T(8,128)(2,1)S(1)}, bf16[1,128,1024]{2,1,0:T(8,128)(2,1)S(1)}, u32[]{:S(2)}, u32[]{:S(2)}) collective-permute-start(bf16[1,128,1024]{2,1,0:T(8,128)(2,1)S(1)} %shard_map.110), channel_id=1, source_target_pairs={{4,8},{8,4},{5,9},{9,5},{6,10},{10,6},{7,11},{11,7},{20,24},{24,20... | collective-permute-start | bytes 786440 | tf_op jit(solution)/shard_map/ppermute | solution.py:751
  75.4 14.0 %collective-permute-start.19 = (bf16[1,128,1024]{2,1,0:T(8,128)(2,1)S(1)}, bf16[1,128,1024]{2,1,0:T(8,128)(2,1)S(1)}, u32[]{:S(2)}, u32[]{:S(2)}) collective-permute-start(bf16[1,128,1024]{2,1,0:T(8,128)(2,1)S(1)} %shard_map.116), channel_id=1, source_target_pairs={{4,0},{8,12},{5,1},{9,13},{6,2},{10,14},{7,3},{11,15},{20,16},{24,... | collective-permute-start | bytes 786440 | tf_op jit(solution)/shard_map/ppermute | solution.py:751
  76.8 27.5 %collective-permute-start.17 = (bf16[1,128,1024]{2,1,0:T(8,128)(2,1)S(1)}, bf16[1,128,1024]{2,1,0:T(8,128)(2,1)S(1)}, u32[]{:S(2)}, u32[]{:S(2)}) collective-permute-start(bf16[1,128,1024]{2,1,0:T(8,128)(2,1)S(1)} %shard_map.113), channel_id=1, source_target_pairs={{4,0},{8,12},{5,1},{9,13},{6,2},{10,14},{7,3},{11,15},{20,16},{24,... | collective-permute-start | bytes 786440 | tf_op jit(solution)/shard_map/ppermute | solution.py:751
  90.2 18.4 %copy-start.6 = (f32[32]{0:T(128)S(1)}, f32[32]{0:T(128)}, u32[]{:S(2)}) copy-start(f32[32]{0:T(128)} %skip_ref.1) | copy-start | bytes 388
  90.2 14.7 %collective-permute-start.22 = (bf16[256,384]{1,0:T(8,128)(2,1)S(1)}, bf16[256,384]{1,0:T(8,128)(2,1)S(1)}, u32[]{:S(2)}, u32[]{:S(2)}) collective-permute-start(bf16[256,384]{1,0:T(8,128)(2,1)S(1)} %shard_map.118.refs_4_), channel_id=1, source_target_pairs={{0,4},{4,8},{8,12},{12,0},{1,5},{5,9},{9,13},{13,1},{2,6},{6,10},{... | collective-permute-start | bytes 589832 | tf_op jit(solution)/shard_map/ppermute | solution.py:761
  90.2 22.8 %collective-permute-start.21 = (bf16[256,384]{1,0:T(8,128)(2,1)S(1)}, bf16[256,384]{1,0:T(8,128)(2,1)S(1)}, u32[]{:S(2)}, u32[]{:S(2)}) collective-permute-start(bf16[256,384]{1,0:T(8,128)(2,1)S(1)} %shard_map.118.refs_4_), channel_id=1, source_target_pairs={{0,8},{4,12},{8,0},{12,4},{1,9},{5,13},{9,1},{13,5},{2,10},{6,14},... | collective-permute-start | bytes 589832 | tf_op jit(solution)/shard_map/ppermute | solution.py:761
  91.6 21.4 %collective-permute-start.20 = (bf16[256,384]{1,0:T(8,128)(2,1)S(1)}, bf16[256,384]{1,0:T(8,128)(2,1)S(1)}, u32[]{:S(2)}, u32[]{:S(2)}) collective-permute-start(bf16[256,384]{1,0:T(8,128)(2,1)S(1)} %shard_map.118.refs_4_), channel_id=1, source_target_pairs={{0,12},{4,0},{8,4},{12,8},{1,13},{5,1},{9,5},{13,9},{2,14},{6,2},{... | collective-permute-start | bytes 589832 | tf_op jit(solution)/shard_map/ppermute | solution.py:761
  104.7 10.1 %collective-permute-start.25 = (bf16[256,128]{1,0:T(8,128)(2,1)S(1)}, bf16[256,128]{1,0:T(8,128)(2,1)S(1)}, u32[]{:S(2)}, u32[]{:S(2)}) collective-permute-start(bf16[256,128]{1,0:T(8,128)(2,1)S(1)} %shard_map.114.refs_8_), channel_id=1, source_target_pairs={{0,4},{4,8},{8,12},{12,0},{1,5},{5,9},{9,13},{13,1},{2,6},{6,10},{... | collective-permute-start | bytes 196616 | tf_op jit(solution)/shard_map/ppermute | solution.py:761
  104.7 10.1 %collective-permute-start.24 = (bf16[256,128]{1,0:T(8,128)(2,1)S(1)}, bf16[256,128]{1,0:T(8,128)(2,1)S(1)}, u32[]{:S(2)}, u32[]{:S(2)}) collective-permute-start(bf16[256,128]{1,0:T(8,128)(2,1)S(1)} %shard_map.114.refs_8_), channel_id=1, source_target_pairs={{0,8},{4,12},{8,0},{12,4},{1,9},{5,13},{9,1},{13,5},{2,10},{6,14},... | collective-permute-start | bytes 196616 | tf_op jit(solution)/shard_map/ppermute | solution.py:761
  104.8 10.0 %collective-permute-start.23 = (bf16[256,128]{1,0:T(8,128)(2,1)S(1)}, bf16[256,128]{1,0:T(8,128)(2,1)S(1)}, u32[]{:S(2)}, u32[]{:S(2)}) collective-permute-start(bf16[256,128]{1,0:T(8,128)(2,1)S(1)} %shard_map.114.refs_8_), channel_id=1, source_target_pairs={{0,12},{4,0},{8,4},{12,8},{1,13},{5,1},{9,5},{13,9},{2,14},{6,2},{... | collective-permute-start | bytes 196616 | tf_op jit(solution)/shard_map/ppermute | solution.py:761

commit v3 on v2

--- a/solution.py
+++ b/solution.py
@@ -251,6 +251,29 @@
     )(*pieces, effective, sibling_effective)
 
 
+def rest_kernel(
+    ready_ref, sibling_ready_ref, piece_ref, weight_ref, sibling_weight_ref, out_ref, sibling_out_ref
+):
+    rows = ready_ref.shape[0]
+    out_ref[:rows, :] = ready_ref[...]
+    sibling_out_ref[:rows, :] = sibling_ready_ref[...]
+    out_ref[rows:, :] = dot(piece_ref[...], weight_ref[...]).astype(BF16)
+    sibling_out_ref[rows:, :] = dot(piece_ref[...], sibling_weight_ref[...]).astype(BF16)
+
+
+def rest_of_partials(ready, piece, effective, sibling_effective):
+    rows, columns = ready[0].shape[0] + piece.shape[0], effective.shape[1]
+    whole = pl.BlockSpec(memory_space=pltpu.VMEM)
+    return call(
+        rest_kernel,
+        (jax.ShapeDtypeStruct((rows, columns), BF16),) * 2,
+        flops=4 * piece.shape[0] * effective.size,
+        moved=(piece.size + 2 * effective.size + 2 * rows * columns) * 2,
+        in_specs=[whole] * 5,
+        out_specs=(whole,) * 2,
+    )(*ready, piece, effective, sibling_effective)
+
+
 def turn_kernel(*refs):
     (*pieces, out_ref) = refs
     start = 0
@@ -717,7 +740,8 @@
         lax.ppermute(same, axes, block_pairs(seq, True, True)),
         lax.ppermute(cross, axes, block_pairs(seq, True, False)),
     ]
-    same, cross = partials(other, effective, sibling_effective)
+    ready = partials(other[:1], effective, sibling_effective)
+    same, cross = rest_of_partials(ready, other[1], effective, sibling_effective)
     terms += [
         lax.ppermute(same, axes, block_pairs(seq, False, True)),
         lax.ppermute(cross, axes, block_pairs(seq, False, False)),
@@ -755,16 +779,20 @@
     (near, *far), (next_near, *next_far) = arrived
     first = first_grads(*projs, xd, yd, mix, mixt, near, far, next_near)
     last = last_grads(projs[1], xd, yd, mix, mixt, next_far)
+    ssd_output = output(
+        None, inner_values, held(cum, last), cumt, skip_gain,
+        projs, [a[0] for a in arrived], [a[1:] for a in arrived],
+    )
     firsts, lasts = (
         [grad]
         + [
-            lax.ppermute(grad, "seq", to_all(seq, seq - distance)) for distance in range(1, seq)
+            lax.ppermute(
+                held(grad, ssd_output) if grad is last and distance == seq - 1 else grad,
+                "seq", to_all(seq, seq - distance),
+            )
+            for distance in range(1, seq)
         ]
         for grad in (first, last)
-    )
-    ssd_output = output(
-        None, inner_values, held(cum, last), cumt, skip_gain,
-        projs, [a[0] for a in arrived], [a[1:] for a in arrived],
     )
     decayed = held(decayed, ssd_output)
     updated = None

time: 117 us -> 117 us (level)
  starting transfers between devices: 47.6 us -> 46.4 us
    ppermute x1, starting transfers between devices: 0.07 us -> 2.06 us  [on_device(): other.append(lax.ppermute(low, 'head', SWAP))]
    ppermute x1, starting transfers between devices: 2.01 us -> 0.07 us  [on_device(): other = [lax.ppermute(top, 'head', SWAP)]]
    ppermute x1, waiting for transfers between devices: 1.05 us -> 2.7 us  [on_device(): lax.ppermute(cross, axes, block_pairs(seq, True, False))]
    ppermute x1, starting transfers between devices: 9.9 us -> 8.67 us  [on_device(): lax.ppermute(same, axes, block_pairs(seq, False, True))]
  transfers between devices with their start and end apart: 26 -> 26, of which waited for: 7 -> 9; matrix products, arithmetic and copies ran while one was open for 1% -> 1% of each run, Pallas kernels for 15% -> 15%
where the time goes in v3:
time: 117 us
  starting transfers between devices  46.4 us (40%)
  waiting for transfers between devices  44.1 us (38%)
  Pallas kernels  20.4 us (17%)
  local copies, waits for them, and re-layouts  4.76 us (4%)
    ppermute x6, waiting for transfers between devices, on_device(): arrived[p].append(lax.ppermute(message, 'seq', pairs))  27.7 us
    ppermute x6, starting transfers between devices, on_device(): arrived[p].append(lax.ppermute(message, 'seq', pairs))  10.8 us
    ppermute x1, starting transfers between devices, on_device(): lax.ppermute(same, axes, block_pairs(seq, False, True))  8.67 us
    ppermute x6, starting transfers between devices, on_device(): lax.ppermute(held(grad, ssd_output) if grad is last and distance == seq -...  8 us
    ppermute x1, starting transfers between devices, on_device(): lax.ppermute(cross, axes, block_pairs(seq, True, False))  7.26 us
    ppermute x1, waiting for transfers between devices, on_device(): lax.ppermute(cross, axes, block_pairs(seq, False, False))  6.98 us
    ppermute x1, waiting for transfers between devices, on_device(): relayed = lax.ppermute(hidden[rows:], axes, beside)  5.87 us
    pallas_call x1, Pallas kernels, before(): call(before_kernel, (jax.ShapeDtypeStruct(values.shape, BF16), jax.ShapeD...  5.18 us
  transfers between devices with their start and end apart: 26, of which 9 were waited for; matrix products, arithmetic and copies ran while one was open for 1% of the time, Pallas kernels for 15%

profile of v3, /device:TPU:0, one launch (start us, length us, event | category | flops | bytes accessed | tf_op | source)
XLA Modules:
  0.0 116.7 jit_solution(12933756999167241972)
XLA Ops:
  0.6 0.5 collective-permute-start.1
  1.1 0.1 collective-permute-start.2
  1.2 1.1 fusion
  2.3 1.3 %collective-permute-start.5 = (bf16[128,1024]{1,0:T(8,128)(2,1)S(1)}, bf16[128,1024]{1,0:T(8,128)(2,1)S(1)}, u32[]{:S(2)}, u32[]{:S(2)}) collective-permute-start(bf16[128,1024]{1,0:T(8,128)(2,1)S(1)} %get-tuple-element.79), channel_id=1, source_target_pairs={{1,3},{2,0},{4,6},{7,5},{9,11},{10,8},{12,14},{15,13},{17,19},{18,... | collective-permute-start | bytes 786440 | tf_op jit(solution)/shard_map/ppermute | solution.py:727
  3.6 0.7 collective-permute-start.4
  4.3 0.7 collective-permute-start
  5.0 5.9 %collective-permute-done.5 = bf16[128,1024]{1,0:T(8,128)(2,1)S(1)} collective-permute-done((bf16[128,1024]{1,0:T(8,128)(2,1)S(1)}, bf16[128,1024]{1,0:T(8,128)(2,1)S(1)}, u32[]{:S(2)}, u32[]{:S(2)}) %collective-permute-start.5) | collective-permute-done | bytes 262176 | tf_op jit(solution)/shard_map/ppermute | solution.py:727
  10.8 4.9 %collective-permute-start.6 = (bf16[128,1024]{1,0:T(8,128)(2,1)S(1)}, bf16[128,1024]{1,0:T(8,128)(2,1)S(1)}, u32[]{:S(2)}, u32[]{:S(2)}) collective-permute-start(bf16[128,1024]{1,0:T(8,128)(2,1)S(1)} %collective-permute-done.5), channel_id=1, source_target_pairs={{3,7},{0,9},{6,2},{5,13},{11,6},{8,8},{14,3},{13,12},{19,23},{16,2... | collective-permute-start | bytes 786440 | tf_op jit(solution)/shard_map/ppermute | solution.py:729
  15.8 1.6 %copy-done = f32[1024,512]{1,0:T(8,128)S(1)} copy-done((f32[1024,512]{1,0:T(8,128)S(1)}, f32[1024,512]{1,0:T(8,128)}, u32[]{:S(2)}) %copy-start) | copy-done | bytes 2097176
  17.3 1.0 copy-done.3
  18.4 1.0 copy-done.4
  19.4 1.7 %shard_map.103 = (bf16[1024,512]{1,0:T(8,128)(2,1)S(1)}, f32[1024,512]{1,0:T(8,128)S(1)}, bf16[1024,512]{1,0:T(8,128)(2,1)S(1)}) custom-call(f32[1024,512]{1,0:T(8,128)S(1)} %copy-done, s32[256,512]{1,0:T(8,128)S(1)} %copy-done.4, s32[256,512]{1,0:T(8,128)S(1)} %copy-done.3), custom_call_target="tpu_custom_call" | custom-call | flops 1572864000 | bytes 7340032 | tf_op jit(solution)/shard_map/pallas_call | solution.py:77
  21.1 1.2 %shard_map.104.refs_2_.refs_4_.sibling_weight_ref = bf16[1024,512]{1,0:T(8,128)(2,1)S(1)} custom-call(f32[1024,512]{1,0:T(8,128)S(1)} %collective-permute-done.1.master_ref, s32[256,512]{1,0:T(8,128)S(1)} %collective-permute-done.2.now_ref), custom_call_target="tpu_custom_call" | custom-call | flops 1572864000 | bytes 3670016 | tf_op jit(solution)/shard_map/pallas_call | solution.py:101
  22.4 0.7 shard_map.106
  23.1 2.1 %collective-permute-start.7 = (bf16[128,1024]{1,0:T(8,128)(2,1)S(1)}, bf16[128,1024]{1,0:T(8,128)(2,1)S(1)}, u32[]{:S(2)}, u32[]{:S(2)}) collective-permute-start(bf16[128,1024]{1,0:T(8,128)(2,1)S(1)} %get-tuple-element.45.refs_1_), channel_id=1, source_target_pairs={{0,2},{2,0},{1,3},{3,1},{4,6},{6,4},{5,7},{7,5},{8,10},{10,8},{9,1... | collective-permute-start | bytes 786440 | tf_op jit(solution)/shard_map/ppermute | solution.py:738
  25.2 0.7 collective-permute-start.8
  25.9 7.3 %collective-permute-start.9 = (bf16[256,512]{1,0:T(8,128)(2,1)S(1)}, bf16[256,512]{1,0:T(8,128)(2,1)S(1)}, u32[]{:S(2)}, u32[]{:S(2)}) collective-permute-start(bf16[256,512]{1,0:T(8,128)(2,1)S(1)} %get-tuple-element.50), channel_id=1, source_target_pairs={{0,1},{1,8},{2,7},{3,14},{4,5},{5,12},{6,11},{7,2},{8,9},{9,0},{10... | collective-permute-start | bytes 786440 | tf_op jit(solution)/shard_map/ppermute | solution.py:741
  33.2 0.4 shard_map.105
  33.6 0.4 shard_map.107
  34.1 8.7 %collective-permute-start.10 = (bf16[256,512]{1,0:T(8,128)(2,1)S(1)}, bf16[256,512]{1,0:T(8,128)(2,1)S(1)}, u32[]{:S(2)}, u32[]{:S(2)}) collective-permute-start(bf16[256,512]{1,0:T(8,128)(2,1)S(1)} %get-tuple-element.46), channel_id=1, source_target_pairs={{0,4},{1,13},{2,2},{3,11},{4,8},{5,1},{6,6},{7,15},{8,12},{9,5},{1... | collective-permute-start | bytes 786440 | tf_op jit(solution)/shard_map/ppermute | solution.py:746
  42.8 5.2 %shard_map.108 = (bf16[256,2048]{1,0:T(8,128)(2,1)S(1)}, bf16[256,2048]{1,0:T(8,128)(2,1)S(1)}, bf16[2,256,256]{2,1,0:T(8,128)(2,1)S(1)}, bf16[2,256,256]{2,1,0:...) custom-call(bf16[256,2048]{1,0:T(8,128)(2,1)S(1)} %copy-done.2, ...), custom_call_target="tpu_custom_call" | custom-call | flops 5242880000 | bytes 4194304 | tf_op jit(solution)/shard_map/pallas_call | solution.py:198
  48.0 2.7 %collective-permute-done.9.refs_1_ = bf16[256,512]{1,0:T(8,128)(2,1)S(1)} collective-permute-done((bf16[256,512]{1,0:T(8,128)(2,1)S(1)}, bf16[256,512]{1,0:T(8,128)(2,1)S(1)}, u32[]{:S(2)}, u32[]{:S(2)}) %collective-permute-start.9) | collective-permute-done | bytes 262176 | tf_op jit(solution)/shard_map/ppermute | solution.py:741
  50.7 7.0 %collective-permute-done.11.refs_3_ = bf16[256,512]{1,0:T(8,128)(2,1)S(1)} collective-permute-done((bf16[256,512]{1,0:T(8,128)(2,1)S(1)}, bf16[256,512]{1,0:T(8,128)(2,1)S(1)}, u32[]{:S(2)}, u32[]{:S(2)}) %collective-permute-start.11) | collective-permute-done | bytes 262176 | tf_op jit(solution)/shard_map/ppermute | solution.py:747
  57.7 0.5 shard_map.110
  58.2 2.5 %collective-permute-start.12 = (bf16[1,128,1024]{2,1,0:T(8,128)(2,1)S(1)}, bf16[1,128,1024]{2,1,0:T(8,128)(2,1)S(1)}, u32[]{:S(2)}, u32[]{:S(2)}) collective-permute-start(bf16[1,128,1024]{2,1,0:T(8,128)(2,1)S(1)} %get-tuple-element.59), channel_id=1, source_target_pairs={{0,4},{12,8},{1,5},{13,9},{2,6},{14,10},{3,7},{15,11},{16,20},{28,... | collective-permute-start | bytes 786440 | tf_op jit(solution)/shard_map/ppermute | solution.py:775
  60.7 0.2 shard_map.112.refs_0_
  61.0 0.2 shard_map.113.refs_2_
  61.2 0.6 collective-permute-start.16
  61.8 0.5 shard_map.109
  62.2 3.2 %collective-permute-done.12.arrived_ref.refs_2_.near_ref = bf16[1,128,1024]{2,1,0:T(8,128)(2,1)S(1)} collective-permute-done((bf16[1,128,1024]{2,1,0:T(8,128)(2,1)S(1)}, bf16[1,128,1024]{2,1,0:T(8,128)(2,1)S(1)}, u32[]{:S(2)}, u32[]{:S(2)}) %collective-permute-start.12) | collective-permute-done | bytes 262176 | tf_op jit(solution)/shard_map/ppermute | solution.py:775
  65.5 4.4 %collective-permute-start.13 = (bf16[1,128,1024]{2,1,0:T(8,128)(2,1)S(1)}, bf16[1,128,1024]{2,1,0:T(8,128)(2,1)S(1)}, u32[]{:S(2)}, u32[]{:S(2)}) collective-permute-start(bf16[1,128,1024]{2,1,0:T(8,128)(2,1)S(1)} %get-tuple-element.60), channel_id=1, source_target_pairs={{0,4},{12,8},{1,5},{13,9},{2,6},{14,10},{3,7},{15,11},{16,20},{28,... | collective-permute-start | bytes 786440 | tf_op jit(solution)/shard_map/ppermute | solution.py:775
  69.9 0.7 collective-permute-start.18
  70.6 3.1 %collective-permute-done.13.arrived_ref.refs_3_.refs_2_ = bf16[1,128,1024]{2,1,0:T(8,128)(2,1)S(1)} collective-permute-done((bf16[1,128,1024]{2,1,0:T(8,128)(2,1)S(1)}, bf16[1,128,1024]{2,1,0:T(8,128)(2,1)S(1)}, u32[]{:S(2)}, u32[]{:S(2)}) %collective-permute-start.13) | collective-permute-done | bytes 262176 | tf_op jit(solution)/shard_map/ppermute | solution.py:775
  73.8 0.7 collective-permute-start.14
  74.6 1.3 %collective-permute-start.19 = (bf16[1,128,1024]{2,1,0:T(8,128)(2,1)S(1)}, bf16[1,128,1024]{2,1,0:T(8,128)(2,1)S(1)}, u32[]{:S(2)}, u32[]{:S(2)}) collective-permute-start(bf16[1,128,1024]{2,1,0:T(8,128)(2,1)S(1)} %shard_map.117), channel_id=1, source_target_pairs={{4,0},{8,12},{5,1},{9,13},{6,2},{10,14},{7,3},{11,15},{20,16},{24,... | collective-permute-start | bytes 786440 | tf_op jit(solution)/shard_map/ppermute | solution.py:775
  76.0 1.3 %collective-permute-start.17 = (bf16[1,128,1024]{2,1,0:T(8,128)(2,1)S(1)}, bf16[1,128,1024]{2,1,0:T(8,128)(2,1)S(1)}, u32[]{:S(2)}, u32[]{:S(2)}) collective-permute-start(bf16[1,128,1024]{2,1,0:T(8,128)(2,1)S(1)} %shard_map.114), channel_id=1, source_target_pairs={{4,0},{8,12},{5,1},{9,13},{6,2},{10,14},{7,3},{11,15},{20,16},{24,... | collective-permute-start | bytes 786440 | tf_op jit(solution)/shard_map/ppermute | solution.py:775
  77.3 12.1 %collective-permute-done.19.refs_5_.refs_1_ = bf16[1,128,1024]{2,1,0:T(8,128)(2,1)S(1)} collective-permute-done((bf16[1,128,1024]{2,1,0:T(8,128)(2,1)S(1)}, bf16[1,128,1024]{2,1,0:T(8,128)(2,1)S(1)}, u32[]{:S(2)}, u32[]{:S(2)}) %collective-permute-start.19) | collective-permute-done | bytes 262176 | tf_op jit(solution)/shard_map/ppermute | solution.py:775
  89.4 0.7 shard_map.119.refs_4_
  90.2 1.4 %collective-permute-start.21 = (bf16[256,384]{1,0:T(8,128)(2,1)S(1)}, bf16[256,384]{1,0:T(8,128)(2,1)S(1)}, u32[]{:S(2)}, u32[]{:S(2)}) collective-permute-start(bf16[256,384]{1,0:T(8,128)(2,1)S(1)} %shard_map.119.refs_4_), channel_id=1, source_target_pairs={{0,8},{4,12},{8,0},{12,4},{1,9},{5,13},{9,1},{13,5},{2,10},{6,14},... | collective-permute-start | bytes 589832 | tf_op jit(solution)/shard_map/ppermute | solution.py:789
  91.6 2.6 %collective-permute-start.20 = (bf16[256,384]{1,0:T(8,128)(2,1)S(1)}, bf16[256,384]{1,0:T(8,128)(2,1)S(1)}, u32[]{:S(2)}, u32[]{:S(2)}) collective-permute-start(bf16[256,384]{1,0:T(8,128)(2,1)S(1)} %shard_map.119.refs_4_), channel_id=1, source_target_pairs={{0,12},{4,0},{8,4},{12,8},{1,13},{5,1},{9,5},{13,9},{2,14},{6,2},{... | collective-permute-start | bytes 589832 | tf_op jit(solution)/shard_map/ppermute | solution.py:789
  94.2 9.2 %collective-permute-done.17.refs_1_.refs_7_ = bf16[1,128,1024]{2,1,0:T(8,128)(2,1)S(1)} collective-permute-done((bf16[1,128,1024]{2,1,0:T(8,128)(2,1)S(1)}, bf16[1,128,1024]{2,1,0:T(8,128)(2,1)S(1)}, u32[]{:S(2)}, u32[]{:S(2)}) %collective-permute-start.17) | collective-permute-done | bytes 262176 | tf_op jit(solution)/shard_map/ppermute | solution.py:775
  103.5 0.3 shard_map.115.refs_8_
  103.9 4.5 %shard_map.118 = bf16[256,2048]{1,0:T(8,128)(2,1)} custom-call(f32[32]{0:T(128)S(1)} %copy-done.6, bf16[256,2048]{1,0:T(8,128)(2,1)S(1)} %copy-done.2, f32[2,256,16]{2,1,0:T(8,128)S(1)} %get-tuple-element.67.cum_ref, f32[2,16,256]{2,1,0:T(8,128)S(1)} %get-tuple-element.68.cumt_ref, bf16[256,256]{1,0:T(8,128)(2,1)S(1)} %get-tuple-element.69.refs_0_.proj_ref, ...), custom_call_target="tpu_custom_call" | custom-call | flops 4194304000 | bytes 2621440 | tf_op jit(solution)/shard_map/pallas_call | solution.py:536
  108.4 3.8 %collective-permute-start.23 = (bf16[256,128]{1,0:T(8,128)(2,1)S(1)}, bf16[256,128]{1,0:T(8,128)(2,1)S(1)}, u32[]{:S(2)}, u32[]{:S(2)}) collective-permute-start(bf16[256,128]{1,0:T(8,128)(2,1)S(1)} %shard_map.115.refs_8_), channel_id=1, source_target_pairs={{0,12},{4,0},{8,4},{12,8},{1,13},{5,1},{9,5},{13,9},{2,14},{6,2},{... | collective-permute-start | bytes 196616 | tf_op jit(solution)/shard_map/ppermute | solution.py:789
  112.2 1.8 %shard_map.120 = (f32[1024,512]{1,0:T(8,128)}, bf16[1024,512]{1,0:T(8,128)(2,1)}) custom-call(bf16[1024,256]{1,0:T(8,128)(2,1)S(1)} %shard_map.112.refs_0_, bf16[1024,256]{1,0:T(8,128)(2,1)S(1)} %collective-permute-done.15.refs_1_, bf16[1024,256]{1,0:T(8,128)(2,1)S(1)} %shard_map.113.refs_2_, bf16[1024,256]{1,0:T(8,128)(2,1)S(1)} %collective-permute-done.16.refs_3_, ...), custom_call_target="tpu_custom_call" | custom-call | flops 536870912 | bytes 5767168 | tf_op jit(solution)/shard_map/pallas_call | solution.py:623
  114.0 0.6 collective-permute-done.25.refs_11_
  114.6 0.2 collective-permute-done.23.refs_9_
  114.8 1.9 %shard_map.121 = (f32[1024,512]{1,0:T(8,128)}, bf16[1024,512]{1,0:T(8,128)(2,1)}) custom-call(bf16[1024,256]{1,0:T(8,128)(2,1)S(1)} %shard_map.112.refs_0_, bf16[1024,256]{1,0:T(8,128)(2,1)S(1)} %collective-permute-done.15.refs_1_, bf16[1024,256]{1,0:T(8,128)(2,1)S(1)} %shard_map.113.refs_2_, ...), custom_call_target="tpu_custom_call", output_to_operand_aliasing={{0}: (14, {}), {1}: (15, {})} | custom-call | flops 536870912 | bytes 5767168 | tf_op jit(solution)/shard_map/pallas_call | solution.py:623
  (38 shorter events, 0.7 us)
Async XLA Ops:
  0.6 20.5 %collective-permute-start.1 = (f32[1024,512]{1,0:T(8,128)}, f32[1024,512]{1,0:T(8,128)S(1)}, u32[]{:S(2)}, u32[]{:S(2)}) collective-permute-start(f32[1024,512]{1,0:T(8,128)} %master_ref.1), channel_id=1, source_target_pairs={{0,1},{1,0},{2,3},{3,2},{4,5},{5,4},{6,7},{7,6},{8,9},{9,8},{10,11... | collective-permute-start | bytes 6291464 | tf_op jit(solution)/shard_map/ppermute | solution.py:732
  1.1 19.9 %collective-permute-start.2 = (s32[256,512]{1,0:T(8,128)}, s32[256,512]{1,0:T(8,128)S(1)}, u32[]{:S(2)}, u32[]{:S(2)}) collective-permute-start(s32[256,512]{1,0:T(8,128)} %now_ref.1), channel_id=1, source_target_pairs={{0,1},{1,0},{2,3},{3,2},{4,5},{5,4},{6,7},{7,6},{8,9},{9,8},{10,11... | collective-permute-start | bytes 1572872 | tf_op jit(solution)/shard_map/ppermute | solution.py:732
  2.3 8.5 %collective-permute-start.5 = (bf16[128,1024]{1,0:T(8,128)(2,1)S(1)}, bf16[128,1024]{1,0:T(8,128)(2,1)S(1)}, u32[]{:S(2)}, u32[]{:S(2)}) collective-permute-start(bf16[128,1024]{1,0:T(8,128)(2,1)S(1)} %get-tuple-element.79), channel_id=1, source_target_pairs={{1,3},{2,0},{4,6},{7,5},{9,11},{10,8},{12,14},{15,13},{17,19},{18,... | collective-permute-start | bytes 786440 | tf_op jit(solution)/shard_map/ppermute | solution.py:727
  3.6 18.8 %collective-permute-start.4 = (bf16[128,1024]{1,0:T(8,128)(2,1)S(1)}, bf16[128,1024]{1,0:T(8,128)(2,1)S(1)}, u32[]{:S(2)}, u32[]{:S(2)}) collective-permute-start(bf16[128,1024]{1,0:T(8,128)(2,1)S(1)} %get-tuple-element.79), channel_id=1, source_target_pairs={{0,0},{3,14},{5,4},{6,11},{8,1},{11,15},{13,5},{14,10},{16,16},{19... | collective-permute-start | bytes 786440 | tf_op jit(solution)/shard_map/ppermute | solution.py:729
  4.3 18.0 %collective-permute-start = (bf16[128,1024]{1,0:T(8,128)(2,1)S(1)}, bf16[128,1024]{1,0:T(8,128)(2,1)S(1)}, u32[]{:S(2)}, u32[]{:S(2)}) collective-permute-start(bf16[128,1024]{1,0:T(8,128)(2,1)S(1)} %get-tuple-element.80), channel_id=1, source_target_pairs={{0,0},{3,14},{5,4},{6,11},{8,1},{11,15},{13,5},{14,10},{1,7},{2,9}... | collective-permute-start | bytes 786440 | tf_op jit(solution)/shard_map/ppermute | solution.py:728
  10.8 11.6 %collective-permute-start.6 = (bf16[128,1024]{1,0:T(8,128)(2,1)S(1)}, bf16[128,1024]{1,0:T(8,128)(2,1)S(1)}, u32[]{:S(2)}, u32[]{:S(2)}) collective-permute-start(bf16[128,1024]{1,0:T(8,128)(2,1)S(1)} %collective-permute-done.5), channel_id=1, source_target_pairs={{3,7},{0,9},{6,2},{5,13},{11,6},{8,8},{14,3},{13,12},{19,23},{16,2... | collective-permute-start | bytes 786440 | tf_op jit(solution)/shard_map/ppermute | solution.py:729
  15.7 1.6 %copy-start = (f32[1024,512]{1,0:T(8,128)S(1)}, f32[1024,512]{1,0:T(8,128)}, u32[]{:S(2)}) copy-start(f32[1024,512]{1,0:T(8,128)} %master_ref.1) | copy-start | bytes 6291460
  17.3 1.0 copy-start.3
  18.4 1.0 copy-start.4
  22.3 10.9 %collective-permute-start.3 = (bf16[128,1024]{1,0:T(8,128)(2,1)S(1)}, bf16[128,1024]{1,0:T(8,128)(2,1)S(1)}, u32[]{:S(2)}, u32[]{:S(2)}) collective-permute-start(bf16[128,1024]{1,0:T(8,128)(2,1)S(1)} %collective-permute-done.refs_0_), channel_id=1, source_target_pairs={{0,2},{2,0},{1,3},{3,1},{4,6},{6,4},{5,7},{7,5},{8,10},{10,8},{9,1... | collective-permute-start | bytes 786440 | tf_op jit(solution)/shard_map/ppermute | solution.py:736
  23.1 10.5 %collective-permute-start.7 = (bf16[128,1024]{1,0:T(8,128)(2,1)S(1)}, bf16[128,1024]{1,0:T(8,128)(2,1)S(1)}, u32[]{:S(2)}, u32[]{:S(2)}) collective-permute-start(bf16[128,1024]{1,0:T(8,128)(2,1)S(1)} %get-tuple-element.45.refs_1_), channel_id=1, source_target_pairs={{0,2},{2,0},{1,3},{3,1},{4,6},{6,4},{5,7},{7,5},{8,10},{10,8},{9,1... | collective-permute-start | bytes 786440 | tf_op jit(solution)/shard_map/ppermute | solution.py:738
  25.2 22.8 %collective-permute-start.8 = (bf16[256,512]{1,0:T(8,128)(2,1)S(1)}, bf16[256,512]{1,0:T(8,128)(2,1)S(1)}, u32[]{:S(2)}, u32[]{:S(2)}) collective-permute-start(bf16[256,512]{1,0:T(8,128)(2,1)S(1)} %get-tuple-element.49), channel_id=1, source_target_pairs={{0,0},{1,9},{2,6},{3,15},{4,4},{5,13},{6,10},{7,3},{8,8},{9,1},{10... | collective-permute-start | bytes 786440 | tf_op jit(solution)/shard_map/ppermute | solution.py:740
  25.9 16.9 %copy-start.1 = (bf16[256,2048]{1,0:T(8,128)(2,1)S(1)}, bf16[256,2048]{1,0:T(8,128)(2,1)}, u32[]{:S(2)}) copy-start(bf16[256,2048]{1,0:T(8,128)(2,1)} %dy_ref.1) | copy-start | bytes 3145732
  25.9 16.9 %copy-start.2 = (bf16[256,2048]{1,0:T(8,128)(2,1)S(1)}, bf16[256,2048]{1,0:T(8,128)(2,1)}, u32[]{:S(2)}) copy-start(bf16[256,2048]{1,0:T(8,128)(2,1)} %x_ref.2) | copy-start | bytes 3145732
  25.9 16.9 %copy-start.5 = (f32[256,32]{0,1:T(8,128)S(1)}, f32[256,32]{0,1:T(8,128)}, u32[]{:S(2)}) copy-start(f32[256,32]{0,1:T(8,128)} %param.10) | copy-start | bytes 98308
  25.9 24.8 %collective-permute-start.9 = (bf16[256,512]{1,0:T(8,128)(2,1)S(1)}, bf16[256,512]{1,0:T(8,128)(2,1)S(1)}, u32[]{:S(2)}, u32[]{:S(2)}) collective-permute-start(bf16[256,512]{1,0:T(8,128)(2,1)S(1)} %get-tuple-element.50), channel_id=1, source_target_pairs={{0,1},{1,8},{2,7},{3,14},{4,5},{5,12},{6,11},{7,2},{8,9},{9,0},{10... | collective-permute-start | bytes 786440 | tf_op jit(solution)/shard_map/ppermute | solution.py:741
  34.1 23.7 %collective-permute-start.10 = (bf16[256,512]{1,0:T(8,128)(2,1)S(1)}, bf16[256,512]{1,0:T(8,128)(2,1)S(1)}, u32[]{:S(2)}, u32[]{:S(2)}) collective-permute-start(bf16[256,512]{1,0:T(8,128)(2,1)S(1)} %get-tuple-element.46), channel_id=1, source_target_pairs={{0,4},{1,13},{2,2},{3,11},{4,8},{5,1},{6,6},{7,15},{8,12},{9,5},{1... | collective-permute-start | bytes 786440 | tf_op jit(solution)/shard_map/ppermute | solution.py:746
  42.8 15.0 %collective-permute-start.11 = (bf16[256,512]{1,0:T(8,128)(2,1)S(1)}, bf16[256,512]{1,0:T(8,128)(2,1)S(1)}, u32[]{:S(2)}, u32[]{:S(2)}) collective-permute-start(bf16[256,512]{1,0:T(8,128)(2,1)S(1)} %get-tuple-element.51), channel_id=1, source_target_pairs={{0,5},{1,12},{2,3},{3,10},{4,9},{5,0},{6,7},{7,14},{8,13},{9,4},{1... | collective-permute-start | bytes 786440 | tf_op jit(solution)/shard_map/ppermute | solution.py:747
  58.2 7.3 %collective-permute-start.12 = (bf16[1,128,1024]{2,1,0:T(8,128)(2,1)S(1)}, bf16[1,128,1024]{2,1,0:T(8,128)(2,1)S(1)}, u32[]{:S(2)}, u32[]{:S(2)}) collective-permute-start(bf16[1,128,1024]{2,1,0:T(8,128)(2,1)S(1)} %get-tuple-element.59), channel_id=1, source_target_pairs={{0,4},{12,8},{1,5},{13,9},{2,6},{14,10},{3,7},{15,11},{16,20},{28,... | collective-permute-start | bytes 786440 | tf_op jit(solution)/shard_map/ppermute | solution.py:775
  60.9 14.9 %collective-permute-start.15 = (bf16[1024,256]{1,0:T(8,128)(2,1)S(1)}, bf16[1024,256]{1,0:T(8,128)(2,1)S(1)}, u32[]{:S(2)}, u32[]{:S(2)}) collective-permute-start(bf16[1024,256]{1,0:T(8,128)(2,1)S(1)} %shard_map.112.refs_0_), channel_id=1, source_target_pairs={{0,1},{1,0},{2,3},{3,2},{4,5},{5,4},{6,7},{7,6},{8,9},{9,8},{10,11... | collective-permute-start | bytes 1572872 | tf_op jit(solution)/shard_map/ppermute | solution.py:765
  61.2 14.7 %collective-permute-start.16 = (bf16[1024,256]{1,0:T(8,128)(2,1)S(1)}, bf16[1024,256]{1,0:T(8,128)(2,1)S(1)}, u32[]{:S(2)}, u32[]{:S(2)}) collective-permute-start(bf16[1024,256]{1,0:T(8,128)(2,1)S(1)} %shard_map.113.refs_2_), channel_id=1, source_target_pairs={{0,1},{1,0},{2,3},{3,2},{4,5},{5,4},{6,7},{7,6},{8,9},{9,8},{10,11... | collective-permute-start | bytes 1572872 | tf_op jit(solution)/shard_map/ppermute | solution.py:765
  65.5 8.3 %collective-permute-start.13 = (bf16[1,128,1024]{2,1,0:T(8,128)(2,1)S(1)}, bf16[1,128,1024]{2,1,0:T(8,128)(2,1)S(1)}, u32[]{:S(2)}, u32[]{:S(2)}) collective-permute-start(bf16[1,128,1024]{2,1,0:T(8,128)(2,1)S(1)} %get-tuple-element.60), channel_id=1, source_target_pairs={{0,4},{12,8},{1,5},{13,9},{2,6},{14,10},{3,7},{15,11},{16,20},{28,... | collective-permute-start | bytes 786440 | tf_op jit(solution)/shard_map/ppermute | solution.py:775
  69.9 4.5 %collective-permute-start.18 = (bf16[1,128,1024]{2,1,0:T(8,128)(2,1)S(1)}, bf16[1,128,1024]{2,1,0:T(8,128)(2,1)S(1)}, u32[]{:S(2)}, u32[]{:S(2)}) collective-permute-start(bf16[1,128,1024]{2,1,0:T(8,128)(2,1)S(1)} %shard_map.116), channel_id=1, source_target_pairs={{4,8},{8,4},{5,9},{9,5},{6,10},{10,6},{7,11},{11,7},{20,24},{24,20... | collective-permute-start | bytes 786440 | tf_op jit(solution)/shard_map/ppermute | solution.py:775
  73.8 2.1 %collective-permute-start.14 = (bf16[1,128,1024]{2,1,0:T(8,128)(2,1)S(1)}, bf16[1,128,1024]{2,1,0:T(8,128)(2,1)S(1)}, u32[]{:S(2)}, u32[]{:S(2)}) collective-permute-start(bf16[1,128,1024]{2,1,0:T(8,128)(2,1)S(1)} %shard_map.111), channel_id=1, source_target_pairs={{4,8},{8,4},{5,9},{9,5},{6,10},{10,6},{7,11},{11,7},{20,24},{24,20... | collective-permute-start | bytes 786440 | tf_op jit(solution)/shard_map/ppermute | solution.py:775
  74.6 14.8 %collective-permute-start.19 = (bf16[1,128,1024]{2,1,0:T(8,128)(2,1)S(1)}, bf16[1,128,1024]{2,1,0:T(8,128)(2,1)S(1)}, u32[]{:S(2)}, u32[]{:S(2)}) collective-permute-start(bf16[1,128,1024]{2,1,0:T(8,128)(2,1)S(1)} %shard_map.117), channel_id=1, source_target_pairs={{4,0},{8,12},{5,1},{9,13},{6,2},{10,14},{7,3},{11,15},{20,16},{24,... | collective-permute-start | bytes 786440 | tf_op jit(solution)/shard_map/ppermute | solution.py:775
  76.0 27.5 %collective-permute-start.17 = (bf16[1,128,1024]{2,1,0:T(8,128)(2,1)S(1)}, bf16[1,128,1024]{2,1,0:T(8,128)(2,1)S(1)}, u32[]{:S(2)}, u32[]{:S(2)}) collective-permute-start(bf16[1,128,1024]{2,1,0:T(8,128)(2,1)S(1)} %shard_map.114), channel_id=1, source_target_pairs={{4,0},{8,12},{5,1},{9,13},{6,2},{10,14},{7,3},{11,15},{20,16},{24,... | collective-permute-start | bytes 786440 | tf_op jit(solution)/shard_map/ppermute | solution.py:775
  90.1 13.8 %copy-start.6 = (f32[32]{0:T(128)S(1)}, f32[32]{0:T(128)}, u32[]{:S(2)}) copy-start(f32[32]{0:T(128)} %skip_ref.1) | copy-start | bytes 388
  90.1 18.3 %collective-permute-start.22 = (bf16[256,384]{1,0:T(8,128)(2,1)S(1)}, bf16[256,384]{1,0:T(8,128)(2,1)S(1)}, u32[]{:S(2)}, u32[]{:S(2)}) collective-permute-start(bf16[256,384]{1,0:T(8,128)(2,1)S(1)} %shard_map.119.refs_4_), channel_id=1, source_target_pairs={{0,4},{4,8},{8,12},{12,0},{1,5},{5,9},{9,13},{13,1},{2,6},{6,10},{... | collective-permute-start | bytes 589832 | tf_op jit(solution)/shard_map/ppermute | solution.py:789
  90.2 22.0 %collective-permute-start.21 = (bf16[256,384]{1,0:T(8,128)(2,1)S(1)}, bf16[256,384]{1,0:T(8,128)(2,1)S(1)}, u32[]{:S(2)}, u32[]{:S(2)}) collective-permute-start(bf16[256,384]{1,0:T(8,128)(2,1)S(1)} %shard_map.119.refs_4_), channel_id=1, source_target_pairs={{0,8},{4,12},{8,0},{12,4},{1,9},{5,13},{9,1},{13,5},{2,10},{6,14},... | collective-permute-start | bytes 589832 | tf_op jit(solution)/shard_map/ppermute | solution.py:789
  91.6 20.6 %collective-permute-start.20 = (bf16[256,384]{1,0:T(8,128)(2,1)S(1)}, bf16[256,384]{1,0:T(8,128)(2,1)S(1)}, u32[]{:S(2)}, u32[]{:S(2)}) collective-permute-start(bf16[256,384]{1,0:T(8,128)(2,1)S(1)} %shard_map.119.refs_4_), channel_id=1, source_target_pairs={{0,12},{4,0},{8,4},{12,8},{1,13},{5,1},{9,5},{13,9},{2,14},{6,2},{... | collective-permute-start | bytes 589832 | tf_op jit(solution)/shard_map/ppermute | solution.py:789
  103.8 10.8 %collective-permute-start.24 = (bf16[256,128]{1,0:T(8,128)(2,1)S(1)}, bf16[256,128]{1,0:T(8,128)(2,1)S(1)}, u32[]{:S(2)}, u32[]{:S(2)}) collective-permute-start(bf16[256,128]{1,0:T(8,128)(2,1)S(1)} %shard_map.115.refs_8_), channel_id=1, source_target_pairs={{0,8},{4,12},{8,0},{12,4},{1,9},{5,13},{9,1},{13,5},{2,10},{6,14},... | collective-permute-start | bytes 196616 | tf_op jit(solution)/shard_map/ppermute | solution.py:789
  108.4 6.2 %collective-permute-start.25 = (bf16[256,128]{1,0:T(8,128)(2,1)S(1)}, bf16[256,128]{1,0:T(8,128)(2,1)S(1)}, u32[]{:S(2)}, u32[]{:S(2)}) collective-permute-start(bf16[256,128]{1,0:T(8,128)(2,1)S(1)} %shard_map.115.refs_8_), channel_id=1, source_target_pairs={{0,4},{4,8},{8,12},{12,0},{1,5},{5,9},{9,13},{13,1},{2,6},{6,10},{... | collective-permute-start | bytes 196616 | tf_op jit(solution)/shard_map/ppermute | solution.py:789
  108.4 6.4 %collective-permute-start.23 = (bf16[256,128]{1,0:T(8,128)(2,1)S(1)}, bf16[256,128]{1,0:T(8,128)(2,1)S(1)}, u32[]{:S(2)}, u32[]{:S(2)}) collective-permute-start(bf16[256,128]{1,0:T(8,128)(2,1)S(1)} %shard_map.115.refs_8_), channel_id=1, source_target_pairs={{0,12},{4,0},{8,4},{12,8},{1,13},{5,1},{9,5},{13,9},{2,14},{6,2},{... | collective-permute-start | bytes 196616 | tf_op jit(solution)/shard_map/ppermute | solution.py:789

commit v4 on v0

--- a/solution.py
+++ b/solution.py
@@ -251,6 +251,29 @@
     )(*pieces, effective, sibling_effective)
 
 
+def rest_kernel(
+    ready_ref, sibling_ready_ref, piece_ref, weight_ref, sibling_weight_ref, out_ref, sibling_out_ref
+):
+    rows = ready_ref.shape[0]
+    out_ref[:rows, :] = ready_ref[...]
+    sibling_out_ref[:rows, :] = sibling_ready_ref[...]
+    out_ref[rows:, :] = dot(piece_ref[...], weight_ref[...]).astype(BF16)
+    sibling_out_ref[rows:, :] = dot(piece_ref[...], sibling_weight_ref[...]).astype(BF16)
+
+
+def rest_of_partials(ready, piece, effective, sibling_effective):
+    rows, columns = ready[0].shape[0] + piece.shape[0], effective.shape[1]
+    whole = pl.BlockSpec(memory_space=pltpu.VMEM)
+    return call(
+        rest_kernel,
+        (jax.ShapeDtypeStruct((rows, columns), BF16),) * 2,
+        flops=4 * piece.shape[0] * effective.size,
+        moved=(piece.size + 2 * effective.size + 2 * rows * columns) * 2,
+        in_specs=[whole] * 5,
+        out_specs=(whole,) * 2,
+    )(*ready, piece, effective, sibling_effective)
+
+
 def turn_kernel(*refs):
     (*pieces, out_ref) = refs
     start = 0
@@ -381,22 +404,16 @@
     )(proj, xd, yd, mix, mixt, near, *far)
 
 
-def output_kernel(parts, hops, ahead, skip_ref, x_ref, cum_ref, cumt_ref, *refs):
-    (*refs, out_ref, proj_ref, start_ref) = refs
-    projs, nears = refs[:parts], refs[parts : 2 * parts]
-    fars = [refs[2 * parts + hops * p : 2 * parts + hops * (p + 1)] for p in range(parts)]
-    each = projs[0].shape[1] // (2 * STATE)
-    for group in range(parts * each):
-        part, at = divmod(group, each)
-
-        @pl.when(pl.program_id(0) == group)
-        def _(part=part, at=at):
-            proj_ref[...] = projs[part][:, at * 2 * STATE : (at + 1) * 2 * STATE]
-
-            def put(start, _):
-                start_ref[...] = added([ref.at[at : at + 1] for ref in start])
-
-            either(ahead, [nears[part]], fars[part], put)
+def output_kernel(
+    ahead, first, skip_ref, x_ref, cum_ref, cumt_ref, proj_ref, near_ref, *refs
+):
+    (*far_refs, out_ref, start_ref) = refs
+    far_refs = [ref for ref in far_refs if ref.shape[1:] == near_ref.shape[1:]]
+
+    def put(start, _):
+        start_ref[...] = added(start)
+
+    either(ahead, [near_ref], far_refs, put)
 
     heads = cum_ref.shape[2]
     half = SPAN // 2
@@ -424,7 +441,7 @@
         carried = dot(read, start_ref[:, cut]) * lanes_of(
             from_start[:, a : a + 1], from_start[:, b : b + 1], wide
         )
-        head = pl.program_id(0) * heads + a
+        head = (pl.program_id(0) + first) * heads + a
         gain = jnp.where(
             lax.broadcasted_iota(jnp.int32, (1, wide), 1) < wide // 2,
             skip_ref[head], skip_ref[head + 1],
@@ -438,28 +455,31 @@
         ).astype(BF16)
 
 
-def output(ahead, values, cum, cumt, skip, projs, nears, fars):
-    groups, _, heads = cum.shape
-    width = values.shape[1] // groups
-    wide = wide_spec(width)
-    pieces = [*projs, *nears, *(ref for far in fars for ref in far)]
-    return call(
-        functools.partial(output_kernel, len(projs), len(fars[0]), ahead),
+def output(ahead, values, cum, cumt, skip, proj, near, far, first, earlier):
+    groups, _, width = near.shape
+    heads = cum.shape[2]
+    wide = pl.BlockSpec((SPAN, width), lambda g: (0, g + first))
+    lead = lead_spec(STATE, width)
+    earlier = [] if earlier is None else [earlier]
+    return call(
+        functools.partial(output_kernel, ahead, first),
         jax.ShapeDtypeStruct(values.shape, BF16),
         flops=groups * heads * SPAN * SPAN * 2000,
-        moved=values.size * 5,
+        moved=groups * SPAN * width * 10,
         exps=groups * heads * SPAN * SPAN,
         grid=(groups,),
         in_specs=[
-            pl.BlockSpec(memory_space=pltpu.SMEM), wide, lead_spec(SPAN, heads),
-            lead_spec(heads, SPAN),
+            pl.BlockSpec(memory_space=pltpu.SMEM), wide,
+            pl.BlockSpec((1, SPAN, heads), lambda g: (g + first, 0, 0)),
+            pl.BlockSpec((1, heads, SPAN), lambda g: (g + first, 0, 0)),
+            pl.BlockSpec((SPAN, 2 * STATE), lambda g: (0, g)),
         ]
-        + [pl.BlockSpec(memory_space=pltpu.VMEM)] * len(pieces),
+        + [lead] * (1 + len(far))
+        + [pl.BlockSpec(memory_space=pl.ANY)] * len(earlier),
         out_specs=wide,
-        scratch_shapes=[
-            pltpu.VMEM((SPAN, 2 * STATE), BF16), pltpu.VMEM((STATE, width), BF16)
-        ],
-    )(skip, values, cum, cumt, *pieces)
+        scratch_shapes=[pltpu.VMEM((STATE, width), BF16)],
+        input_output_aliases={6 + len(far): 0} if earlier else {},
+    )(skip, values, cum, cumt, proj, near, *far, *earlier)
 
 
 def spot_of(block, spots):
@@ -602,7 +622,7 @@
     grad = grads(True, proj, xd, yd, mix, mixt, start, [adjoint_in], 0)
     blocks = [lax.all_gather(grad, "seq", axis=0, tiled=True)]
     ssd_output = output(
-        True, inner_values, cum, cumt, skip_gain, [proj], [start], [[adjoint_in]]
+        True, inner_values, cum, cumt, skip_gain, proj, start, [adjoint_in], 0, None
     )
     return ssd_output, *update([layer.T], blocks, decayed, keep, 0, None, 40 * MIB)
 
@@ -630,7 +650,8 @@
         lax.ppermute(same, axes, block_pairs(seq, True, True)),
         lax.ppermute(cross, axes, block_pairs(seq, True, False)),
     ]
-    same, cross = partials(other, effective, sibling_effective)
+    ready = partials(other[:1], effective, sibling_effective)
+    same, cross = rest_of_partials(ready, other[1], effective, sibling_effective)
     terms += [
         lax.ppermute(same, axes, block_pairs(seq, False, True)),
         lax.ppermute(cross, axes, block_pairs(seq, False, False)),
@@ -665,26 +686,25 @@
         for p in spans:
             if own_terms:
                 messages[p] = handed_on(decay, arrived[p][-1], own_terms[p], p * each)
-    blocks = []
+    gradients, moved, ssd_output = [], [], None
     for p in spans:
-        grad = grads(
-            None, projs[p], xd, yd, mix, mixt, arrived[p][0], arrived[p][1:], p * each
+        near, far = arrived[p][0], arrived[p][1:]
+        proj = projs[p] if not p else held(projs[p], ssd_output)
+        grad = grads(None, proj, xd, yd, mix, mixt, near, far, p * each)
+        ssd_output = output(
+            None, inner_values, held(cum, grad), cumt, skip_gain, projs[p], near, far, p * each,
+            ssd_output,
         )
-        blocks.append([grad])
+        blocks = [grad]
         for distance in range(1, seq):
-            pairs = to_all(seq, seq - distance)
-            blocks[p].append(lax.ppermute(grad, "seq", pairs))
-
-    decayed = held(decayed, blocks[-1][0])
+            if not p and distance == seq - 1:
+                grad = held(grad, ssd_output)
+            blocks.append(lax.ppermute(grad, "seq", to_all(seq, seq - distance)))
+        moved.append(blocks)
+    decayed = held(decayed, ssd_output)
     updated = None
     for p in spans:
-        updated = update(turned_hidden, blocks[p], decayed, keep, p, updated, 16 * MIB)
-        if not p:
-            cum = held(cum, *updated)
-    ssd_output = output(
-        None, inner_values, cum, cumt, skip_gain,
-        projs, [a[0] for a in arrived], [a[1:] for a in arrived],
-    )
+        updated = update(turned_hidden, moved[p], decayed, keep, p, updated, 16 * MIB)
     return ssd_output, *updated
 
 

time: 116 us -> 115 us (level)
  starting transfers between devices: 49.6 us -> 45.5 us
  Pallas kernels: 20.2 us -> 21.9 us
    ppermute x6, starting transfers between devices: 10.7 us -> 7.13 us  [on_device(): blocks.append(lax.ppermute(grad, 'seq', to_all(seq, seq - distance)))]
    pallas_call x1 -> x3, Pallas kernels: 4.49 us -> 6.37 us  [the longest x2 5.93 us: output(): call(functools.partial(output_kernel, ahead, first), jax.ShapeDtypeStruct...]
  transfers between devices with their start and end apart: 26 -> 26, of which waited for: 8 -> 8; matrix products, arithmetic and copies ran while one was open for 1% -> 1% of each run, Pallas kernels for 15% -> 17%
where the time goes in v4:
time: 115 us; the launch traced here: 114 us
  starting transfers between devices  45.5 us (40%)
  waiting for transfers between devices  41.1 us (36%)
  Pallas kernels  21.9 us (19%)
  local copies, waits for them, and re-layouts  4.76 us (4%)
  between operations  1.21 us (1%)
    ppermute x6, waiting for transfers between devices, on_device(): arrived[p].append(lax.ppermute(message, 'seq', pairs))  25 us
    ppermute x6, starting transfers between devices, on_device(): arrived[p].append(lax.ppermute(message, 'seq', pairs))  10.9 us
    ppermute x1, starting transfers between devices, on_device(): lax.ppermute(same, axes, block_pairs(seq, False, True))  8.66 us
    ppermute x1, starting transfers between devices, on_device(): lax.ppermute(cross, axes, block_pairs(seq, True, False))  7.26 us
    ppermute x6, starting transfers between devices, on_device(): blocks.append(lax.ppermute(grad, 'seq', to_all(seq, seq - distance)))  7.13 us
    ppermute x1, waiting for transfers between devices, on_device(): lax.ppermute(cross, axes, block_pairs(seq, False, False))  6.97 us
    pallas_call x2, Pallas kernels, output(): call(functools.partial(output_kernel, ahead, first), jax.ShapeDtypeStruct...  5.93 us
    ppermute x1, waiting for transfers between devices, on_device(): relayed = lax.ppermute(hidden[rows:], axes, beside)  5.87 us
  transfers between devices with their start and end apart: 26, of which 8 were waited for; matrix products, arithmetic and copies ran while one was open for 1% of the time, Pallas kernels for 17%

profile of v4, /device:TPU:0, one launch (start us, length us, event | category | flops | bytes accessed | tf_op | source)
XLA Modules:
  0.0 114.5 jit_solution(17217562629960629826)
XLA Ops:
  0.6 0.5 collective-permute-start.1
  1.2 1.1 fusion
  2.3 1.3 %collective-permute-start.5 = (bf16[128,1024]{1,0:T(8,128)(2,1)S(1)}, bf16[128,1024]{1,0:T(8,128)(2,1)S(1)}, u32[]{:S(2)}, u32[]{:S(2)}) collective-permute-start(bf16[128,1024]{1,0:T(8,128)(2,1)S(1)} %get-tuple-element.83), channel_id=1, source_target_pairs={{1,3},{2,0},{4,6},{7,5},{9,11},{10,8},{12,14},{15,13},{17,19},{18,... | collective-permute-start | bytes 786440 | tf_op jit(solution)/shard_map/ppermute | solution.py:637
  3.6 0.7 collective-permute-start.4
  4.3 0.7 collective-permute-start
  5.0 5.9 %collective-permute-done.5 = bf16[128,1024]{1,0:T(8,128)(2,1)S(1)} collective-permute-done((bf16[128,1024]{1,0:T(8,128)(2,1)S(1)}, bf16[128,1024]{1,0:T(8,128)(2,1)S(1)}, u32[]{:S(2)}, u32[]{:S(2)}) %collective-permute-start.5) | collective-permute-done | bytes 262176 | tf_op jit(solution)/shard_map/ppermute | solution.py:637
  10.8 4.9 %collective-permute-start.6 = (bf16[128,1024]{1,0:T(8,128)(2,1)S(1)}, bf16[128,1024]{1,0:T(8,128)(2,1)S(1)}, u32[]{:S(2)}, u32[]{:S(2)}) collective-permute-start(bf16[128,1024]{1,0:T(8,128)(2,1)S(1)} %collective-permute-done.5), channel_id=1, source_target_pairs={{3,7},{0,9},{6,2},{5,13},{11,6},{8,8},{14,3},{13,12},{19,23},{16,2... | collective-permute-start | bytes 786440 | tf_op jit(solution)/shard_map/ppermute | solution.py:639
  15.8 1.6 %copy-done = f32[1024,512]{1,0:T(8,128)S(1)} copy-done((f32[1024,512]{1,0:T(8,128)S(1)}, f32[1024,512]{1,0:T(8,128)}, u32[]{:S(2)}) %copy-start) | copy-done | bytes 2097176
  17.3 1.0 copy-done.3
  18.4 1.0 copy-done.4
  19.4 1.7 %shard_map.103 = (bf16[1024,512]{1,0:T(8,128)(2,1)S(1)}, f32[1024,512]{1,0:T(8,128)S(1)}, bf16[1024,512]{1,0:T(8,128)(2,1)S(1)}) custom-call(f32[1024,512]{1,0:T(8,128)S(1)} %copy-done, s32[256,512]{1,0:T(8,128)S(1)} %copy-done.4, s32[256,512]{1,0:T(8,128)S(1)} %copy-done.3), custom_call_target="tpu_custom_call" | custom-call | flops 1572864000 | bytes 7340032 | tf_op jit(solution)/shard_map/pallas_call | solution.py:77
  21.1 1.2 %shard_map.104.refs_2_.refs_4_.sibling_weight_ref = bf16[1024,512]{1,0:T(8,128)(2,1)S(1)} custom-call(f32[1024,512]{1,0:T(8,128)S(1)} %collective-permute-done.1.master_ref, s32[256,512]{1,0:T(8,128)S(1)} %collective-permute-done.2.now_ref), custom_call_target="tpu_custom_call" | custom-call | flops 1572864000 | bytes 3670016 | tf_op jit(solution)/shard_map/pallas_call | solution.py:101
  22.4 0.7 shard_map.106
  23.1 2.1 %collective-permute-start.7 = (bf16[128,1024]{1,0:T(8,128)(2,1)S(1)}, bf16[128,1024]{1,0:T(8,128)(2,1)S(1)}, u32[]{:S(2)}, u32[]{:S(2)}) collective-permute-start(bf16[128,1024]{1,0:T(8,128)(2,1)S(1)} %get-tuple-element.47.refs_1_), channel_id=1, source_target_pairs={{0,2},{2,0},{1,3},{3,1},{4,6},{6,4},{5,7},{7,5},{8,10},{10,8},{9,1... | collective-permute-start | bytes 786440 | tf_op jit(solution)/shard_map/ppermute | solution.py:648
  25.2 0.7 collective-permute-start.8
  25.9 7.3 %collective-permute-start.9 = (bf16[256,512]{1,0:T(8,128)(2,1)S(1)}, bf16[256,512]{1,0:T(8,128)(2,1)S(1)}, u32[]{:S(2)}, u32[]{:S(2)}) collective-permute-start(bf16[256,512]{1,0:T(8,128)(2,1)S(1)} %get-tuple-element.52), channel_id=1, source_target_pairs={{0,1},{1,8},{2,7},{3,14},{4,5},{5,12},{6,11},{7,2},{8,9},{9,0},{10... | collective-permute-start | bytes 786440 | tf_op jit(solution)/shard_map/ppermute | solution.py:651
  33.2 0.4 shard_map.105
  33.6 0.4 shard_map.107
  34.1 8.7 %collective-permute-start.10 = (bf16[256,512]{1,0:T(8,128)(2,1)S(1)}, bf16[256,512]{1,0:T(8,128)(2,1)S(1)}, u32[]{:S(2)}, u32[]{:S(2)}) collective-permute-start(bf16[256,512]{1,0:T(8,128)(2,1)S(1)} %get-tuple-element.48), channel_id=1, source_target_pairs={{0,4},{1,13},{2,2},{3,11},{4,8},{5,1},{6,6},{7,15},{8,12},{9,5},{1... | collective-permute-start | bytes 786440 | tf_op jit(solution)/shard_map/ppermute | solution.py:656
  42.9 5.2 %shard_map.108 = (bf16[256,2048]{1,0:T(8,128)(2,1)S(1)}, bf16[256,2048]{1,0:T(8,128)(2,1)S(1)}, bf16[2,256,256]{2,1,0:T(8,128)(2,1)S(1)}, bf16[2,256,256]{2,1,0:...) custom-call(bf16[256,2048]{1,0:T(8,128)(2,1)S(1)} %copy-done.2, ...), custom_call_target="tpu_custom_call" | custom-call | flops 5242880000 | bytes 4194304 | tf_op jit(solution)/shard_map/pallas_call | solution.py:198
  48.0 2.7 %collective-permute-done.9.refs_1_ = bf16[256,512]{1,0:T(8,128)(2,1)S(1)} collective-permute-done((bf16[256,512]{1,0:T(8,128)(2,1)S(1)}, bf16[256,512]{1,0:T(8,128)(2,1)S(1)}, u32[]{:S(2)}, u32[]{:S(2)}) %collective-permute-start.9) | collective-permute-done | bytes 262176 | tf_op jit(solution)/shard_map/ppermute | solution.py:651
  50.8 7.0 %collective-permute-done.11.refs_3_ = bf16[256,512]{1,0:T(8,128)(2,1)S(1)} collective-permute-done((bf16[256,512]{1,0:T(8,128)(2,1)S(1)}, bf16[256,512]{1,0:T(8,128)(2,1)S(1)}, u32[]{:S(2)}, u32[]{:S(2)}) %collective-permute-start.11) | collective-permute-done | bytes 262176 | tf_op jit(solution)/shard_map/ppermute | solution.py:657
  57.7 0.5 shard_map.110
  58.2 2.5 %collective-permute-start.12 = (bf16[1,128,1024]{2,1,0:T(8,128)(2,1)S(1)}, bf16[1,128,1024]{2,1,0:T(8,128)(2,1)S(1)}, u32[]{:S(2)}, u32[]{:S(2)}) collective-permute-start(bf16[1,128,1024]{2,1,0:T(8,128)(2,1)S(1)} %get-tuple-element.60), channel_id=1, source_target_pairs={{0,4},{12,8},{1,5},{13,9},{2,6},{14,10},{3,7},{15,11},{16,20},{28,... | collective-permute-start | bytes 786440 | tf_op jit(solution)/shard_map/ppermute | solution.py:685
  61.0 0.2 shard_map.117.refs_2_
  61.2 0.6 collective-permute-start.18
  61.8 0.5 shard_map.109
  62.3 3.2 %collective-permute-done.12.arrived_ref.near_ref = bf16[1,128,1024]{2,1,0:T(8,128)(2,1)S(1)} collective-permute-done((bf16[1,128,1024]{2,1,0:T(8,128)(2,1)S(1)}, bf16[1,128,1024]{2,1,0:T(8,128)(2,1)S(1)}, u32[]{:S(2)}, u32[]{:S(2)}) %collective-permute-start.12) | collective-permute-done | bytes 262176 | tf_op jit(solution)/shard_map/ppermute | solution.py:685
  65.5 4.4 %collective-permute-start.15 = (bf16[1,128,1024]{2,1,0:T(8,128)(2,1)S(1)}, bf16[1,128,1024]{2,1,0:T(8,128)(2,1)S(1)}, u32[]{:S(2)}, u32[]{:S(2)}) collective-permute-start(bf16[1,128,1024]{2,1,0:T(8,128)(2,1)S(1)} %get-tuple-element.68), channel_id=1, source_target_pairs={{0,4},{12,8},{1,5},{13,9},{2,6},{14,10},{3,7},{15,11},{16,20},{28,... | collective-permute-start | bytes 786440 | tf_op jit(solution)/shard_map/ppermute | solution.py:685
  70.0 0.7 collective-permute-start.13
  70.6 3.1 %collective-permute-done.15.arrived_ref.near_ref = bf16[1,128,1024]{2,1,0:T(8,128)(2,1)S(1)} collective-permute-done((bf16[1,128,1024]{2,1,0:T(8,128)(2,1)S(1)}, bf16[1,128,1024]{2,1,0:T(8,128)(2,1)S(1)}, u32[]{:S(2)}, u32[]{:S(2)}) %collective-permute-start.15) | collective-permute-done | bytes 262176 | tf_op jit(solution)/shard_map/ppermute | solution.py:685
  73.8 0.7 collective-permute-start.16
  74.6 1.3 %collective-permute-start.14 = (bf16[1,128,1024]{2,1,0:T(8,128)(2,1)S(1)}, bf16[1,128,1024]{2,1,0:T(8,128)(2,1)S(1)}, u32[]{:S(2)}, u32[]{:S(2)}) collective-permute-start(bf16[1,128,1024]{2,1,0:T(8,128)(2,1)S(1)} %shard_map.112), channel_id=1, source_target_pairs={{4,0},{8,12},{5,1},{9,13},{6,2},{10,14},{7,3},{11,15},{20,16},{24,... | collective-permute-start | bytes 786440 | tf_op jit(solution)/shard_map/ppermute | solution.py:685
  76.0 1.3 %collective-permute-start.19 = (bf16[1,128,1024]{2,1,0:T(8,128)(2,1)S(1)}, bf16[1,128,1024]{2,1,0:T(8,128)(2,1)S(1)}, u32[]{:S(2)}, u32[]{:S(2)}) collective-permute-start(bf16[1,128,1024]{2,1,0:T(8,128)(2,1)S(1)} %shard_map.118), channel_id=1, source_target_pairs={{4,0},{8,12},{5,1},{9,13},{6,2},{10,14},{7,3},{11,15},{20,16},{24,... | collective-permute-start | bytes 786440 | tf_op jit(solution)/shard_map/ppermute | solution.py:685
  77.3 12.1 %collective-permute-done.14.refs_1_ = bf16[1,128,1024]{2,1,0:T(8,128)(2,1)S(1)} collective-permute-done((bf16[1,128,1024]{2,1,0:T(8,128)(2,1)S(1)}, bf16[1,128,1024]{2,1,0:T(8,128)(2,1)S(1)}, u32[]{:S(2)}, u32[]{:S(2)}) %collective-permute-start.14) | collective-permute-done | bytes 262176 | tf_op jit(solution)/shard_map/ppermute | solution.py:685
  89.4 0.6 shard_map.113.refs_4_
  90.0 1.2 %collective-permute-start.24 = (bf16[256,256]{1,0:T(8,128)(2,1)S(1)}, bf16[256,256]{1,0:T(8,128)(2,1)S(1)}, u32[]{:S(2)}, u32[]{:S(2)}) collective-permute-start(bf16[256,256]{1,0:T(8,128)(2,1)S(1)} %shard_map.113.refs_4_), channel_id=1, source_target_pairs={{0,8},{4,12},{8,0},{12,4},{1,9},{5,13},{9,1},{13,5},{2,10},{6,14},... | collective-permute-start | bytes 393224 | tf_op jit(solution)/shard_map/ppermute | solution.py:702
  91.2 1.2 %collective-permute-start.23 = (bf16[256,256]{1,0:T(8,128)(2,1)S(1)}, bf16[256,256]{1,0:T(8,128)(2,1)S(1)}, u32[]{:S(2)}, u32[]{:S(2)}) collective-permute-start(bf16[256,256]{1,0:T(8,128)(2,1)S(1)} %shard_map.113.refs_4_), channel_id=1, source_target_pairs={{0,12},{4,0},{8,4},{12,8},{1,13},{5,1},{9,5},{13,9},{2,14},{6,2},{... | collective-permute-start | bytes 393224 | tf_op jit(solution)/shard_map/ppermute | solution.py:702
  92.4 2.9 %shard_map.114.refs_2_ = bf16[256,2048]{1,0:T(8,128)(2,1)} custom-call(f32[32]{0:T(128)S(1)} %copy-done.6, bf16[256,2048]{1,0:T(8,128)(2,1)S(1)} %copy-done.2, f32[2,256,16]{2,1,0:T(8,128)S(1)} %get-tuple-element.74.cum_ref, f32[2,16,256]{2,1,0:T(8,128)S(1)} %get-tuple-element.65.cumt_ref, bf16[256,256]{1,0:T(8,128)(2,1)S(1)} %get-tuple-element.57.proj_ref, ...), custom_call_target="tpu_custom_call" | custom-call | flops 2097152000 | bytes 2621440 | tf_op jit(solution)/shard_map/pallas_call | solution.py:464
  95.3 0.8 collective-permute-start.25
  96.1 6.6 %collective-permute-done.19.refs_1_ = bf16[1,128,1024]{2,1,0:T(8,128)(2,1)S(1)} collective-permute-done((bf16[1,128,1024]{2,1,0:T(8,128)(2,1)S(1)}, bf16[1,128,1024]{2,1,0:T(8,128)(2,1)S(1)}, u32[]{:S(2)}, u32[]{:S(2)}) %collective-permute-start.19) | collective-permute-done | bytes 262176 | tf_op jit(solution)/shard_map/ppermute | solution.py:685
  102.7 0.6 shard_map.119.refs_4_
  103.4 1.8 %collective-permute-start.21 = (bf16[256,256]{1,0:T(8,128)(2,1)S(1)}, bf16[256,256]{1,0:T(8,128)(2,1)S(1)}, u32[]{:S(2)}, u32[]{:S(2)}) collective-permute-start(bf16[256,256]{1,0:T(8,128)(2,1)S(1)} %shard_map.119.refs_4_), channel_id=1, source_target_pairs={{0,8},{4,12},{8,0},{12,4},{1,9},{5,13},{9,1},{13,5},{2,10},{6,14},... | collective-permute-start | bytes 393224 | tf_op jit(solution)/shard_map/ppermute | solution.py:702
  105.2 2.0 %collective-permute-start.20 = (bf16[256,256]{1,0:T(8,128)(2,1)S(1)}, bf16[256,256]{1,0:T(8,128)(2,1)S(1)}, u32[]{:S(2)}, u32[]{:S(2)}) collective-permute-start(bf16[256,256]{1,0:T(8,128)(2,1)S(1)} %shard_map.119.refs_4_), channel_id=1, source_target_pairs={{0,12},{4,0},{8,4},{12,8},{1,13},{5,1},{9,5},{13,9},{2,14},{6,2},{... | collective-permute-start | bytes 393224 | tf_op jit(solution)/shard_map/ppermute | solution.py:702
  107.2 3.0 %shard_map.120 = bf16[256,2048]{1,0:T(8,128)(2,1)} custom-call(f32[32]{0:T(128)S(1)} %copy-done.6, bf16[256,2048]{1,0:T(8,128)(2,1)S(1)} %copy-done.2, f32[2,256,16]{2,1,0:T(8,128)S(1)} %get-tuple-element.74.cum_ref, f32[2,16,256]{2,1,0:T(8,128)S(1)} %get-tuple-element.65.cumt_ref, ...), custom_call_target="tpu_custom_call", output_to_operand_aliasing={{}: (8, {})} | custom-call | flops 2097152000 | bytes 2621440 | tf_op jit(solution)/shard_map/pallas_call | solution.py:464
  110.2 1.8 %shard_map.121 = (f32[1024,512]{1,0:T(8,128)}, bf16[1024,512]{1,0:T(8,128)(2,1)}) custom-call(bf16[1024,256]{1,0:T(8,128)(2,1)S(1)} %shard_map.116.refs_0_, bf16[1024,256]{1,0:T(8,128)(2,1)S(1)} %collective-permute-done.17.refs_1_, bf16[1024,256]{1,0:T(8,128)(2,1)S(1)} %shard_map.117.refs_2_, bf16[1024,256]{1,0:T(8,128)(2,1)S(1)} %collective-permute-done.18.refs_3_, ...), custom_call_target="tpu_custom_call" | custom-call | flops 536870912 | bytes 5767168 | tf_op jit(solution)/shard_map/pallas_call | solution.py:535
  112.0 0.5 collective-permute-done.21.refs_6_
  112.5 1.8 %shard_map.122 = (f32[1024,512]{1,0:T(8,128)}, bf16[1024,512]{1,0:T(8,128)(2,1)}) custom-call(bf16[1024,256]{1,0:T(8,128)(2,1)S(1)} %shard_map.116.refs_0_, bf16[1024,256]{1,0:T(8,128)(2,1)S(1)} %collective-permute-done.17.refs_1_, bf16[1024,256]{1,0:T(8,128)(2,1)S(1)} %shard_map.117.refs_2_, ...), custom_call_target="tpu_custom_call", output_to_operand_aliasing={{0}: (10, {}), {1}: (11, {})} | custom-call | flops 536870912 | bytes 5767168 | tf_op jit(solution)/shard_map/pallas_call | solution.py:535
  (39 shorter events, 0.9 us)
Async XLA Ops:
  0.6 20.5 %collective-permute-start.1 = (f32[1024,512]{1,0:T(8,128)}, f32[1024,512]{1,0:T(8,128)S(1)}, u32[]{:S(2)}, u32[]{:S(2)}) collective-permute-start(f32[1024,512]{1,0:T(8,128)} %master_ref.1), channel_id=1, source_target_pairs={{0,1},{1,0},{2,3},{3,2},{4,5},{5,4},{6,7},{7,6},{8,9},{9,8},{10,11... | collective-permute-start | bytes 6291464 | tf_op jit(solution)/shard_map/ppermute | solution.py:642
  1.1 20.0 %collective-permute-start.2 = (s32[256,512]{1,0:T(8,128)}, s32[256,512]{1,0:T(8,128)S(1)}, u32[]{:S(2)}, u32[]{:S(2)}) collective-permute-start(s32[256,512]{1,0:T(8,128)} %now_ref.1), channel_id=1, source_target_pairs={{0,1},{1,0},{2,3},{3,2},{4,5},{5,4},{6,7},{7,6},{8,9},{9,8},{10,11... | collective-permute-start | bytes 1572872 | tf_op jit(solution)/shard_map/ppermute | solution.py:642
  2.3 8.5 %collective-permute-start.5 = (bf16[128,1024]{1,0:T(8,128)(2,1)S(1)}, bf16[128,1024]{1,0:T(8,128)(2,1)S(1)}, u32[]{:S(2)}, u32[]{:S(2)}) collective-permute-start(bf16[128,1024]{1,0:T(8,128)(2,1)S(1)} %get-tuple-element.83), channel_id=1, source_target_pairs={{1,3},{2,0},{4,6},{7,5},{9,11},{10,8},{12,14},{15,13},{17,19},{18,... | collective-permute-start | bytes 786440 | tf_op jit(solution)/shard_map/ppermute | solution.py:637
  3.6 18.8 %collective-permute-start.4 = (bf16[128,1024]{1,0:T(8,128)(2,1)S(1)}, bf16[128,1024]{1,0:T(8,128)(2,1)S(1)}, u32[]{:S(2)}, u32[]{:S(2)}) collective-permute-start(bf16[128,1024]{1,0:T(8,128)(2,1)S(1)} %get-tuple-element.83), channel_id=1, source_target_pairs={{0,0},{3,14},{5,4},{6,11},{8,1},{11,15},{13,5},{14,10},{16,16},{19... | collective-permute-start | bytes 786440 | tf_op jit(solution)/shard_map/ppermute | solution.py:639
  4.3 18.0 %collective-permute-start = (bf16[128,1024]{1,0:T(8,128)(2,1)S(1)}, bf16[128,1024]{1,0:T(8,128)(2,1)S(1)}, u32[]{:S(2)}, u32[]{:S(2)}) collective-permute-start(bf16[128,1024]{1,0:T(8,128)(2,1)S(1)} %get-tuple-element.84), channel_id=1, source_target_pairs={{0,0},{3,14},{5,4},{6,11},{8,1},{11,15},{13,5},{14,10},{1,7},{2,9}... | collective-permute-start | bytes 786440 | tf_op jit(solution)/shard_map/ppermute | solution.py:638
  10.8 11.6 %collective-permute-start.6 = (bf16[128,1024]{1,0:T(8,128)(2,1)S(1)}, bf16[128,1024]{1,0:T(8,128)(2,1)S(1)}, u32[]{:S(2)}, u32[]{:S(2)}) collective-permute-start(bf16[128,1024]{1,0:T(8,128)(2,1)S(1)} %collective-permute-done.5), channel_id=1, source_target_pairs={{3,7},{0,9},{6,2},{5,13},{11,6},{8,8},{14,3},{13,12},{19,23},{16,2... | collective-permute-start | bytes 786440 | tf_op jit(solution)/shard_map/ppermute | solution.py:639
  15.7 1.6 %copy-start = (f32[1024,512]{1,0:T(8,128)S(1)}, f32[1024,512]{1,0:T(8,128)}, u32[]{:S(2)}) copy-start(f32[1024,512]{1,0:T(8,128)} %master_ref.1) | copy-start | bytes 6291460
  17.3 1.0 copy-start.3
  18.4 1.0 copy-start.4
  22.3 10.9 %collective-permute-start.3 = (bf16[128,1024]{1,0:T(8,128)(2,1)S(1)}, bf16[128,1024]{1,0:T(8,128)(2,1)S(1)}, u32[]{:S(2)}, u32[]{:S(2)}) collective-permute-start(bf16[128,1024]{1,0:T(8,128)(2,1)S(1)} %collective-permute-done.refs_0_), channel_id=1, source_target_pairs={{0,2},{2,0},{1,3},{3,1},{4,6},{6,4},{5,7},{7,5},{8,10},{10,8},{9,1... | collective-permute-start | bytes 786440 | tf_op jit(solution)/shard_map/ppermute | solution.py:646
  23.1 10.5 %collective-permute-start.7 = (bf16[128,1024]{1,0:T(8,128)(2,1)S(1)}, bf16[128,1024]{1,0:T(8,128)(2,1)S(1)}, u32[]{:S(2)}, u32[]{:S(2)}) collective-permute-start(bf16[128,1024]{1,0:T(8,128)(2,1)S(1)} %get-tuple-element.47.refs_1_), channel_id=1, source_target_pairs={{0,2},{2,0},{1,3},{3,1},{4,6},{6,4},{5,7},{7,5},{8,10},{10,8},{9,1... | collective-permute-start | bytes 786440 | tf_op jit(solution)/shard_map/ppermute | solution.py:648
  25.2 22.8 %collective-permute-start.8 = (bf16[256,512]{1,0:T(8,128)(2,1)S(1)}, bf16[256,512]{1,0:T(8,128)(2,1)S(1)}, u32[]{:S(2)}, u32[]{:S(2)}) collective-permute-start(bf16[256,512]{1,0:T(8,128)(2,1)S(1)} %get-tuple-element.51), channel_id=1, source_target_pairs={{0,0},{1,9},{2,6},{3,15},{4,4},{5,13},{6,10},{7,3},{8,8},{9,1},{10... | collective-permute-start | bytes 786440 | tf_op jit(solution)/shard_map/ppermute | solution.py:650
  25.9 16.9 %copy-start.1 = (bf16[256,2048]{1,0:T(8,128)(2,1)S(1)}, bf16[256,2048]{1,0:T(8,128)(2,1)}, u32[]{:S(2)}) copy-start(bf16[256,2048]{1,0:T(8,128)(2,1)} %dy_ref.1) | copy-start | bytes 3145732
  25.9 16.9 %copy-start.2 = (bf16[256,2048]{1,0:T(8,128)(2,1)S(1)}, bf16[256,2048]{1,0:T(8,128)(2,1)}, u32[]{:S(2)}) copy-start(bf16[256,2048]{1,0:T(8,128)(2,1)} %x_ref.4) | copy-start | bytes 3145732
  25.9 16.9 %copy-start.5 = (f32[256,32]{0,1:T(8,128)S(1)}, f32[256,32]{0,1:T(8,128)}, u32[]{:S(2)}) copy-start(f32[256,32]{0,1:T(8,128)} %param.10) | copy-start | bytes 98308
  25.9 24.8 %collective-permute-start.9 = (bf16[256,512]{1,0:T(8,128)(2,1)S(1)}, bf16[256,512]{1,0:T(8,128)(2,1)S(1)}, u32[]{:S(2)}, u32[]{:S(2)}) collective-permute-start(bf16[256,512]{1,0:T(8,128)(2,1)S(1)} %get-tuple-element.52), channel_id=1, source_target_pairs={{0,1},{1,8},{2,7},{3,14},{4,5},{5,12},{6,11},{7,2},{8,9},{9,0},{10... | collective-permute-start | bytes 786440 | tf_op jit(solution)/shard_map/ppermute | solution.py:651
  34.1 23.6 %collective-permute-start.10 = (bf16[256,512]{1,0:T(8,128)(2,1)S(1)}, bf16[256,512]{1,0:T(8,128)(2,1)S(1)}, u32[]{:S(2)}, u32[]{:S(2)}) collective-permute-start(bf16[256,512]{1,0:T(8,128)(2,1)S(1)} %get-tuple-element.48), channel_id=1, source_target_pairs={{0,4},{1,13},{2,2},{3,11},{4,8},{5,1},{6,6},{7,15},{8,12},{9,5},{1... | collective-permute-start | bytes 786440 | tf_op jit(solution)/shard_map/ppermute | solution.py:656
  42.8 15.0 %collective-permute-start.11 = (bf16[256,512]{1,0:T(8,128)(2,1)S(1)}, bf16[256,512]{1,0:T(8,128)(2,1)S(1)}, u32[]{:S(2)}, u32[]{:S(2)}) collective-permute-start(bf16[256,512]{1,0:T(8,128)(2,1)S(1)} %get-tuple-element.53), channel_id=1, source_target_pairs={{0,5},{1,12},{2,3},{3,10},{4,9},{5,0},{6,7},{7,14},{8,13},{9,4},{1... | collective-permute-start | bytes 786440 | tf_op jit(solution)/shard_map/ppermute | solution.py:657
  58.2 7.3 %collective-permute-start.12 = (bf16[1,128,1024]{2,1,0:T(8,128)(2,1)S(1)}, bf16[1,128,1024]{2,1,0:T(8,128)(2,1)S(1)}, u32[]{:S(2)}, u32[]{:S(2)}) collective-permute-start(bf16[1,128,1024]{2,1,0:T(8,128)(2,1)S(1)} %get-tuple-element.60), channel_id=1, source_target_pairs={{0,4},{12,8},{1,5},{13,9},{2,6},{14,10},{3,7},{15,11},{16,20},{28,... | collective-permute-start | bytes 786440 | tf_op jit(solution)/shard_map/ppermute | solution.py:685
  60.9 14.9 %collective-permute-start.17 = (bf16[1024,256]{1,0:T(8,128)(2,1)S(1)}, bf16[1024,256]{1,0:T(8,128)(2,1)S(1)}, u32[]{:S(2)}, u32[]{:S(2)}) collective-permute-start(bf16[1024,256]{1,0:T(8,128)(2,1)S(1)} %shard_map.116.refs_0_), channel_id=1, source_target_pairs={{0,1},{1,0},{2,3},{3,2},{4,5},{5,4},{6,7},{7,6},{8,9},{9,8},{10,11... | collective-permute-start | bytes 1572872 | tf_op jit(solution)/shard_map/ppermute | solution.py:675
  61.2 14.7 %collective-permute-start.18 = (bf16[1024,256]{1,0:T(8,128)(2,1)S(1)}, bf16[1024,256]{1,0:T(8,128)(2,1)S(1)}, u32[]{:S(2)}, u32[]{:S(2)}) collective-permute-start(bf16[1024,256]{1,0:T(8,128)(2,1)S(1)} %shard_map.117.refs_2_), channel_id=1, source_target_pairs={{0,1},{1,0},{2,3},{3,2},{4,5},{5,4},{6,7},{7,6},{8,9},{9,8},{10,11... | collective-permute-start | bytes 1572872 | tf_op jit(solution)/shard_map/ppermute | solution.py:675
  65.5 8.3 %collective-permute-start.15 = (bf16[1,128,1024]{2,1,0:T(8,128)(2,1)S(1)}, bf16[1,128,1024]{2,1,0:T(8,128)(2,1)S(1)}, u32[]{:S(2)}, u32[]{:S(2)}) collective-permute-start(bf16[1,128,1024]{2,1,0:T(8,128)(2,1)S(1)} %get-tuple-element.68), channel_id=1, source_target_pairs={{0,4},{12,8},{1,5},{13,9},{2,6},{14,10},{3,7},{15,11},{16,20},{28,... | collective-permute-start | bytes 786440 | tf_op jit(solution)/shard_map/ppermute | solution.py:685
  70.0 4.5 %collective-permute-start.13 = (bf16[1,128,1024]{2,1,0:T(8,128)(2,1)S(1)}, bf16[1,128,1024]{2,1,0:T(8,128)(2,1)S(1)}, u32[]{:S(2)}, u32[]{:S(2)}) collective-permute-start(bf16[1,128,1024]{2,1,0:T(8,128)(2,1)S(1)} %shard_map.111), channel_id=1, source_target_pairs={{4,8},{8,4},{5,9},{9,5},{6,10},{10,6},{7,11},{11,7},{20,24},{24,20... | collective-permute-start | bytes 786440 | tf_op jit(solution)/shard_map/ppermute | solution.py:685
  73.8 2.1 %collective-permute-start.16 = (bf16[1,128,1024]{2,1,0:T(8,128)(2,1)S(1)}, bf16[1,128,1024]{2,1,0:T(8,128)(2,1)S(1)}, u32[]{:S(2)}, u32[]{:S(2)}) collective-permute-start(bf16[1,128,1024]{2,1,0:T(8,128)(2,1)S(1)} %shard_map.115), channel_id=1, source_target_pairs={{4,8},{8,4},{5,9},{9,5},{6,10},{10,6},{7,11},{11,7},{20,24},{24,20... | collective-permute-start | bytes 786440 | tf_op jit(solution)/shard_map/ppermute | solution.py:685
  74.6 14.8 %collective-permute-start.14 = (bf16[1,128,1024]{2,1,0:T(8,128)(2,1)S(1)}, bf16[1,128,1024]{2,1,0:T(8,128)(2,1)S(1)}, u32[]{:S(2)}, u32[]{:S(2)}) collective-permute-start(bf16[1,128,1024]{2,1,0:T(8,128)(2,1)S(1)} %shard_map.112), channel_id=1, source_target_pairs={{4,0},{8,12},{5,1},{9,13},{6,2},{10,14},{7,3},{11,15},{20,16},{24,... | collective-permute-start | bytes 786440 | tf_op jit(solution)/shard_map/ppermute | solution.py:685
  76.0 16.4 %copy-start.6 = (f32[32]{0:T(128)S(1)}, f32[32]{0:T(128)}, u32[]{:S(2)}) copy-start(f32[32]{0:T(128)} %skip_ref.3) | copy-start | bytes 388
  76.0 26.7 %collective-permute-start.19 = (bf16[1,128,1024]{2,1,0:T(8,128)(2,1)S(1)}, bf16[1,128,1024]{2,1,0:T(8,128)(2,1)S(1)}, u32[]{:S(2)}, u32[]{:S(2)}) collective-permute-start(bf16[1,128,1024]{2,1,0:T(8,128)(2,1)S(1)} %shard_map.118), channel_id=1, source_target_pairs={{4,0},{8,12},{5,1},{9,13},{6,2},{10,14},{7,3},{11,15},{20,16},{24,... | collective-permute-start | bytes 786440 | tf_op jit(solution)/shard_map/ppermute | solution.py:685
  90.0 15.2 %collective-permute-start.24 = (bf16[256,256]{1,0:T(8,128)(2,1)S(1)}, bf16[256,256]{1,0:T(8,128)(2,1)S(1)}, u32[]{:S(2)}, u32[]{:S(2)}) collective-permute-start(bf16[256,256]{1,0:T(8,128)(2,1)S(1)} %shard_map.113.refs_4_), channel_id=1, source_target_pairs={{0,8},{4,12},{8,0},{12,4},{1,9},{5,13},{9,1},{13,5},{2,10},{6,14},... | collective-permute-start | bytes 393224 | tf_op jit(solution)/shard_map/ppermute | solution.py:702
  91.2 19.1 %collective-permute-start.23 = (bf16[256,256]{1,0:T(8,128)(2,1)S(1)}, bf16[256,256]{1,0:T(8,128)(2,1)S(1)}, u32[]{:S(2)}, u32[]{:S(2)}) collective-permute-start(bf16[256,256]{1,0:T(8,128)(2,1)S(1)} %shard_map.113.refs_4_), channel_id=1, source_target_pairs={{0,12},{4,0},{8,4},{12,8},{1,13},{5,1},{9,5},{13,9},{2,14},{6,2},{... | collective-permute-start | bytes 393224 | tf_op jit(solution)/shard_map/ppermute | solution.py:702
  95.3 15.0 %collective-permute-start.25 = (bf16[256,256]{1,0:T(8,128)(2,1)S(1)}, bf16[256,256]{1,0:T(8,128)(2,1)S(1)}, u32[]{:S(2)}, u32[]{:S(2)}) collective-permute-start(bf16[256,256]{1,0:T(8,128)(2,1)S(1)} %shard_map.113.refs_4_), channel_id=1, source_target_pairs={{0,4},{4,8},{8,12},{12,0},{1,5},{5,9},{9,13},{13,1},{2,6},{6,10},{... | collective-permute-start | bytes 393224 | tf_op jit(solution)/shard_map/ppermute | solution.py:702
  103.3 8.7 %collective-permute-start.22 = (bf16[256,256]{1,0:T(8,128)(2,1)S(1)}, bf16[256,256]{1,0:T(8,128)(2,1)S(1)}, u32[]{:S(2)}, u32[]{:S(2)}) collective-permute-start(bf16[256,256]{1,0:T(8,128)(2,1)S(1)} %shard_map.119.refs_4_), channel_id=1, source_target_pairs={{0,4},{4,8},{8,12},{12,0},{1,5},{5,9},{9,13},{13,1},{2,6},{6,10},{... | collective-permute-start | bytes 393224 | tf_op jit(solution)/shard_map/ppermute | solution.py:702
  103.4 9.1 %collective-permute-start.21 = (bf16[256,256]{1,0:T(8,128)(2,1)S(1)}, bf16[256,256]{1,0:T(8,128)(2,1)S(1)}, u32[]{:S(2)}, u32[]{:S(2)}) collective-permute-start(bf16[256,256]{1,0:T(8,128)(2,1)S(1)} %shard_map.119.refs_4_), channel_id=1, source_target_pairs={{0,8},{4,12},{8,0},{12,4},{1,9},{5,13},{9,1},{13,5},{2,10},{6,14},... | collective-permute-start | bytes 393224 | tf_op jit(solution)/shard_map/ppermute | solution.py:702
  105.2 7.3 %collective-permute-start.20 = (bf16[256,256]{1,0:T(8,128)(2,1)S(1)}, bf16[256,256]{1,0:T(8,128)(2,1)S(1)}, u32[]{:S(2)}, u32[]{:S(2)}) collective-permute-start(bf16[256,256]{1,0:T(8,128)(2,1)S(1)} %shard_map.119.refs_4_), channel_id=1, source_target_pairs={{0,12},{4,0},{8,4},{12,8},{1,13},{5,1},{9,5},{13,9},{2,14},{6,2},{... | collective-permute-start | bytes 393224 | tf_op jit(solution)/shard_map/ppermute | solution.py:702

commit v5 on v4

--- a/solution.py
+++ b/solution.py
@@ -697,9 +697,10 @@
         )
         blocks = [grad]
         for distance in range(1, seq):
-            if not p and distance == seq - 1:
-                grad = held(grad, ssd_output)
-            blocks.append(lax.ppermute(grad, "seq", to_all(seq, seq - distance)))
+            payload = grad
+            if not p and distance != seq // 2:
+                payload = held(grad, ssd_output)
+            blocks.append(lax.ppermute(payload, "seq", to_all(seq, seq - distance)))
         moved.append(blocks)
     decayed = held(decayed, ssd_output)
     updated = None

time: 115 us -> 115 us (level)
  waiting for transfers between devices: 41.1 us -> 39.2 us
  starting transfers between devices: 45.5 us -> 47.3 us
    ppermute x6, waiting for transfers between devices: 25 us -> 22.6 us  [on_device(): arrived[p].append(lax.ppermute(message, 'seq', pairs))]
    ppermute x6, starting transfers between devices: 7.13 us -> 8.93 us  [on_device(): blocks.append(lax.ppermute(payload, 'seq', to_all(seq, seq - distance)))]
where the time goes in v5:
time: 115 us; the launch traced here: 114 us
  starting transfers between devices  47.3 us (41%)
  waiting for transfers between devices  39.2 us (34%)
  Pallas kernels  21.9 us (19%)
  local copies, waits for them, and re-layouts  4.76 us (4%)
  between operations  1.21 us (1%)
    ppermute x6, waiting for transfers between devices, on_device(): arrived[p].append(lax.ppermute(message, 'seq', pairs))  22.6 us
    ppermute x6, starting transfers between devices, on_device(): arrived[p].append(lax.ppermute(message, 'seq', pairs))  10.9 us
    ppermute x6, starting transfers between devices, on_device(): blocks.append(lax.ppermute(payload, 'seq', to_all(seq, seq - distance)))  8.93 us
    ppermute x1, starting transfers between devices, on_device(): lax.ppermute(same, axes, block_pairs(seq, False, True))  8.66 us
    ppermute x1, starting transfers between devices, on_device(): lax.ppermute(cross, axes, block_pairs(seq, True, False))  7.26 us
    ppermute x1, waiting for transfers between devices, on_device(): lax.ppermute(cross, axes, block_pairs(seq, False, False))  6.97 us
    pallas_call x2, Pallas kernels, output(): call(functools.partial(output_kernel, ahead, first), jax.ShapeDtypeStruct...  5.93 us
    ppermute x1, waiting for transfers between devices, on_device(): relayed = lax.ppermute(hidden[rows:], axes, beside)  5.87 us
  transfers between devices with their start and end apart: 26, of which 8 were waited for; matrix products, arithmetic and copies ran while one was open for 1% of the time, Pallas kernels for 17%

profile of v5, /device:TPU:0, one launch (start us, length us, event | category | flops | bytes accessed | tf_op | source)
XLA Modules:
  0.0 114.4 jit_solution(12349740903439387416)
XLA Ops:
  0.6 0.5 collective-permute-start.1
  1.2 1.1 fusion
  2.3 1.3 %collective-permute-start.5 = (bf16[128,1024]{1,0:T(8,128)(2,1)S(1)}, bf16[128,1024]{1,0:T(8,128)(2,1)S(1)}, u32[]{:S(2)}, u32[]{:S(2)}) collective-permute-start(bf16[128,1024]{1,0:T(8,128)(2,1)S(1)} %get-tuple-element.83), channel_id=1, source_target_pairs={{1,3},{2,0},{4,6},{7,5},{9,11},{10,8},{12,14},{15,13},{17,19},{18,... | collective-permute-start | bytes 786440 | tf_op jit(solution)/shard_map/ppermute | solution.py:637
  3.6 0.7 collective-permute-start.4
  4.3 0.7 collective-permute-start
  5.0 5.9 %collective-permute-done.5 = bf16[128,1024]{1,0:T(8,128)(2,1)S(1)} collective-permute-done((bf16[128,1024]{1,0:T(8,128)(2,1)S(1)}, bf16[128,1024]{1,0:T(8,128)(2,1)S(1)}, u32[]{:S(2)}, u32[]{:S(2)}) %collective-permute-start.5) | collective-permute-done | bytes 262176 | tf_op jit(solution)/shard_map/ppermute | solution.py:637
  10.8 4.9 %collective-permute-start.6 = (bf16[128,1024]{1,0:T(8,128)(2,1)S(1)}, bf16[128,1024]{1,0:T(8,128)(2,1)S(1)}, u32[]{:S(2)}, u32[]{:S(2)}) collective-permute-start(bf16[128,1024]{1,0:T(8,128)(2,1)S(1)} %collective-permute-done.5), channel_id=1, source_target_pairs={{3,7},{0,9},{6,2},{5,13},{11,6},{8,8},{14,3},{13,12},{19,23},{16,2... | collective-permute-start | bytes 786440 | tf_op jit(solution)/shard_map/ppermute | solution.py:639
  15.8 1.6 %copy-done = f32[1024,512]{1,0:T(8,128)S(1)} copy-done((f32[1024,512]{1,0:T(8,128)S(1)}, f32[1024,512]{1,0:T(8,128)}, u32[]{:S(2)}) %copy-start) | copy-done | bytes 2097176
  17.3 1.0 copy-done.3
  18.4 1.0 copy-done.4
  19.4 1.7 %shard_map.103 = (bf16[1024,512]{1,0:T(8,128)(2,1)S(1)}, f32[1024,512]{1,0:T(8,128)S(1)}, bf16[1024,512]{1,0:T(8,128)(2,1)S(1)}) custom-call(f32[1024,512]{1,0:T(8,128)S(1)} %copy-done, s32[256,512]{1,0:T(8,128)S(1)} %copy-done.4, s32[256,512]{1,0:T(8,128)S(1)} %copy-done.3), custom_call_target="tpu_custom_call" | custom-call | flops 1572864000 | bytes 7340032 | tf_op jit(solution)/shard_map/pallas_call | solution.py:77
  21.1 1.2 %shard_map.104.refs_2_.refs_4_.sibling_weight_ref = bf16[1024,512]{1,0:T(8,128)(2,1)S(1)} custom-call(f32[1024,512]{1,0:T(8,128)S(1)} %collective-permute-done.1.master_ref, s32[256,512]{1,0:T(8,128)S(1)} %collective-permute-done.2.now_ref), custom_call_target="tpu_custom_call" | custom-call | flops 1572864000 | bytes 3670016 | tf_op jit(solution)/shard_map/pallas_call | solution.py:101
  22.4 0.7 shard_map.106
  23.1 2.1 %collective-permute-start.7 = (bf16[128,1024]{1,0:T(8,128)(2,1)S(1)}, bf16[128,1024]{1,0:T(8,128)(2,1)S(1)}, u32[]{:S(2)}, u32[]{:S(2)}) collective-permute-start(bf16[128,1024]{1,0:T(8,128)(2,1)S(1)} %get-tuple-element.47.refs_1_), channel_id=1, source_target_pairs={{0,2},{2,0},{1,3},{3,1},{4,6},{6,4},{5,7},{7,5},{8,10},{10,8},{9,1... | collective-permute-start | bytes 786440 | tf_op jit(solution)/shard_map/ppermute | solution.py:648
  25.2 0.7 collective-permute-start.8
  25.9 7.3 %collective-permute-start.9 = (bf16[256,512]{1,0:T(8,128)(2,1)S(1)}, bf16[256,512]{1,0:T(8,128)(2,1)S(1)}, u32[]{:S(2)}, u32[]{:S(2)}) collective-permute-start(bf16[256,512]{1,0:T(8,128)(2,1)S(1)} %get-tuple-element.52), channel_id=1, source_target_pairs={{0,1},{1,8},{2,7},{3,14},{4,5},{5,12},{6,11},{7,2},{8,9},{9,0},{10... | collective-permute-start | bytes 786440 | tf_op jit(solution)/shard_map/ppermute | solution.py:651
  33.2 0.4 shard_map.105
  33.6 0.4 shard_map.107
  34.1 8.7 %collective-permute-start.10 = (bf16[256,512]{1,0:T(8,128)(2,1)S(1)}, bf16[256,512]{1,0:T(8,128)(2,1)S(1)}, u32[]{:S(2)}, u32[]{:S(2)}) collective-permute-start(bf16[256,512]{1,0:T(8,128)(2,1)S(1)} %get-tuple-element.48), channel_id=1, source_target_pairs={{0,4},{1,13},{2,2},{3,11},{4,8},{5,1},{6,6},{7,15},{8,12},{9,5},{1... | collective-permute-start | bytes 786440 | tf_op jit(solution)/shard_map/ppermute | solution.py:656
  42.9 5.2 %shard_map.108 = (bf16[256,2048]{1,0:T(8,128)(2,1)S(1)}, bf16[256,2048]{1,0:T(8,128)(2,1)S(1)}, bf16[2,256,256]{2,1,0:T(8,128)(2,1)S(1)}, bf16[2,256,256]{2,1,0:...) custom-call(bf16[256,2048]{1,0:T(8,128)(2,1)S(1)} %copy-done.2, ...), custom_call_target="tpu_custom_call" | custom-call | flops 5242880000 | bytes 4194304 | tf_op jit(solution)/shard_map/pallas_call | solution.py:198
  48.0 2.7 %collective-permute-done.9.refs_1_ = bf16[256,512]{1,0:T(8,128)(2,1)S(1)} collective-permute-done((bf16[256,512]{1,0:T(8,128)(2,1)S(1)}, bf16[256,512]{1,0:T(8,128)(2,1)S(1)}, u32[]{:S(2)}, u32[]{:S(2)}) %collective-permute-start.9) | collective-permute-done | bytes 262176 | tf_op jit(solution)/shard_map/ppermute | solution.py:651
  50.8 7.0 %collective-permute-done.11.refs_3_ = bf16[256,512]{1,0:T(8,128)(2,1)S(1)} collective-permute-done((bf16[256,512]{1,0:T(8,128)(2,1)S(1)}, bf16[256,512]{1,0:T(8,128)(2,1)S(1)}, u32[]{:S(2)}, u32[]{:S(2)}) %collective-permute-start.11) | collective-permute-done | bytes 262176 | tf_op jit(solution)/shard_map/ppermute | solution.py:657
  57.7 0.5 shard_map.110
  58.2 2.5 %collective-permute-start.12 = (bf16[1,128,1024]{2,1,0:T(8,128)(2,1)S(1)}, bf16[1,128,1024]{2,1,0:T(8,128)(2,1)S(1)}, u32[]{:S(2)}, u32[]{:S(2)}) collective-permute-start(bf16[1,128,1024]{2,1,0:T(8,128)(2,1)S(1)} %get-tuple-element.60), channel_id=1, source_target_pairs={{0,4},{12,8},{1,5},{13,9},{2,6},{14,10},{3,7},{15,11},{16,20},{28,... | collective-permute-start | bytes 786440 | tf_op jit(solution)/shard_map/ppermute | solution.py:685
  60.7 0.2 shard_map.116.refs_0_
  61.2 0.6 collective-permute-start.18
  61.8 0.5 shard_map.109
  62.3 3.2 %collective-permute-done.12.arrived_ref.near_ref = bf16[1,128,1024]{2,1,0:T(8,128)(2,1)S(1)} collective-permute-done((bf16[1,128,1024]{2,1,0:T(8,128)(2,1)S(1)}, bf16[1,128,1024]{2,1,0:T(8,128)(2,1)S(1)}, u32[]{:S(2)}, u32[]{:S(2)}) %collective-permute-start.12) | collective-permute-done | bytes 262176 | tf_op jit(solution)/shard_map/ppermute | solution.py:685
  65.5 4.4 %collective-permute-start.15 = (bf16[1,128,1024]{2,1,0:T(8,128)(2,1)S(1)}, bf16[1,128,1024]{2,1,0:T(8,128)(2,1)S(1)}, u32[]{:S(2)}, u32[]{:S(2)}) collective-permute-start(bf16[1,128,1024]{2,1,0:T(8,128)(2,1)S(1)} %get-tuple-element.68), channel_id=1, source_target_pairs={{0,4},{12,8},{1,5},{13,9},{2,6},{14,10},{3,7},{15,11},{16,20},{28,... | collective-permute-start | bytes 786440 | tf_op jit(solution)/shard_map/ppermute | solution.py:685
  70.0 0.7 collective-permute-start.13
  70.6 3.1 %collective-permute-done.15.arrived_ref.near_ref = bf16[1,128,1024]{2,1,0:T(8,128)(2,1)S(1)} collective-permute-done((bf16[1,128,1024]{2,1,0:T(8,128)(2,1)S(1)}, bf16[1,128,1024]{2,1,0:T(8,128)(2,1)S(1)}, u32[]{:S(2)}, u32[]{:S(2)}) %collective-permute-start.15) | collective-permute-done | bytes 262176 | tf_op jit(solution)/shard_map/ppermute | solution.py:685
  73.8 0.7 collective-permute-start.16
  74.6 1.3 %collective-permute-start.14 = (bf16[1,128,1024]{2,1,0:T(8,128)(2,1)S(1)}, bf16[1,128,1024]{2,1,0:T(8,128)(2,1)S(1)}, u32[]{:S(2)}, u32[]{:S(2)}) collective-permute-start(bf16[1,128,1024]{2,1,0:T(8,128)(2,1)S(1)} %shard_map.112), channel_id=1, source_target_pairs={{4,0},{8,12},{5,1},{9,13},{6,2},{10,14},{7,3},{11,15},{20,16},{24,... | collective-permute-start | bytes 786440 | tf_op jit(solution)/shard_map/ppermute | solution.py:685
  76.0 1.3 %collective-permute-start.19 = (bf16[1,128,1024]{2,1,0:T(8,128)(2,1)S(1)}, bf16[1,128,1024]{2,1,0:T(8,128)(2,1)S(1)}, u32[]{:S(2)}, u32[]{:S(2)}) collective-permute-start(bf16[1,128,1024]{2,1,0:T(8,128)(2,1)S(1)} %shard_map.118), channel_id=1, source_target_pairs={{4,0},{8,12},{5,1},{9,13},{6,2},{10,14},{7,3},{11,15},{20,16},{24,... | collective-permute-start | bytes 786440 | tf_op jit(solution)/shard_map/ppermute | solution.py:685
  77.3 12.1 %collective-permute-done.14.refs_1_ = bf16[1,128,1024]{2,1,0:T(8,128)(2,1)S(1)} collective-permute-done((bf16[1,128,1024]{2,1,0:T(8,128)(2,1)S(1)}, bf16[1,128,1024]{2,1,0:T(8,128)(2,1)S(1)}, u32[]{:S(2)}, u32[]{:S(2)}) %collective-permute-start.14) | collective-permute-done | bytes 262176 | tf_op jit(solution)/shard_map/ppermute | solution.py:685
  89.4 0.6 shard_map.113.refs_4_
  90.0 1.2 %collective-permute-start.24 = (bf16[256,256]{1,0:T(8,128)(2,1)S(1)}, bf16[256,256]{1,0:T(8,128)(2,1)S(1)}, u32[]{:S(2)}, u32[]{:S(2)}) collective-permute-start(bf16[256,256]{1,0:T(8,128)(2,1)S(1)} %shard_map.113.refs_4_), channel_id=1, source_target_pairs={{0,8},{4,12},{8,0},{12,4},{1,9},{5,13},{9,1},{13,5},{2,10},{6,14},... | collective-permute-start | bytes 393224 | tf_op jit(solution)/shard_map/ppermute | solution.py:703
  91.2 2.9 %shard_map.114.refs_2_ = bf16[256,2048]{1,0:T(8,128)(2,1)} custom-call(f32[32]{0:T(128)S(1)} %copy-done.6, bf16[256,2048]{1,0:T(8,128)(2,1)S(1)} %copy-done.2, f32[2,256,16]{2,1,0:T(8,128)S(1)} %get-tuple-element.74.cum_ref, f32[2,16,256]{2,1,0:T(8,128)S(1)} %get-tuple-element.65.cumt_ref, bf16[256,256]{1,0:T(8,128)(2,1)S(1)} %get-tuple-element.57.proj_ref, ...), custom_call_target="tpu_custom_call" | custom-call | flops 2097152000 | bytes 2621440 | tf_op jit(solution)/shard_map/pallas_call | solution.py:464
  94.1 0.3 collective-permute-start.25
  94.3 3.6 %collective-permute-start.23 = (bf16[256,256]{1,0:T(8,128)(2,1)S(1)}, bf16[256,256]{1,0:T(8,128)(2,1)S(1)}, u32[]{:S(2)}, u32[]{:S(2)}) collective-permute-start(bf16[256,256]{1,0:T(8,128)(2,1)S(1)} %shard_map.113.refs_4_), channel_id=1, source_target_pairs={{0,12},{4,0},{8,4},{12,8},{1,13},{5,1},{9,5},{13,9},{2,14},{6,2},{... | collective-permute-start | bytes 393224 | tf_op jit(solution)/shard_map/ppermute | solution.py:703
  97.9 4.2 %collective-permute-done.19.refs_1_ = bf16[1,128,1024]{2,1,0:T(8,128)(2,1)S(1)} collective-permute-done((bf16[1,128,1024]{2,1,0:T(8,128)(2,1)S(1)}, bf16[1,128,1024]{2,1,0:T(8,128)(2,1)S(1)}, u32[]{:S(2)}, u32[]{:S(2)}) %collective-permute-start.19) | collective-permute-done | bytes 262176 | tf_op jit(solution)/shard_map/ppermute | solution.py:685
  102.1 0.6 shard_map.119.refs_4_
  102.7 1.3 %collective-permute-start.21 = (bf16[256,256]{1,0:T(8,128)(2,1)S(1)}, bf16[256,256]{1,0:T(8,128)(2,1)S(1)}, u32[]{:S(2)}, u32[]{:S(2)}) collective-permute-start(bf16[256,256]{1,0:T(8,128)(2,1)S(1)} %shard_map.119.refs_4_), channel_id=1, source_target_pairs={{0,8},{4,12},{8,0},{12,4},{1,9},{5,13},{9,1},{13,5},{2,10},{6,14},... | collective-permute-start | bytes 393224 | tf_op jit(solution)/shard_map/ppermute | solution.py:703
  104.1 2.5 %collective-permute-start.20 = (bf16[256,256]{1,0:T(8,128)(2,1)S(1)}, bf16[256,256]{1,0:T(8,128)(2,1)S(1)}, u32[]{:S(2)}, u32[]{:S(2)}) collective-permute-start(bf16[256,256]{1,0:T(8,128)(2,1)S(1)} %shard_map.119.refs_4_), channel_id=1, source_target_pairs={{0,12},{4,0},{8,4},{12,8},{1,13},{5,1},{9,5},{13,9},{2,14},{6,2},{... | collective-permute-start | bytes 393224 | tf_op jit(solution)/shard_map/ppermute | solution.py:703
  106.5 3.0 %shard_map.120 = bf16[256,2048]{1,0:T(8,128)(2,1)} custom-call(f32[32]{0:T(128)S(1)} %copy-done.6, bf16[256,2048]{1,0:T(8,128)(2,1)S(1)} %copy-done.2, f32[2,256,16]{2,1,0:T(8,128)S(1)} %get-tuple-element.74.cum_ref, f32[2,16,256]{2,1,0:T(8,128)S(1)} %get-tuple-element.65.cumt_ref, ...), custom_call_target="tpu_custom_call", output_to_operand_aliasing={{}: (8, {})} | custom-call | flops 2097152000 | bytes 2621440 | tf_op jit(solution)/shard_map/pallas_call | solution.py:464
  109.6 1.8 %shard_map.121 = (f32[1024,512]{1,0:T(8,128)}, bf16[1024,512]{1,0:T(8,128)(2,1)}) custom-call(bf16[1024,256]{1,0:T(8,128)(2,1)S(1)} %shard_map.116.refs_0_, bf16[1024,256]{1,0:T(8,128)(2,1)S(1)} %collective-permute-done.17.refs_1_, bf16[1024,256]{1,0:T(8,128)(2,1)S(1)} %shard_map.117.refs_2_, bf16[1024,256]{1,0:T(8,128)(2,1)S(1)} %collective-permute-done.18.refs_3_, ...), custom_call_target="tpu_custom_call" | custom-call | flops 536870912 | bytes 5767168 | tf_op jit(solution)/shard_map/pallas_call | solution.py:535
  111.4 1.1 collective-permute-done.21.refs_6_
  112.5 1.8 %shard_map.122 = (f32[1024,512]{1,0:T(8,128)}, bf16[1024,512]{1,0:T(8,128)(2,1)}) custom-call(bf16[1024,256]{1,0:T(8,128)(2,1)S(1)} %shard_map.116.refs_0_, bf16[1024,256]{1,0:T(8,128)(2,1)S(1)} %collective-permute-done.17.refs_1_, bf16[1024,256]{1,0:T(8,128)(2,1)S(1)} %shard_map.117.refs_2_, ...), custom_call_target="tpu_custom_call", output_to_operand_aliasing={{0}: (10, {}), {1}: (11, {})} | custom-call | flops 536870912 | bytes 5767168 | tf_op jit(solution)/shard_map/pallas_call | solution.py:535
  (39 shorter events, 0.9 us)
Async XLA Ops:
  0.6 20.5 %collective-permute-start.1 = (f32[1024,512]{1,0:T(8,128)}, f32[1024,512]{1,0:T(8,128)S(1)}, u32[]{:S(2)}, u32[]{:S(2)}) collective-permute-start(f32[1024,512]{1,0:T(8,128)} %master_ref.1), channel_id=1, source_target_pairs={{0,1},{1,0},{2,3},{3,2},{4,5},{5,4},{6,7},{7,6},{8,9},{9,8},{10,11... | collective-permute-start | bytes 6291464 | tf_op jit(solution)/shard_map/ppermute | solution.py:642
  1.1 20.0 %collective-permute-start.2 = (s32[256,512]{1,0:T(8,128)}, s32[256,512]{1,0:T(8,128)S(1)}, u32[]{:S(2)}, u32[]{:S(2)}) collective-permute-start(s32[256,512]{1,0:T(8,128)} %now_ref.1), channel_id=1, source_target_pairs={{0,1},{1,0},{2,3},{3,2},{4,5},{5,4},{6,7},{7,6},{8,9},{9,8},{10,11... | collective-permute-start | bytes 1572872 | tf_op jit(solution)/shard_map/ppermute | solution.py:642
  2.3 8.5 %collective-permute-start.5 = (bf16[128,1024]{1,0:T(8,128)(2,1)S(1)}, bf16[128,1024]{1,0:T(8,128)(2,1)S(1)}, u32[]{:S(2)}, u32[]{:S(2)}) collective-permute-start(bf16[128,1024]{1,0:T(8,128)(2,1)S(1)} %get-tuple-element.83), channel_id=1, source_target_pairs={{1,3},{2,0},{4,6},{7,5},{9,11},{10,8},{12,14},{15,13},{17,19},{18,... | collective-permute-start | bytes 786440 | tf_op jit(solution)/shard_map/ppermute | solution.py:637
  3.6 18.8 %collective-permute-start.4 = (bf16[128,1024]{1,0:T(8,128)(2,1)S(1)}, bf16[128,1024]{1,0:T(8,128)(2,1)S(1)}, u32[]{:S(2)}, u32[]{:S(2)}) collective-permute-start(bf16[128,1024]{1,0:T(8,128)(2,1)S(1)} %get-tuple-element.83), channel_id=1, source_target_pairs={{0,0},{3,14},{5,4},{6,11},{8,1},{11,15},{13,5},{14,10},{16,16},{19... | collective-permute-start | bytes 786440 | tf_op jit(solution)/shard_map/ppermute | solution.py:639
  4.3 18.0 %collective-permute-start = (bf16[128,1024]{1,0:T(8,128)(2,1)S(1)}, bf16[128,1024]{1,0:T(8,128)(2,1)S(1)}, u32[]{:S(2)}, u32[]{:S(2)}) collective-permute-start(bf16[128,1024]{1,0:T(8,128)(2,1)S(1)} %get-tuple-element.84), channel_id=1, source_target_pairs={{0,0},{3,14},{5,4},{6,11},{8,1},{11,15},{13,5},{14,10},{1,7},{2,9}... | collective-permute-start | bytes 786440 | tf_op jit(solution)/shard_map/ppermute | solution.py:638
  10.8 11.6 %collective-permute-start.6 = (bf16[128,1024]{1,0:T(8,128)(2,1)S(1)}, bf16[128,1024]{1,0:T(8,128)(2,1)S(1)}, u32[]{:S(2)}, u32[]{:S(2)}) collective-permute-start(bf16[128,1024]{1,0:T(8,128)(2,1)S(1)} %collective-permute-done.5), channel_id=1, source_target_pairs={{3,7},{0,9},{6,2},{5,13},{11,6},{8,8},{14,3},{13,12},{19,23},{16,2... | collective-permute-start | bytes 786440 | tf_op jit(solution)/shard_map/ppermute | solution.py:639
  15.7 1.6 %copy-start = (f32[1024,512]{1,0:T(8,128)S(1)}, f32[1024,512]{1,0:T(8,128)}, u32[]{:S(2)}) copy-start(f32[1024,512]{1,0:T(8,128)} %master_ref.1) | copy-start | bytes 6291460
  17.3 1.0 copy-start.3
  18.4 1.0 copy-start.4
  22.3 10.9 %collective-permute-start.3 = (bf16[128,1024]{1,0:T(8,128)(2,1)S(1)}, bf16[128,1024]{1,0:T(8,128)(2,1)S(1)}, u32[]{:S(2)}, u32[]{:S(2)}) collective-permute-start(bf16[128,1024]{1,0:T(8,128)(2,1)S(1)} %collective-permute-done.refs_0_), channel_id=1, source_target_pairs={{0,2},{2,0},{1,3},{3,1},{4,6},{6,4},{5,7},{7,5},{8,10},{10,8},{9,1... | collective-permute-start | bytes 786440 | tf_op jit(solution)/shard_map/ppermute | solution.py:646
  23.1 10.5 %collective-permute-start.7 = (bf16[128,1024]{1,0:T(8,128)(2,1)S(1)}, bf16[128,1024]{1,0:T(8,128)(2,1)S(1)}, u32[]{:S(2)}, u32[]{:S(2)}) collective-permute-start(bf16[128,1024]{1,0:T(8,128)(2,1)S(1)} %get-tuple-element.47.refs_1_), channel_id=1, source_target_pairs={{0,2},{2,0},{1,3},{3,1},{4,6},{6,4},{5,7},{7,5},{8,10},{10,8},{9,1... | collective-permute-start | bytes 786440 | tf_op jit(solution)/shard_map/ppermute | solution.py:648
  25.2 22.8 %collective-permute-start.8 = (bf16[256,512]{1,0:T(8,128)(2,1)S(1)}, bf16[256,512]{1,0:T(8,128)(2,1)S(1)}, u32[]{:S(2)}, u32[]{:S(2)}) collective-permute-start(bf16[256,512]{1,0:T(8,128)(2,1)S(1)} %get-tuple-element.51), channel_id=1, source_target_pairs={{0,0},{1,9},{2,6},{3,15},{4,4},{5,13},{6,10},{7,3},{8,8},{9,1},{10... | collective-permute-start | bytes 786440 | tf_op jit(solution)/shard_map/ppermute | solution.py:650
  25.9 16.9 %copy-start.1 = (bf16[256,2048]{1,0:T(8,128)(2,1)S(1)}, bf16[256,2048]{1,0:T(8,128)(2,1)}, u32[]{:S(2)}) copy-start(bf16[256,2048]{1,0:T(8,128)(2,1)} %dy_ref.1) | copy-start | bytes 3145732
  25.9 16.9 %copy-start.2 = (bf16[256,2048]{1,0:T(8,128)(2,1)S(1)}, bf16[256,2048]{1,0:T(8,128)(2,1)}, u32[]{:S(2)}) copy-start(bf16[256,2048]{1,0:T(8,128)(2,1)} %x_ref.4) | copy-start | bytes 3145732
  25.9 16.9 %copy-start.5 = (f32[256,32]{0,1:T(8,128)S(1)}, f32[256,32]{0,1:T(8,128)}, u32[]{:S(2)}) copy-start(f32[256,32]{0,1:T(8,128)} %param.10) | copy-start | bytes 98308
  25.9 24.8 %collective-permute-start.9 = (bf16[256,512]{1,0:T(8,128)(2,1)S(1)}, bf16[256,512]{1,0:T(8,128)(2,1)S(1)}, u32[]{:S(2)}, u32[]{:S(2)}) collective-permute-start(bf16[256,512]{1,0:T(8,128)(2,1)S(1)} %get-tuple-element.52), channel_id=1, source_target_pairs={{0,1},{1,8},{2,7},{3,14},{4,5},{5,12},{6,11},{7,2},{8,9},{9,0},{10... | collective-permute-start | bytes 786440 | tf_op jit(solution)/shard_map/ppermute | solution.py:651
  34.1 23.6 %collective-permute-start.10 = (bf16[256,512]{1,0:T(8,128)(2,1)S(1)}, bf16[256,512]{1,0:T(8,128)(2,1)S(1)}, u32[]{:S(2)}, u32[]{:S(2)}) collective-permute-start(bf16[256,512]{1,0:T(8,128)(2,1)S(1)} %get-tuple-element.48), channel_id=1, source_target_pairs={{0,4},{1,13},{2,2},{3,11},{4,8},{5,1},{6,6},{7,15},{8,12},{9,5},{1... | collective-permute-start | bytes 786440 | tf_op jit(solution)/shard_map/ppermute | solution.py:656
  42.8 15.0 %collective-permute-start.11 = (bf16[256,512]{1,0:T(8,128)(2,1)S(1)}, bf16[256,512]{1,0:T(8,128)(2,1)S(1)}, u32[]{:S(2)}, u32[]{:S(2)}) collective-permute-start(bf16[256,512]{1,0:T(8,128)(2,1)S(1)} %get-tuple-element.53), channel_id=1, source_target_pairs={{0,5},{1,12},{2,3},{3,10},{4,9},{5,0},{6,7},{7,14},{8,13},{9,4},{1... | collective-permute-start | bytes 786440 | tf_op jit(solution)/shard_map/ppermute | solution.py:657
  58.2 7.3 %collective-permute-start.12 = (bf16[1,128,1024]{2,1,0:T(8,128)(2,1)S(1)}, bf16[1,128,1024]{2,1,0:T(8,128)(2,1)S(1)}, u32[]{:S(2)}, u32[]{:S(2)}) collective-permute-start(bf16[1,128,1024]{2,1,0:T(8,128)(2,1)S(1)} %get-tuple-element.60), channel_id=1, source_target_pairs={{0,4},{12,8},{1,5},{13,9},{2,6},{14,10},{3,7},{15,11},{16,20},{28,... | collective-permute-start | bytes 786440 | tf_op jit(solution)/shard_map/ppermute | solution.py:685
  60.9 14.9 %collective-permute-start.17 = (bf16[1024,256]{1,0:T(8,128)(2,1)S(1)}, bf16[1024,256]{1,0:T(8,128)(2,1)S(1)}, u32[]{:S(2)}, u32[]{:S(2)}) collective-permute-start(bf16[1024,256]{1,0:T(8,128)(2,1)S(1)} %shard_map.116.refs_0_), channel_id=1, source_target_pairs={{0,1},{1,0},{2,3},{3,2},{4,5},{5,4},{6,7},{7,6},{8,9},{9,8},{10,11... | collective-permute-start | bytes 1572872 | tf_op jit(solution)/shard_map/ppermute | solution.py:675
  61.2 14.7 %collective-permute-start.18 = (bf16[1024,256]{1,0:T(8,128)(2,1)S(1)}, bf16[1024,256]{1,0:T(8,128)(2,1)S(1)}, u32[]{:S(2)}, u32[]{:S(2)}) collective-permute-start(bf16[1024,256]{1,0:T(8,128)(2,1)S(1)} %shard_map.117.refs_2_), channel_id=1, source_target_pairs={{0,1},{1,0},{2,3},{3,2},{4,5},{5,4},{6,7},{7,6},{8,9},{9,8},{10,11... | collective-permute-start | bytes 1572872 | tf_op jit(solution)/shard_map/ppermute | solution.py:675
  65.5 8.3 %collective-permute-start.15 = (bf16[1,128,1024]{2,1,0:T(8,128)(2,1)S(1)}, bf16[1,128,1024]{2,1,0:T(8,128)(2,1)S(1)}, u32[]{:S(2)}, u32[]{:S(2)}) collective-permute-start(bf16[1,128,1024]{2,1,0:T(8,128)(2,1)S(1)} %get-tuple-element.68), channel_id=1, source_target_pairs={{0,4},{12,8},{1,5},{13,9},{2,6},{14,10},{3,7},{15,11},{16,20},{28,... | collective-permute-start | bytes 786440 | tf_op jit(solution)/shard_map/ppermute | solution.py:685
  70.0 4.5 %collective-permute-start.13 = (bf16[1,128,1024]{2,1,0:T(8,128)(2,1)S(1)}, bf16[1,128,1024]{2,1,0:T(8,128)(2,1)S(1)}, u32[]{:S(2)}, u32[]{:S(2)}) collective-permute-start(bf16[1,128,1024]{2,1,0:T(8,128)(2,1)S(1)} %shard_map.111), channel_id=1, source_target_pairs={{4,8},{8,4},{5,9},{9,5},{6,10},{10,6},{7,11},{11,7},{20,24},{24,20... | collective-permute-start | bytes 786440 | tf_op jit(solution)/shard_map/ppermute | solution.py:685
  73.8 2.1 %collective-permute-start.16 = (bf16[1,128,1024]{2,1,0:T(8,128)(2,1)S(1)}, bf16[1,128,1024]{2,1,0:T(8,128)(2,1)S(1)}, u32[]{:S(2)}, u32[]{:S(2)}) collective-permute-start(bf16[1,128,1024]{2,1,0:T(8,128)(2,1)S(1)} %shard_map.115), channel_id=1, source_target_pairs={{4,8},{8,4},{5,9},{9,5},{6,10},{10,6},{7,11},{11,7},{20,24},{24,20... | collective-permute-start | bytes 786440 | tf_op jit(solution)/shard_map/ppermute | solution.py:685
  74.6 14.8 %collective-permute-start.14 = (bf16[1,128,1024]{2,1,0:T(8,128)(2,1)S(1)}, bf16[1,128,1024]{2,1,0:T(8,128)(2,1)S(1)}, u32[]{:S(2)}, u32[]{:S(2)}) collective-permute-start(bf16[1,128,1024]{2,1,0:T(8,128)(2,1)S(1)} %shard_map.112), channel_id=1, source_target_pairs={{4,0},{8,12},{5,1},{9,13},{6,2},{10,14},{7,3},{11,15},{20,16},{24,... | collective-permute-start | bytes 786440 | tf_op jit(solution)/shard_map/ppermute | solution.py:685
  76.0 15.2 %copy-start.6 = (f32[32]{0:T(128)S(1)}, f32[32]{0:T(128)}, u32[]{:S(2)}) copy-start(f32[32]{0:T(128)} %skip_ref.3) | copy-start | bytes 388
  76.0 26.1 %collective-permute-start.19 = (bf16[1,128,1024]{2,1,0:T(8,128)(2,1)S(1)}, bf16[1,128,1024]{2,1,0:T(8,128)(2,1)S(1)}, u32[]{:S(2)}, u32[]{:S(2)}) collective-permute-start(bf16[1,128,1024]{2,1,0:T(8,128)(2,1)S(1)} %shard_map.118), channel_id=1, source_target_pairs={{4,0},{8,12},{5,1},{9,13},{6,2},{10,14},{7,3},{11,15},{20,16},{24,... | collective-permute-start | bytes 786440 | tf_op jit(solution)/shard_map/ppermute | solution.py:685
  90.0 14.1 %collective-permute-start.24 = (bf16[256,256]{1,0:T(8,128)(2,1)S(1)}, bf16[256,256]{1,0:T(8,128)(2,1)S(1)}, u32[]{:S(2)}, u32[]{:S(2)}) collective-permute-start(bf16[256,256]{1,0:T(8,128)(2,1)S(1)} %shard_map.113.refs_4_), channel_id=1, source_target_pairs={{0,8},{4,12},{8,0},{12,4},{1,9},{5,13},{9,1},{13,5},{2,10},{6,14},... | collective-permute-start | bytes 393224 | tf_op jit(solution)/shard_map/ppermute | solution.py:703
  94.1 15.5 %collective-permute-start.25 = (bf16[256,256]{1,0:T(8,128)(2,1)S(1)}, bf16[256,256]{1,0:T(8,128)(2,1)S(1)}, u32[]{:S(2)}, u32[]{:S(2)}) collective-permute-start(bf16[256,256]{1,0:T(8,128)(2,1)S(1)} %shard_map.113.refs_4_), channel_id=1, source_target_pairs={{0,4},{4,8},{8,12},{12,0},{1,5},{5,9},{9,13},{13,1},{2,6},{6,10},{... | collective-permute-start | bytes 393224 | tf_op jit(solution)/shard_map/ppermute | solution.py:703
  94.3 15.2 %collective-permute-start.23 = (bf16[256,256]{1,0:T(8,128)(2,1)S(1)}, bf16[256,256]{1,0:T(8,128)(2,1)S(1)}, u32[]{:S(2)}, u32[]{:S(2)}) collective-permute-start(bf16[256,256]{1,0:T(8,128)(2,1)S(1)} %shard_map.113.refs_4_), channel_id=1, source_target_pairs={{0,12},{4,0},{8,4},{12,8},{1,13},{5,1},{9,5},{13,9},{2,14},{6,2},{... | collective-permute-start | bytes 393224 | tf_op jit(solution)/shard_map/ppermute | solution.py:703
  102.7 8.7 %collective-permute-start.22 = (bf16[256,256]{1,0:T(8,128)(2,1)S(1)}, bf16[256,256]{1,0:T(8,128)(2,1)S(1)}, u32[]{:S(2)}, u32[]{:S(2)}) collective-permute-start(bf16[256,256]{1,0:T(8,128)(2,1)S(1)} %shard_map.119.refs_4_), channel_id=1, source_target_pairs={{0,4},{4,8},{8,12},{12,0},{1,5},{5,9},{9,13},{13,1},{2,6},{6,10},{... | collective-permute-start | bytes 393224 | tf_op jit(solution)/shard_map/ppermute | solution.py:703
  102.7 9.8 %collective-permute-start.21 = (bf16[256,256]{1,0:T(8,128)(2,1)S(1)}, bf16[256,256]{1,0:T(8,128)(2,1)S(1)}, u32[]{:S(2)}, u32[]{:S(2)}) collective-permute-start(bf16[256,256]{1,0:T(8,128)(2,1)S(1)} %shard_map.119.refs_4_), channel_id=1, source_target_pairs={{0,8},{4,12},{8,0},{12,4},{1,9},{5,13},{9,1},{13,5},{2,10},{6,14},... | collective-permute-start | bytes 393224 | tf_op jit(solution)/shard_map/ppermute | solution.py:703
  104.1 8.4 %collective-permute-start.20 = (bf16[256,256]{1,0:T(8,128)(2,1)S(1)}, bf16[256,256]{1,0:T(8,128)(2,1)S(1)}, u32[]{:S(2)}, u32[]{:S(2)}) collective-permute-start(bf16[256,256]{1,0:T(8,128)(2,1)S(1)} %shard_map.119.refs_4_), channel_id=1, source_target_pairs={{0,12},{4,0},{8,4},{12,8},{1,13},{5,1},{9,5},{13,9},{2,14},{6,2},{... | collective-permute-start | bytes 393224 | tf_op jit(solution)/shard_map/ppermute | solution.py:703

commit v6 on v5

--- a/solution.py
+++ b/solution.py
@@ -632,7 +632,7 @@
 ):
     groups = master.shape[1] // (2 * STATE)
     axes = ("seq", "head", "sub")
-    rows = hidden.shape[0] // 2
+    rows = hidden.shape[0] * 3 // 8
     stays, crosses, beside, onward = transpose_pairs(seq)
     relayed = lax.ppermute(hidden[rows:], axes, beside)
     top = lax.ppermute(hidden[:rows], axes, stays + crosses)

time: 115 us -> 116 us (level)
  starting transfers between devices: 47.3 us -> 44.8 us
  waiting for transfers between devices: 39.2 us -> 41.2 us
    ppermute x1, waiting for transfers between devices: 0.01 us -> 4.15 us  [on_device(): other = [lax.ppermute(top, 'head', SWAP)]]
    ppermute x1, waiting for transfers between devices: 2.71 us -> 0.01 us  [on_device(): lax.ppermute(cross, axes, block_pairs(seq, True, False))]
    ppermute x1, starting transfers between devices: 8.66 us -> 6.66 us  [on_device(): lax.ppermute(same, axes, block_pairs(seq, False, True))]
    ppermute x1, starting transfers between devices: 4.9 us -> 3.49 us  [on_device(): lax.ppermute(relayed, axes, onward)]
    ppermute x1, waiting for transfers between devices: 5.87 us -> 7.25 us  [on_device(): relayed = lax.ppermute(hidden[rows:], axes, beside)]
    ppermute x1, starting transfers between devices: 7.26 us -> 6.01 us  [on_device(): lax.ppermute(cross, axes, block_pairs(seq, True, False))]
  transfers between devices with their start and end apart: 26 -> 26, of which waited for: 8 -> 8; matrix products, arithmetic and copies ran while one was open for 1% -> 2% of each run, Pallas kernels for 17% -> 17%
where the time goes in v6:
time: 116 us; the launch traced here: 115 us
  starting transfers between devices  44.8 us (39%)
  waiting for transfers between devices  41.2 us (36%)
  Pallas kernels  22.3 us (19%)
  local copies, waits for them, and re-layouts  5.63 us (5%)
  between operations  1.2 us (1%)
    ppermute x6, waiting for transfers between devices, on_device(): arrived[p].append(lax.ppermute(message, 'seq', pairs))  22.2 us
    ppermute x6, starting transfers between devices, on_device(): arrived[p].append(lax.ppermute(message, 'seq', pairs))  11 us
    ppermute x6, starting transfers between devices, on_device(): blocks.append(lax.ppermute(payload, 'seq', to_all(seq, seq - distance)))  9.39 us
    ppermute x1, waiting for transfers between devices, on_device(): relayed = lax.ppermute(hidden[rows:], axes, beside)  7.25 us
    ppermute x1, starting transfers between devices, on_device(): lax.ppermute(same, axes, block_pairs(seq, False, True))  6.66 us
    ppermute x1, waiting for transfers between devices, on_device(): lax.ppermute(cross, axes, block_pairs(seq, False, False))  6.39 us
    ppermute x1, starting transfers between devices, on_device(): lax.ppermute(cross, axes, block_pairs(seq, True, False))  6.01 us
    pallas_call x2, Pallas kernels, output(): call(functools.partial(output_kernel, ahead, first), jax.ShapeDtypeStruct...  5.75 us
  transfers between devices with their start and end apart: 26, of which 8 were waited for; matrix products, arithmetic and copies ran while one was open for 2% of the time, Pallas kernels for 17%

profile of v6, /device:TPU:0, one launch (start us, length us, event | category | flops | bytes accessed | tf_op | source)
XLA Modules:
  0.0 115.2 jit_solution(11965943486697546946)
XLA Ops:
  0.6 0.5 collective-permute-start.1
  1.2 1.0 slice.8
  2.2 1.3 %collective-permute-start.5 = (bf16[160,1024]{1,0:T(8,128)(2,1)S(1)}, bf16[160,1024]{1,0:T(8,128)(2,1)S(1)}, u32[]{:S(2)}, u32[]{:S(2)}) collective-permute-start(bf16[160,1024]{1,0:T(8,128)(2,1)S(1)} %slice.8), channel_id=1, source_target_pairs={{1,3},{2,0},{4,6},{7,5},{9,11},{10,8},{12,14},{15,13},{17,19},{18,... | collective-permute-start | bytes 983048 | tf_op jit(solution)/shard_map/ppermute | solution.py:637
  3.5 0.7 collective-permute-start.4
  4.2 7.3 %collective-permute-done.5 = bf16[160,1024]{1,0:T(8,128)(2,1)S(1)} collective-permute-done((bf16[160,1024]{1,0:T(8,128)(2,1)S(1)}, bf16[160,1024]{1,0:T(8,128)(2,1)S(1)}, u32[]{:S(2)}, u32[]{:S(2)}) %collective-permute-start.5) | collective-permute-done | bytes 327712 | tf_op jit(solution)/shard_map/ppermute | solution.py:637
  11.5 3.5 %collective-permute-start.6 = (bf16[160,1024]{1,0:T(8,128)(2,1)S(1)}, bf16[160,1024]{1,0:T(8,128)(2,1)S(1)}, u32[]{:S(2)}, u32[]{:S(2)}) collective-permute-start(bf16[160,1024]{1,0:T(8,128)(2,1)S(1)} %collective-permute-done.5), channel_id=1, source_target_pairs={{3,7},{0,9},{6,2},{5,13},{11,6},{8,8},{14,3},{13,12},{19,23},{16,2... | collective-permute-start | bytes 983048 | tf_op jit(solution)/shard_map/ppermute | solution.py:639
  15.0 0.9 slice.7
  15.9 0.7 collective-permute-start
  16.6 1.6 %copy-done = f32[1024,512]{1,0:T(8,128)S(1)} copy-done((f32[1024,512]{1,0:T(8,128)S(1)}, f32[1024,512]{1,0:T(8,128)}, u32[]{:S(2)}) %copy-start) | copy-done | bytes 2097176
  18.2 1.0 copy-done.3
  19.2 1.0 copy-done.4
  20.3 1.7 %shard_map.103 = (bf16[1024,512]{1,0:T(8,128)(2,1)S(1)}, f32[1024,512]{1,0:T(8,128)S(1)}, bf16[1024,512]{1,0:T(8,128)(2,1)S(1)}) custom-call(f32[1024,512]{1,0:T(8,128)S(1)} %copy-done, s32[256,512]{1,0:T(8,128)S(1)} %copy-done.4, s32[256,512]{1,0:T(8,128)S(1)} %copy-done.3), custom_call_target="tpu_custom_call" | custom-call | flops 1572864000 | bytes 7340032 | tf_op jit(solution)/shard_map/pallas_call | solution.py:77
  22.0 1.2 %shard_map.104.refs_2_.refs_4_.sibling_weight_ref = bf16[1024,512]{1,0:T(8,128)(2,1)S(1)} custom-call(f32[1024,512]{1,0:T(8,128)S(1)} %collective-permute-done.1.master_ref, s32[256,512]{1,0:T(8,128)S(1)} %collective-permute-done.2.now_ref), custom_call_target="tpu_custom_call" | custom-call | flops 1572864000 | bytes 3670016 | tf_op jit(solution)/shard_map/pallas_call | solution.py:101
  23.2 0.8 shard_map.106
  24.0 3.0 %collective-permute-start.7 = (bf16[160,1024]{1,0:T(8,128)(2,1)S(1)}, bf16[160,1024]{1,0:T(8,128)(2,1)S(1)}, u32[]{:S(2)}, u32[]{:S(2)}) collective-permute-start(bf16[160,1024]{1,0:T(8,128)(2,1)S(1)} %get-tuple-element.47.refs_1_), channel_id=1, source_target_pairs={{0,2},{2,0},{1,3},{3,1},{4,6},{6,4},{5,7},{7,5},{8,10},{10,8},{9,1... | collective-permute-start | bytes 983048 | tf_op jit(solution)/shard_map/ppermute | solution.py:648
  27.1 0.7 collective-permute-start.8
  27.8 6.0 %collective-permute-start.9 = (bf16[256,512]{1,0:T(8,128)(2,1)S(1)}, bf16[256,512]{1,0:T(8,128)(2,1)S(1)}, u32[]{:S(2)}, u32[]{:S(2)}) collective-permute-start(bf16[256,512]{1,0:T(8,128)(2,1)S(1)} %get-tuple-element.52), channel_id=1, source_target_pairs={{0,1},{1,8},{2,7},{3,14},{4,5},{5,12},{6,11},{7,2},{8,9},{9,0},{10... | collective-permute-start | bytes 786440 | tf_op jit(solution)/shard_map/ppermute | solution.py:651
  33.8 4.1 %collective-permute-done.3.refs_0_ = bf16[96,1024]{1,0:T(8,128)(2,1)S(1)} collective-permute-done((bf16[96,1024]{1,0:T(8,128)(2,1)S(1)}, bf16[96,1024]{1,0:T(8,128)(2,1)S(1)}, u32[]{:S(2)}, u32[]{:S(2)}) %collective-permute-start.3) | collective-permute-done | bytes 196640 | tf_op jit(solution)/shard_map/ppermute | solution.py:646
  38.0 0.5 shard_map.105
  38.5 0.5 shard_map.107
  39.0 6.7 %collective-permute-start.10 = (bf16[256,512]{1,0:T(8,128)(2,1)S(1)}, bf16[256,512]{1,0:T(8,128)(2,1)S(1)}, u32[]{:S(2)}, u32[]{:S(2)}) collective-permute-start(bf16[256,512]{1,0:T(8,128)(2,1)S(1)} %get-tuple-element.48), channel_id=1, source_target_pairs={{0,4},{1,13},{2,2},{3,11},{4,8},{5,1},{6,6},{7,15},{8,12},{9,5},{1... | collective-permute-start | bytes 786440 | tf_op jit(solution)/shard_map/ppermute | solution.py:656
  45.7 5.2 %shard_map.108 = (bf16[256,2048]{1,0:T(8,128)(2,1)S(1)}, bf16[256,2048]{1,0:T(8,128)(2,1)S(1)}, bf16[2,256,256]{2,1,0:T(8,128)(2,1)S(1)}, bf16[2,256,256]{2,1,0:...) custom-call(bf16[256,2048]{1,0:T(8,128)(2,1)S(1)} %copy-done.2, ...), custom_call_target="tpu_custom_call" | custom-call | flops 5242880000 | bytes 4194304 | tf_op jit(solution)/shard_map/pallas_call | solution.py:198
  51.0 6.4 %collective-permute-done.11.refs_3_ = bf16[256,512]{1,0:T(8,128)(2,1)S(1)} collective-permute-done((bf16[256,512]{1,0:T(8,128)(2,1)S(1)}, bf16[256,512]{1,0:T(8,128)(2,1)S(1)}, u32[]{:S(2)}, u32[]{:S(2)}) %collective-permute-start.11) | collective-permute-done | bytes 262176 | tf_op jit(solution)/shard_map/ppermute | solution.py:657
  57.3 0.4 shard_map.110
  57.8 2.7 %collective-permute-start.12 = (bf16[1,128,1024]{2,1,0:T(8,128)(2,1)S(1)}, bf16[1,128,1024]{2,1,0:T(8,128)(2,1)S(1)}, u32[]{:S(2)}, u32[]{:S(2)}) collective-permute-start(bf16[1,128,1024]{2,1,0:T(8,128)(2,1)S(1)} %get-tuple-element.60), channel_id=1, source_target_pairs={{0,4},{12,8},{1,5},{13,9},{2,6},{14,10},{3,7},{15,11},{16,20},{28,... | collective-permute-start | bytes 786440 | tf_op jit(solution)/shard_map/ppermute | solution.py:685
  61.0 1.1 collective-permute-start.17
  62.5 0.5 shard_map.109
  63.0 3.9 %collective-permute-done.12.arrived_ref.near_ref = bf16[1,128,1024]{2,1,0:T(8,128)(2,1)S(1)} collective-permute-done((bf16[1,128,1024]{2,1,0:T(8,128)(2,1)S(1)}, bf16[1,128,1024]{2,1,0:T(8,128)(2,1)S(1)}, u32[]{:S(2)}, u32[]{:S(2)}) %collective-permute-start.12) | collective-permute-done | bytes 262176 | tf_op jit(solution)/shard_map/ppermute | solution.py:685
  66.9 4.4 %collective-permute-start.15 = (bf16[1,128,1024]{2,1,0:T(8,128)(2,1)S(1)}, bf16[1,128,1024]{2,1,0:T(8,128)(2,1)S(1)}, u32[]{:S(2)}, u32[]{:S(2)}) collective-permute-start(bf16[1,128,1024]{2,1,0:T(8,128)(2,1)S(1)} %get-tuple-element.68), channel_id=1, source_target_pairs={{0,4},{12,8},{1,5},{13,9},{2,6},{14,10},{3,7},{15,11},{16,20},{28,... | collective-permute-start | bytes 786440 | tf_op jit(solution)/shard_map/ppermute | solution.py:685
  71.4 0.7 collective-permute-start.13
  72.0 5.1 %collective-permute-done.15.arrived_ref.near_ref = bf16[1,128,1024]{2,1,0:T(8,128)(2,1)S(1)} collective-permute-done((bf16[1,128,1024]{2,1,0:T(8,128)(2,1)S(1)}, bf16[1,128,1024]{2,1,0:T(8,128)(2,1)S(1)}, u32[]{:S(2)}, u32[]{:S(2)}) %collective-permute-start.15) | collective-permute-done | bytes 262176 | tf_op jit(solution)/shard_map/ppermute | solution.py:685
  77.2 0.7 collective-permute-start.16
  78.0 1.3 %collective-permute-start.14 = (bf16[1,128,1024]{2,1,0:T(8,128)(2,1)S(1)}, bf16[1,128,1024]{2,1,0:T(8,128)(2,1)S(1)}, u32[]{:S(2)}, u32[]{:S(2)}) collective-permute-start(bf16[1,128,1024]{2,1,0:T(8,128)(2,1)S(1)} %shard_map.112), channel_id=1, source_target_pairs={{4,0},{8,12},{5,1},{9,13},{6,2},{10,14},{7,3},{11,15},{20,16},{24,... | collective-permute-start | bytes 786440 | tf_op jit(solution)/shard_map/ppermute | solution.py:685
  79.4 1.3 %collective-permute-start.19 = (bf16[1,128,1024]{2,1,0:T(8,128)(2,1)S(1)}, bf16[1,128,1024]{2,1,0:T(8,128)(2,1)S(1)}, u32[]{:S(2)}, u32[]{:S(2)}) collective-permute-start(bf16[1,128,1024]{2,1,0:T(8,128)(2,1)S(1)} %shard_map.118), channel_id=1, source_target_pairs={{4,0},{8,12},{5,1},{9,13},{6,2},{10,14},{7,3},{11,15},{20,16},{24,... | collective-permute-start | bytes 786440 | tf_op jit(solution)/shard_map/ppermute | solution.py:685
  80.7 9.1 %collective-permute-done.14.refs_1_ = bf16[1,128,1024]{2,1,0:T(8,128)(2,1)S(1)} collective-permute-done((bf16[1,128,1024]{2,1,0:T(8,128)(2,1)S(1)}, bf16[1,128,1024]{2,1,0:T(8,128)(2,1)S(1)}, u32[]{:S(2)}, u32[]{:S(2)}) %collective-permute-start.14) | collective-permute-done | bytes 262176 | tf_op jit(solution)/shard_map/ppermute | solution.py:685
  89.8 0.6 shard_map.113.refs_4_
  90.4 1.5 %collective-permute-start.24 = (bf16[256,256]{1,0:T(8,128)(2,1)S(1)}, bf16[256,256]{1,0:T(8,128)(2,1)S(1)}, u32[]{:S(2)}, u32[]{:S(2)}) collective-permute-start(bf16[256,256]{1,0:T(8,128)(2,1)S(1)} %shard_map.113.refs_4_), channel_id=1, source_target_pairs={{0,8},{4,12},{8,0},{12,4},{1,9},{5,13},{9,1},{13,5},{2,10},{6,14},... | collective-permute-start | bytes 393224 | tf_op jit(solution)/shard_map/ppermute | solution.py:703
  91.9 2.9 %shard_map.114.refs_2_ = bf16[256,2048]{1,0:T(8,128)(2,1)} custom-call(f32[32]{0:T(128)S(1)} %copy-done.6, bf16[256,2048]{1,0:T(8,128)(2,1)S(1)} %copy-done.2, f32[2,256,16]{2,1,0:T(8,128)S(1)} %get-tuple-element.74.cum_ref, f32[2,16,256]{2,1,0:T(8,128)S(1)} %get-tuple-element.65.cumt_ref, bf16[256,256]{1,0:T(8,128)(2,1)S(1)} %get-tuple-element.57.proj_ref, ...), custom_call_target="tpu_custom_call" | custom-call | flops 2097152000 | bytes 2621440 | tf_op jit(solution)/shard_map/pallas_call | solution.py:464
  94.8 0.7 collective-permute-start.25
  95.5 3.1 %collective-permute-start.23 = (bf16[256,256]{1,0:T(8,128)(2,1)S(1)}, bf16[256,256]{1,0:T(8,128)(2,1)S(1)}, u32[]{:S(2)}, u32[]{:S(2)}) collective-permute-start(bf16[256,256]{1,0:T(8,128)(2,1)S(1)} %shard_map.113.refs_4_), channel_id=1, source_target_pairs={{0,12},{4,0},{8,4},{12,8},{1,13},{5,1},{9,5},{13,9},{2,14},{6,2},{... | collective-permute-start | bytes 393224 | tf_op jit(solution)/shard_map/ppermute | solution.py:703
  98.6 4.2 %collective-permute-done.19.refs_1_ = bf16[1,128,1024]{2,1,0:T(8,128)(2,1)S(1)} collective-permute-done((bf16[1,128,1024]{2,1,0:T(8,128)(2,1)S(1)}, bf16[1,128,1024]{2,1,0:T(8,128)(2,1)S(1)}, u32[]{:S(2)}, u32[]{:S(2)}) %collective-permute-start.19) | collective-permute-done | bytes 262176 | tf_op jit(solution)/shard_map/ppermute | solution.py:685
  102.8 0.6 shard_map.119.refs_4_
  103.6 1.2 %collective-permute-start.21 = (bf16[256,256]{1,0:T(8,128)(2,1)S(1)}, bf16[256,256]{1,0:T(8,128)(2,1)S(1)}, u32[]{:S(2)}, u32[]{:S(2)}) collective-permute-start(bf16[256,256]{1,0:T(8,128)(2,1)S(1)} %shard_map.119.refs_4_), channel_id=1, source_target_pairs={{0,8},{4,12},{8,0},{12,4},{1,9},{5,13},{9,1},{13,5},{2,10},{6,14},... | collective-permute-start | bytes 393224 | tf_op jit(solution)/shard_map/ppermute | solution.py:703
  104.8 2.6 %collective-permute-start.20 = (bf16[256,256]{1,0:T(8,128)(2,1)S(1)}, bf16[256,256]{1,0:T(8,128)(2,1)S(1)}, u32[]{:S(2)}, u32[]{:S(2)}) collective-permute-start(bf16[256,256]{1,0:T(8,128)(2,1)S(1)} %shard_map.119.refs_4_), channel_id=1, source_target_pairs={{0,12},{4,0},{8,4},{12,8},{1,13},{5,1},{9,5},{13,9},{2,14},{6,2},{... | collective-permute-start | bytes 393224 | tf_op jit(solution)/shard_map/ppermute | solution.py:703
  107.4 2.9 %shard_map.120 = bf16[256,2048]{1,0:T(8,128)(2,1)} custom-call(f32[32]{0:T(128)S(1)} %copy-done.6, bf16[256,2048]{1,0:T(8,128)(2,1)S(1)} %copy-done.2, f32[2,256,16]{2,1,0:T(8,128)S(1)} %get-tuple-element.74.cum_ref, f32[2,16,256]{2,1,0:T(8,128)S(1)} %get-tuple-element.65.cumt_ref, ...), custom_call_target="tpu_custom_call", output_to_operand_aliasing={{}: (8, {})} | custom-call | flops 2097152000 | bytes 2621440 | tf_op jit(solution)/shard_map/pallas_call | solution.py:464
  110.3 1.8 %shard_map.121 = (f32[1024,512]{1,0:T(8,128)}, bf16[1024,512]{1,0:T(8,128)(2,1)}) custom-call(bf16[1024,256]{1,0:T(8,128)(2,1)S(1)} %shard_map.116.refs_0_, bf16[1024,256]{1,0:T(8,128)(2,1)S(1)} %collective-permute-done.17.refs_1_, bf16[1024,256]{1,0:T(8,128)(2,1)S(1)} %shard_map.117.refs_2_, bf16[1024,256]{1,0:T(8,128)(2,1)S(1)} %collective-permute-done.18.refs_3_, ...), custom_call_target="tpu_custom_call" | custom-call | flops 536870912 | bytes 5767168 | tf_op jit(solution)/shard_map/pallas_call | solution.py:535
  112.1 1.1 collective-permute-done.21.refs_6_
  113.2 1.8 %shard_map.122 = (f32[1024,512]{1,0:T(8,128)}, bf16[1024,512]{1,0:T(8,128)(2,1)}) custom-call(bf16[1024,256]{1,0:T(8,128)(2,1)S(1)} %shard_map.116.refs_0_, bf16[1024,256]{1,0:T(8,128)(2,1)S(1)} %collective-permute-done.17.refs_1_, bf16[1024,256]{1,0:T(8,128)(2,1)S(1)} %shard_map.117.refs_2_, ...), custom_call_target="tpu_custom_call", output_to_operand_aliasing={{0}: (10, {}), {1}: (11, {})} | custom-call | flops 536870912 | bytes 5767168 | tf_op jit(solution)/shard_map/pallas_call | solution.py:535
  (40 shorter events, 1.8 us)
Async XLA Ops:
  0.6 21.3 %collective-permute-start.1 = (f32[1024,512]{1,0:T(8,128)}, f32[1024,512]{1,0:T(8,128)S(1)}, u32[]{:S(2)}, u32[]{:S(2)}) collective-permute-start(f32[1024,512]{1,0:T(8,128)} %master_ref.1), channel_id=1, source_target_pairs={{0,1},{1,0},{2,3},{3,2},{4,5},{5,4},{6,7},{7,6},{8,9},{9,8},{10,11... | collective-permute-start | bytes 6291464 | tf_op jit(solution)/shard_map/ppermute | solution.py:642
  1.1 20.8 %collective-permute-start.2 = (s32[256,512]{1,0:T(8,128)}, s32[256,512]{1,0:T(8,128)S(1)}, u32[]{:S(2)}, u32[]{:S(2)}) collective-permute-start(s32[256,512]{1,0:T(8,128)} %now_ref.1), channel_id=1, source_target_pairs={{0,1},{1,0},{2,3},{3,2},{4,5},{5,4},{6,7},{7,6},{8,9},{9,8},{10,11... | collective-permute-start | bytes 1572872 | tf_op jit(solution)/shard_map/ppermute | solution.py:642
  2.2 9.2 %collective-permute-start.5 = (bf16[160,1024]{1,0:T(8,128)(2,1)S(1)}, bf16[160,1024]{1,0:T(8,128)(2,1)S(1)}, u32[]{:S(2)}, u32[]{:S(2)}) collective-permute-start(bf16[160,1024]{1,0:T(8,128)(2,1)S(1)} %slice.8), channel_id=1, source_target_pairs={{1,3},{2,0},{4,6},{7,5},{9,11},{10,8},{12,14},{15,13},{17,19},{18,... | collective-permute-start | bytes 983048 | tf_op jit(solution)/shard_map/ppermute | solution.py:637
  3.5 19.6 %collective-permute-start.4 = (bf16[160,1024]{1,0:T(8,128)(2,1)S(1)}, bf16[160,1024]{1,0:T(8,128)(2,1)S(1)}, u32[]{:S(2)}, u32[]{:S(2)}) collective-permute-start(bf16[160,1024]{1,0:T(8,128)(2,1)S(1)} %slice.8), channel_id=1, source_target_pairs={{0,0},{3,14},{5,4},{6,11},{8,1},{11,15},{13,5},{14,10},{16,16},{19... | collective-permute-start | bytes 983048 | tf_op jit(solution)/shard_map/ppermute | solution.py:639
  11.5 11.7 %collective-permute-start.6 = (bf16[160,1024]{1,0:T(8,128)(2,1)S(1)}, bf16[160,1024]{1,0:T(8,128)(2,1)S(1)}, u32[]{:S(2)}, u32[]{:S(2)}) collective-permute-start(bf16[160,1024]{1,0:T(8,128)(2,1)S(1)} %collective-permute-done.5), channel_id=1, source_target_pairs={{3,7},{0,9},{6,2},{5,13},{11,6},{8,8},{14,3},{13,12},{19,23},{16,2... | collective-permute-start | bytes 983048 | tf_op jit(solution)/shard_map/ppermute | solution.py:639
  15.9 7.2 %collective-permute-start = (bf16[96,1024]{1,0:T(8,128)(2,1)S(1)}, bf16[96,1024]{1,0:T(8,128)(2,1)S(1)}, u32[]{:S(2)}, u32[]{:S(2)}) collective-permute-start(bf16[96,1024]{1,0:T(8,128)(2,1)S(1)} %slice.7), channel_id=1, source_target_pairs={{0,0},{3,14},{5,4},{6,11},{8,1},{11,15},{13,5},{14,10},{1,7},{2,9}... | collective-permute-start | bytes 589832 | tf_op jit(solution)/shard_map/ppermute | solution.py:638
  16.6 1.6 %copy-start = (f32[1024,512]{1,0:T(8,128)S(1)}, f32[1024,512]{1,0:T(8,128)}, u32[]{:S(2)}) copy-start(f32[1024,512]{1,0:T(8,128)} %master_ref.1) | copy-start | bytes 6291460
  18.2 1.0 copy-start.3
  19.2 1.0 copy-start.4
  24.0 14.4 %collective-permute-start.7 = (bf16[160,1024]{1,0:T(8,128)(2,1)S(1)}, bf16[160,1024]{1,0:T(8,128)(2,1)S(1)}, u32[]{:S(2)}, u32[]{:S(2)}) collective-permute-start(bf16[160,1024]{1,0:T(8,128)(2,1)S(1)} %get-tuple-element.47.refs_1_), channel_id=1, source_target_pairs={{0,2},{2,0},{1,3},{3,1},{4,6},{6,4},{5,7},{7,5},{8,10},{10,8},{9,1... | collective-permute-start | bytes 983048 | tf_op jit(solution)/shard_map/ppermute | solution.py:648
  27.0 10.9 %collective-permute-start.3 = (bf16[96,1024]{1,0:T(8,128)(2,1)S(1)}, bf16[96,1024]{1,0:T(8,128)(2,1)S(1)}, u32[]{:S(2)}, u32[]{:S(2)}) collective-permute-start(bf16[96,1024]{1,0:T(8,128)(2,1)S(1)} %collective-permute-done.refs_0_), channel_id=1, source_target_pairs={{0,2},{2,0},{1,3},{3,1},{4,6},{6,4},{5,7},{7,5},{8,10},{10,8},{9,1... | collective-permute-start | bytes 589832 | tf_op jit(solution)/shard_map/ppermute | solution.py:646
  27.1 23.8 %collective-permute-start.8 = (bf16[256,512]{1,0:T(8,128)(2,1)S(1)}, bf16[256,512]{1,0:T(8,128)(2,1)S(1)}, u32[]{:S(2)}, u32[]{:S(2)}) collective-permute-start(bf16[256,512]{1,0:T(8,128)(2,1)S(1)} %get-tuple-element.51), channel_id=1, source_target_pairs={{0,0},{1,9},{2,6},{3,15},{4,4},{5,13},{6,10},{7,3},{8,8},{9,1},{10... | collective-permute-start | bytes 786440 | tf_op jit(solution)/shard_map/ppermute | solution.py:650
  27.8 17.9 %copy-start.1 = (bf16[256,2048]{1,0:T(8,128)(2,1)S(1)}, bf16[256,2048]{1,0:T(8,128)(2,1)}, u32[]{:S(2)}) copy-start(bf16[256,2048]{1,0:T(8,128)(2,1)} %dy_ref.1) | copy-start | bytes 3145732
  27.8 17.9 %copy-start.2 = (bf16[256,2048]{1,0:T(8,128)(2,1)S(1)}, bf16[256,2048]{1,0:T(8,128)(2,1)}, u32[]{:S(2)}) copy-start(bf16[256,2048]{1,0:T(8,128)(2,1)} %x_ref.4) | copy-start | bytes 3145732
  27.8 17.9 %copy-start.5 = (f32[256,32]{0,1:T(8,128)S(1)}, f32[256,32]{0,1:T(8,128)}, u32[]{:S(2)}) copy-start(f32[256,32]{0,1:T(8,128)} %param.10) | copy-start | bytes 98308
  27.8 23.1 %collective-permute-start.9 = (bf16[256,512]{1,0:T(8,128)(2,1)S(1)}, bf16[256,512]{1,0:T(8,128)(2,1)S(1)}, u32[]{:S(2)}, u32[]{:S(2)}) collective-permute-start(bf16[256,512]{1,0:T(8,128)(2,1)S(1)} %get-tuple-element.52), channel_id=1, source_target_pairs={{0,1},{1,8},{2,7},{3,14},{4,5},{5,12},{6,11},{7,2},{8,9},{9,0},{10... | collective-permute-start | bytes 786440 | tf_op jit(solution)/shard_map/ppermute | solution.py:651
  39.0 18.4 %collective-permute-start.10 = (bf16[256,512]{1,0:T(8,128)(2,1)S(1)}, bf16[256,512]{1,0:T(8,128)(2,1)S(1)}, u32[]{:S(2)}, u32[]{:S(2)}) collective-permute-start(bf16[256,512]{1,0:T(8,128)(2,1)S(1)} %get-tuple-element.48), channel_id=1, source_target_pairs={{0,4},{1,13},{2,2},{3,11},{4,8},{5,1},{6,6},{7,15},{8,12},{9,5},{1... | collective-permute-start | bytes 786440 | tf_op jit(solution)/shard_map/ppermute | solution.py:656
  45.7 11.7 %collective-permute-start.11 = (bf16[256,512]{1,0:T(8,128)(2,1)S(1)}, bf16[256,512]{1,0:T(8,128)(2,1)S(1)}, u32[]{:S(2)}, u32[]{:S(2)}) collective-permute-start(bf16[256,512]{1,0:T(8,128)(2,1)S(1)} %get-tuple-element.53), channel_id=1, source_target_pairs={{0,5},{1,12},{2,3},{3,10},{4,9},{5,0},{6,7},{7,14},{8,13},{9,4},{1... | collective-permute-start | bytes 786440 | tf_op jit(solution)/shard_map/ppermute | solution.py:657
  57.8 9.1 %collective-permute-start.12 = (bf16[1,128,1024]{2,1,0:T(8,128)(2,1)S(1)}, bf16[1,128,1024]{2,1,0:T(8,128)(2,1)S(1)}, u32[]{:S(2)}, u32[]{:S(2)}) collective-permute-start(bf16[1,128,1024]{2,1,0:T(8,128)(2,1)S(1)} %get-tuple-element.60), channel_id=1, source_target_pairs={{0,4},{12,8},{1,5},{13,9},{2,6},{14,10},{3,7},{15,11},{16,20},{28,... | collective-permute-start | bytes 786440 | tf_op jit(solution)/shard_map/ppermute | solution.py:685
  61.0 18.3 %collective-permute-start.17 = (bf16[1024,256]{1,0:T(8,128)(2,1)S(1)}, bf16[1024,256]{1,0:T(8,128)(2,1)S(1)}, u32[]{:S(2)}, u32[]{:S(2)}) collective-permute-start(bf16[1024,256]{1,0:T(8,128)(2,1)S(1)} %shard_map.116.refs_0_), channel_id=1, source_target_pairs={{0,1},{1,0},{2,3},{3,2},{4,5},{5,4},{6,7},{7,6},{8,9},{9,8},{10,11... | collective-permute-start | bytes 1572872 | tf_op jit(solution)/shard_map/ppermute | solution.py:675
  62.5 16.8 %collective-permute-start.18 = (bf16[1024,256]{1,0:T(8,128)(2,1)S(1)}, bf16[1024,256]{1,0:T(8,128)(2,1)S(1)}, u32[]{:S(2)}, u32[]{:S(2)}) collective-permute-start(bf16[1024,256]{1,0:T(8,128)(2,1)S(1)} %shard_map.117.refs_2_), channel_id=1, source_target_pairs={{0,1},{1,0},{2,3},{3,2},{4,5},{5,4},{6,7},{7,6},{8,9},{9,8},{10,11... | collective-permute-start | bytes 1572872 | tf_op jit(solution)/shard_map/ppermute | solution.py:675
  66.9 10.2 %collective-permute-start.15 = (bf16[1,128,1024]{2,1,0:T(8,128)(2,1)S(1)}, bf16[1,128,1024]{2,1,0:T(8,128)(2,1)S(1)}, u32[]{:S(2)}, u32[]{:S(2)}) collective-permute-start(bf16[1,128,1024]{2,1,0:T(8,128)(2,1)S(1)} %get-tuple-element.68), channel_id=1, source_target_pairs={{0,4},{12,8},{1,5},{13,9},{2,6},{14,10},{3,7},{15,11},{16,20},{28,... | collective-permute-start | bytes 786440 | tf_op jit(solution)/shard_map/ppermute | solution.py:685
  71.4 6.5 %collective-permute-start.13 = (bf16[1,128,1024]{2,1,0:T(8,128)(2,1)S(1)}, bf16[1,128,1024]{2,1,0:T(8,128)(2,1)S(1)}, u32[]{:S(2)}, u32[]{:S(2)}) collective-permute-start(bf16[1,128,1024]{2,1,0:T(8,128)(2,1)S(1)} %shard_map.111), channel_id=1, source_target_pairs={{4,8},{8,4},{5,9},{9,5},{6,10},{10,6},{7,11},{11,7},{20,24},{24,20... | collective-permute-start | bytes 786440 | tf_op jit(solution)/shard_map/ppermute | solution.py:685
  77.2 2.1 %collective-permute-start.16 = (bf16[1,128,1024]{2,1,0:T(8,128)(2,1)S(1)}, bf16[1,128,1024]{2,1,0:T(8,128)(2,1)S(1)}, u32[]{:S(2)}, u32[]{:S(2)}) collective-permute-start(bf16[1,128,1024]{2,1,0:T(8,128)(2,1)S(1)} %shard_map.115), channel_id=1, source_target_pairs={{4,8},{8,4},{5,9},{9,5},{6,10},{10,6},{7,11},{11,7},{20,24},{24,20... | collective-permute-start | bytes 786440 | tf_op jit(solution)/shard_map/ppermute | solution.py:685
  78.0 11.8 %collective-permute-start.14 = (bf16[1,128,1024]{2,1,0:T(8,128)(2,1)S(1)}, bf16[1,128,1024]{2,1,0:T(8,128)(2,1)S(1)}, u32[]{:S(2)}, u32[]{:S(2)}) collective-permute-start(bf16[1,128,1024]{2,1,0:T(8,128)(2,1)S(1)} %shard_map.112), channel_id=1, source_target_pairs={{4,0},{8,12},{5,1},{9,13},{6,2},{10,14},{7,3},{11,15},{20,16},{24,... | collective-permute-start | bytes 786440 | tf_op jit(solution)/shard_map/ppermute | solution.py:685
  79.4 12.5 %copy-start.6 = (f32[32]{0:T(128)S(1)}, f32[32]{0:T(128)}, u32[]{:S(2)}) copy-start(f32[32]{0:T(128)} %skip_ref.3) | copy-start | bytes 388
  79.4 23.4 %collective-permute-start.19 = (bf16[1,128,1024]{2,1,0:T(8,128)(2,1)S(1)}, bf16[1,128,1024]{2,1,0:T(8,128)(2,1)S(1)}, u32[]{:S(2)}, u32[]{:S(2)}) collective-permute-start(bf16[1,128,1024]{2,1,0:T(8,128)(2,1)S(1)} %shard_map.118), channel_id=1, source_target_pairs={{4,0},{8,12},{5,1},{9,13},{6,2},{10,14},{7,3},{11,15},{20,16},{24,... | collective-permute-start | bytes 786440 | tf_op jit(solution)/shard_map/ppermute | solution.py:685
  90.4 14.4 %collective-permute-start.24 = (bf16[256,256]{1,0:T(8,128)(2,1)S(1)}, bf16[256,256]{1,0:T(8,128)(2,1)S(1)}, u32[]{:S(2)}, u32[]{:S(2)}) collective-permute-start(bf16[256,256]{1,0:T(8,128)(2,1)S(1)} %shard_map.113.refs_4_), channel_id=1, source_target_pairs={{0,8},{4,12},{8,0},{12,4},{1,9},{5,13},{9,1},{13,5},{2,10},{6,14},... | collective-permute-start | bytes 393224 | tf_op jit(solution)/shard_map/ppermute | solution.py:703
  94.8 15.5 %collective-permute-start.25 = (bf16[256,256]{1,0:T(8,128)(2,1)S(1)}, bf16[256,256]{1,0:T(8,128)(2,1)S(1)}, u32[]{:S(2)}, u32[]{:S(2)}) collective-permute-start(bf16[256,256]{1,0:T(8,128)(2,1)S(1)} %shard_map.113.refs_4_), channel_id=1, source_target_pairs={{0,4},{4,8},{8,12},{12,0},{1,5},{5,9},{9,13},{13,1},{2,6},{6,10},{... | collective-permute-start | bytes 393224 | tf_op jit(solution)/shard_map/ppermute | solution.py:703
  95.5 14.8 %collective-permute-start.23 = (bf16[256,256]{1,0:T(8,128)(2,1)S(1)}, bf16[256,256]{1,0:T(8,128)(2,1)S(1)}, u32[]{:S(2)}, u32[]{:S(2)}) collective-permute-start(bf16[256,256]{1,0:T(8,128)(2,1)S(1)} %shard_map.113.refs_4_), channel_id=1, source_target_pairs={{0,12},{4,0},{8,4},{12,8},{1,13},{5,1},{9,5},{13,9},{2,14},{6,2},{... | collective-permute-start | bytes 393224 | tf_op jit(solution)/shard_map/ppermute | solution.py:703
  103.4 8.7 %collective-permute-start.22 = (bf16[256,256]{1,0:T(8,128)(2,1)S(1)}, bf16[256,256]{1,0:T(8,128)(2,1)S(1)}, u32[]{:S(2)}, u32[]{:S(2)}) collective-permute-start(bf16[256,256]{1,0:T(8,128)(2,1)S(1)} %shard_map.119.refs_4_), channel_id=1, source_target_pairs={{0,4},{4,8},{8,12},{12,0},{1,5},{5,9},{9,13},{13,1},{2,6},{6,10},{... | collective-permute-start | bytes 393224 | tf_op jit(solution)/shard_map/ppermute | solution.py:703
  103.6 9.6 %collective-permute-start.21 = (bf16[256,256]{1,0:T(8,128)(2,1)S(1)}, bf16[256,256]{1,0:T(8,128)(2,1)S(1)}, u32[]{:S(2)}, u32[]{:S(2)}) collective-permute-start(bf16[256,256]{1,0:T(8,128)(2,1)S(1)} %shard_map.119.refs_4_), channel_id=1, source_target_pairs={{0,8},{4,12},{8,0},{12,4},{1,9},{5,13},{9,1},{13,5},{2,10},{6,14},... | collective-permute-start | bytes 393224 | tf_op jit(solution)/shard_map/ppermute | solution.py:703
  104.8 8.4 %collective-permute-start.20 = (bf16[256,256]{1,0:T(8,128)(2,1)S(1)}, bf16[256,256]{1,0:T(8,128)(2,1)S(1)}, u32[]{:S(2)}, u32[]{:S(2)}) collective-permute-start(bf16[256,256]{1,0:T(8,128)(2,1)S(1)} %shard_map.119.refs_4_), channel_id=1, source_target_pairs={{0,12},{4,0},{8,4},{12,8},{1,13},{5,1},{9,5},{13,9},{2,14},{6,2},{... | collective-permute-start | bytes 393224 | tf_op jit(solution)/shard_map/ppermute | solution.py:703

commit v7 on v5

--- a/solution.py
+++ b/solution.py
@@ -639,7 +639,8 @@
     low = [lax.ppermute(hidden[rows:], axes, stays), lax.ppermute(relayed, axes, onward)]
     effective, decayed, keep = weights(master, mask_now, mask_next)
     sibling_effective = effective_of(
-        lax.ppermute(master, "sub", SWAP), lax.ppermute(mask_now, "sub", SWAP)
+        lax.ppermute(held(master, relayed), "sub", SWAP),
+        lax.ppermute(held(mask_now, relayed), "sub", SWAP),
     )
     top = held(top, effective, sibling_effective)
 

time: 115 us -> 120 us (1.043)
  starting transfers between devices: 47.3 us -> 52.3 us
    ppermute x1, starting transfers between devices: 4.9 us -> 9.09 us  [on_device(): lax.ppermute(relayed, axes, onward)]
    ppermute x1, waiting for transfers between devices: 5.87 us -> 7.26 us  [on_device(): relayed = lax.ppermute(hidden[rows:], axes, beside)]
  transfers between devices with their start and end apart: 26 -> 26, of which waited for: 8 -> 8; matrix products, arithmetic and copies ran while one was open for 1% -> 0% of each run, Pallas kernels for 17% -> 16%
where the time goes in v7:
time: 120 us
  starting transfers between devices  52.3 us (44%)
  waiting for transfers between devices  39.8 us (33%)
  Pallas kernels  21.9 us (18%)
  local copies, waits for them, and re-layouts  4.76 us (4%)
  between operations  1.21 us (1%)
    ppermute x6, waiting for transfers between devices, on_device(): arrived[p].append(lax.ppermute(message, 'seq', pairs))  21.7 us
    ppermute x6, starting transfers between devices, on_device(): arrived[p].append(lax.ppermute(message, 'seq', pairs))  10.9 us
    ppermute x1, starting transfers between devices, on_device(): lax.ppermute(same, axes, block_pairs(seq, False, True))  9.49 us
    ppermute x1, starting transfers between devices, on_device(): lax.ppermute(relayed, axes, onward)  9.09 us
    ppermute x6, starting transfers between devices, on_device(): blocks.append(lax.ppermute(payload, 'seq', to_all(seq, seq - distance)))  8.92 us
    ppermute x1, starting transfers between devices, on_device(): lax.ppermute(cross, axes, block_pairs(seq, True, False))  7.27 us
    ppermute x1, waiting for transfers between devices, on_device(): relayed = lax.ppermute(hidden[rows:], axes, beside)  7.26 us
    ppermute x1, waiting for transfers between devices, on_device(): lax.ppermute(cross, axes, block_pairs(seq, False, False))  6.9 us
  transfers between devices with their start and end apart: 26, of which 8 were waited for; matrix products, arithmetic and copies ran while one was open for 0% of the time, Pallas kernels for 16%

profile of v7, /device:TPU:0, one launch (start us, length us, event | category | flops | bytes accessed | tf_op | source)
XLA Modules:
  0.0 119.9 jit_solution(13355884839298949214)
XLA Ops:
  0.6 1.1 fusion
  1.7 1.3 %collective-permute-start.1 = (bf16[128,1024]{1,0:T(8,128)(2,1)S(1)}, bf16[128,1024]{1,0:T(8,128)(2,1)S(1)}, u32[]{:S(2)}, u32[]{:S(2)}) collective-permute-start(bf16[128,1024]{1,0:T(8,128)(2,1)S(1)} %get-tuple-element.87), channel_id=1, source_target_pairs={{1,3},{2,0},{4,6},{7,5},{9,11},{10,8},{12,14},{15,13},{17,19},{18,... | collective-permute-start | bytes 786440 | tf_op jit(solution)/shard_map/ppermute | solution.py:637
  3.0 7.3 %collective-permute-done.1 = bf16[128,1024]{1,0:T(8,128)(2,1)S(1)} collective-permute-done((bf16[128,1024]{1,0:T(8,128)(2,1)S(1)}, bf16[128,1024]{1,0:T(8,128)(2,1)S(1)}, u32[]{:S(2)}, u32[]{:S(2)}) %collective-permute-start.1) | collective-permute-done | bytes 262176 | tf_op jit(solution)/shard_map/ppermute | solution.py:637
  10.3 0.5 collective-permute-start.3
  10.8 0.7 collective-permute-start.5
  11.4 0.7 collective-permute-start
  12.1 9.1 %collective-permute-start.6 = (bf16[128,1024]{1,0:T(8,128)(2,1)S(1)}, bf16[128,1024]{1,0:T(8,128)(2,1)S(1)}, u32[]{:S(2)}, u32[]{:S(2)}) collective-permute-start(bf16[128,1024]{1,0:T(8,128)(2,1)S(1)} %collective-permute-done.1), channel_id=1, source_target_pairs={{3,7},{0,9},{6,2},{5,13},{11,6},{8,8},{14,3},{13,12},{19,23},{16,2... | collective-permute-start | bytes 786440 | tf_op jit(solution)/shard_map/ppermute | solution.py:639
  21.2 1.6 %copy-done = f32[1024,512]{1,0:T(8,128)S(1)} copy-done((f32[1024,512]{1,0:T(8,128)S(1)}, f32[1024,512]{1,0:T(8,128)}, u32[]{:S(2)}) %copy-start) | copy-done | bytes 2097176
  22.8 1.0 copy-done.3
  23.9 1.0 copy-done.4
  24.9 1.7 %shard_map.103 = (bf16[1024,512]{1,0:T(8,128)(2,1)S(1)}, f32[1024,512]{1,0:T(8,128)S(1)}, bf16[1024,512]{1,0:T(8,128)(2,1)S(1)}) custom-call(f32[1024,512]{1,0:T(8,128)S(1)} %copy-done, s32[256,512]{1,0:T(8,128)S(1)} %copy-done.4, s32[256,512]{1,0:T(8,128)S(1)} %copy-done.3), custom_call_target="tpu_custom_call" | custom-call | flops 1572864000 | bytes 7340032 | tf_op jit(solution)/shard_map/pallas_call | solution.py:77
  26.6 1.2 shard_map.104.refs_2_.refs_4_.sibling_weight_ref
  27.9 0.7 shard_map.106
  28.6 2.1 %collective-permute-start.7 = (bf16[128,1024]{1,0:T(8,128)(2,1)S(1)}, bf16[128,1024]{1,0:T(8,128)(2,1)S(1)}, u32[]{:S(2)}, u32[]{:S(2)}) collective-permute-start(bf16[128,1024]{1,0:T(8,128)(2,1)S(1)} %get-tuple-element.51.refs_1_), channel_id=1, source_target_pairs={{0,2},{2,0},{1,3},{3,1},{4,6},{6,4},{5,7},{7,5},{8,10},{10,8},{9,1... | collective-permute-start | bytes 786440 | tf_op jit(solution)/shard_map/ppermute | solution.py:649
  30.7 0.7 collective-permute-start.8
  31.4 7.3 %collective-permute-start.9 = (bf16[256,512]{1,0:T(8,128)(2,1)S(1)}, bf16[256,512]{1,0:T(8,128)(2,1)S(1)}, u32[]{:S(2)}, u32[]{:S(2)}) collective-permute-start(bf16[256,512]{1,0:T(8,128)(2,1)S(1)} %get-tuple-element.56), channel_id=1, source_target_pairs={{0,1},{1,8},{2,7},{3,14},{4,5},{5,12},{6,11},{7,2},{8,9},{9,0},{10... | collective-permute-start | bytes 786440 | tf_op jit(solution)/shard_map/ppermute | solution.py:652
  38.7 0.4 shard_map.105
  39.1 0.4 shard_map.107
  39.6 9.5 %collective-permute-start.10 = (bf16[256,512]{1,0:T(8,128)(2,1)S(1)}, bf16[256,512]{1,0:T(8,128)(2,1)S(1)}, u32[]{:S(2)}, u32[]{:S(2)}) collective-permute-start(bf16[256,512]{1,0:T(8,128)(2,1)S(1)} %get-tuple-element.52), channel_id=1, source_target_pairs={{0,4},{1,13},{2,2},{3,11},{4,8},{5,1},{6,6},{7,15},{8,12},{9,5},{1... | collective-permute-start | bytes 786440 | tf_op jit(solution)/shard_map/ppermute | solution.py:657
  49.2 5.2 %shard_map.108 = (bf16[256,2048]{1,0:T(8,128)(2,1)S(1)}, bf16[256,2048]{1,0:T(8,128)(2,1)S(1)}, bf16[2,256,256]{2,1,0:T(8,128)(2,1)S(1)}, bf16[2,256,256]{2,1,0:...) custom-call(bf16[256,2048]{1,0:T(8,128)(2,1)S(1)} %copy-done.2, ...), custom_call_target="tpu_custom_call" | custom-call | flops 5242880000 | bytes 4194304 | tf_op jit(solution)/shard_map/pallas_call | solution.py:198
  54.4 2.8 %collective-permute-done.9.refs_1_ = bf16[256,512]{1,0:T(8,128)(2,1)S(1)} collective-permute-done((bf16[256,512]{1,0:T(8,128)(2,1)S(1)}, bf16[256,512]{1,0:T(8,128)(2,1)S(1)}, u32[]{:S(2)}, u32[]{:S(2)}) %collective-permute-start.9) | collective-permute-done | bytes 262176 | tf_op jit(solution)/shard_map/ppermute | solution.py:652
  57.2 6.9 %collective-permute-done.11.refs_3_ = bf16[256,512]{1,0:T(8,128)(2,1)S(1)} collective-permute-done((bf16[256,512]{1,0:T(8,128)(2,1)S(1)}, bf16[256,512]{1,0:T(8,128)(2,1)S(1)}, u32[]{:S(2)}, u32[]{:S(2)}) %collective-permute-start.11) | collective-permute-done | bytes 262176 | tf_op jit(solution)/shard_map/ppermute | solution.py:658
  64.1 0.5 shard_map.110
  64.5 2.5 %collective-permute-start.12 = (bf16[1,128,1024]{2,1,0:T(8,128)(2,1)S(1)}, bf16[1,128,1024]{2,1,0:T(8,128)(2,1)S(1)}, u32[]{:S(2)}, u32[]{:S(2)}) collective-permute-start(bf16[1,128,1024]{2,1,0:T(8,128)(2,1)S(1)} %get-tuple-element.64), channel_id=1, source_target_pairs={{0,4},{12,8},{1,5},{13,9},{2,6},{14,10},{3,7},{15,11},{16,20},{28,... | collective-permute-start | bytes 786440 | tf_op jit(solution)/shard_map/ppermute | solution.py:686
  67.1 0.2 shard_map.116.refs_0_
  67.6 0.6 collective-permute-start.18
  68.1 0.5 shard_map.109
  68.6 3.2 %collective-permute-done.12.arrived_ref.near_ref = bf16[1,128,1024]{2,1,0:T(8,128)(2,1)S(1)} collective-permute-done((bf16[1,128,1024]{2,1,0:T(8,128)(2,1)S(1)}, bf16[1,128,1024]{2,1,0:T(8,128)(2,1)S(1)}, u32[]{:S(2)}, u32[]{:S(2)}) %collective-permute-start.12) | collective-permute-done | bytes 262176 | tf_op jit(solution)/shard_map/ppermute | solution.py:686
  71.8 4.4 %collective-permute-start.15 = (bf16[1,128,1024]{2,1,0:T(8,128)(2,1)S(1)}, bf16[1,128,1024]{2,1,0:T(8,128)(2,1)S(1)}, u32[]{:S(2)}, u32[]{:S(2)}) collective-permute-start(bf16[1,128,1024]{2,1,0:T(8,128)(2,1)S(1)} %get-tuple-element.72), channel_id=1, source_target_pairs={{0,4},{12,8},{1,5},{13,9},{2,6},{14,10},{3,7},{15,11},{16,20},{28,... | collective-permute-start | bytes 786440 | tf_op jit(solution)/shard_map/ppermute | solution.py:686
  76.3 0.7 collective-permute-start.13
  77.0 3.1 %collective-permute-done.15.arrived_ref.near_ref = bf16[1,128,1024]{2,1,0:T(8,128)(2,1)S(1)} collective-permute-done((bf16[1,128,1024]{2,1,0:T(8,128)(2,1)S(1)}, bf16[1,128,1024]{2,1,0:T(8,128)(2,1)S(1)}, u32[]{:S(2)}, u32[]{:S(2)}) %collective-permute-start.15) | collective-permute-done | bytes 262176 | tf_op jit(solution)/shard_map/ppermute | solution.py:686
  80.1 0.7 collective-permute-start.16
  80.9 1.3 %collective-permute-start.14 = (bf16[1,128,1024]{2,1,0:T(8,128)(2,1)S(1)}, bf16[1,128,1024]{2,1,0:T(8,128)(2,1)S(1)}, u32[]{:S(2)}, u32[]{:S(2)}) collective-permute-start(bf16[1,128,1024]{2,1,0:T(8,128)(2,1)S(1)} %shard_map.112), channel_id=1, source_target_pairs={{4,0},{8,12},{5,1},{9,13},{6,2},{10,14},{7,3},{11,15},{20,16},{24,... | collective-permute-start | bytes 786440 | tf_op jit(solution)/shard_map/ppermute | solution.py:686
  82.3 1.3 %collective-permute-start.19 = (bf16[1,128,1024]{2,1,0:T(8,128)(2,1)S(1)}, bf16[1,128,1024]{2,1,0:T(8,128)(2,1)S(1)}, u32[]{:S(2)}, u32[]{:S(2)}) collective-permute-start(bf16[1,128,1024]{2,1,0:T(8,128)(2,1)S(1)} %shard_map.118), channel_id=1, source_target_pairs={{4,0},{8,12},{5,1},{9,13},{6,2},{10,14},{7,3},{11,15},{20,16},{24,... | collective-permute-start | bytes 786440 | tf_op jit(solution)/shard_map/ppermute | solution.py:686
  83.6 11.2 %collective-permute-done.14.refs_1_ = bf16[1,128,1024]{2,1,0:T(8,128)(2,1)S(1)} collective-permute-done((bf16[1,128,1024]{2,1,0:T(8,128)(2,1)S(1)}, bf16[1,128,1024]{2,1,0:T(8,128)(2,1)S(1)}, u32[]{:S(2)}, u32[]{:S(2)}) %collective-permute-start.14) | collective-permute-done | bytes 262176 | tf_op jit(solution)/shard_map/ppermute | solution.py:686
  94.9 0.6 shard_map.113.refs_4_
  95.4 1.2 %collective-permute-start.24 = (bf16[256,256]{1,0:T(8,128)(2,1)S(1)}, bf16[256,256]{1,0:T(8,128)(2,1)S(1)}, u32[]{:S(2)}, u32[]{:S(2)}) collective-permute-start(bf16[256,256]{1,0:T(8,128)(2,1)S(1)} %shard_map.113.refs_4_), channel_id=1, source_target_pairs={{0,8},{4,12},{8,0},{12,4},{1,9},{5,13},{9,1},{13,5},{2,10},{6,14},... | collective-permute-start | bytes 393224 | tf_op jit(solution)/shard_map/ppermute | solution.py:704
  96.7 2.9 %shard_map.114.refs_2_ = bf16[256,2048]{1,0:T(8,128)(2,1)} custom-call(f32[32]{0:T(128)S(1)} %copy-done.6, bf16[256,2048]{1,0:T(8,128)(2,1)S(1)} %copy-done.2, f32[2,256,16]{2,1,0:T(8,128)S(1)} %get-tuple-element.78.cum_ref, f32[2,16,256]{2,1,0:T(8,128)S(1)} %get-tuple-element.69.cumt_ref, bf16[256,256]{1,0:T(8,128)(2,1)S(1)} %get-tuple-element.61.proj_ref, ...), custom_call_target="tpu_custom_call" | custom-call | flops 2097152000 | bytes 2621440 | tf_op jit(solution)/shard_map/pallas_call | solution.py:464
  99.6 0.3 collective-permute-start.25
  99.8 3.5 %collective-permute-start.23 = (bf16[256,256]{1,0:T(8,128)(2,1)S(1)}, bf16[256,256]{1,0:T(8,128)(2,1)S(1)}, u32[]{:S(2)}, u32[]{:S(2)}) collective-permute-start(bf16[256,256]{1,0:T(8,128)(2,1)S(1)} %shard_map.113.refs_4_), channel_id=1, source_target_pairs={{0,12},{4,0},{8,4},{12,8},{1,13},{5,1},{9,5},{13,9},{2,14},{6,2},{... | collective-permute-start | bytes 393224 | tf_op jit(solution)/shard_map/ppermute | solution.py:704
  103.4 4.2 %collective-permute-done.19.refs_1_ = bf16[1,128,1024]{2,1,0:T(8,128)(2,1)S(1)} collective-permute-done((bf16[1,128,1024]{2,1,0:T(8,128)(2,1)S(1)}, bf16[1,128,1024]{2,1,0:T(8,128)(2,1)S(1)}, u32[]{:S(2)}, u32[]{:S(2)}) %collective-permute-start.19) | collective-permute-done | bytes 262176 | tf_op jit(solution)/shard_map/ppermute | solution.py:686
  107.6 0.6 shard_map.119.refs_4_
  108.2 1.3 %collective-permute-start.21 = (bf16[256,256]{1,0:T(8,128)(2,1)S(1)}, bf16[256,256]{1,0:T(8,128)(2,1)S(1)}, u32[]{:S(2)}, u32[]{:S(2)}) collective-permute-start(bf16[256,256]{1,0:T(8,128)(2,1)S(1)} %shard_map.119.refs_4_), channel_id=1, source_target_pairs={{0,8},{4,12},{8,0},{12,4},{1,9},{5,13},{9,1},{13,5},{2,10},{6,14},... | collective-permute-start | bytes 393224 | tf_op jit(solution)/shard_map/ppermute | solution.py:704
  109.6 2.5 %collective-permute-start.20 = (bf16[256,256]{1,0:T(8,128)(2,1)S(1)}, bf16[256,256]{1,0:T(8,128)(2,1)S(1)}, u32[]{:S(2)}, u32[]{:S(2)}) collective-permute-start(bf16[256,256]{1,0:T(8,128)(2,1)S(1)} %shard_map.119.refs_4_), channel_id=1, source_target_pairs={{0,12},{4,0},{8,4},{12,8},{1,13},{5,1},{9,5},{13,9},{2,14},{6,2},{... | collective-permute-start | bytes 393224 | tf_op jit(solution)/shard_map/ppermute | solution.py:704
  112.0 3.0 %shard_map.120 = bf16[256,2048]{1,0:T(8,128)(2,1)} custom-call(f32[32]{0:T(128)S(1)} %copy-done.6, bf16[256,2048]{1,0:T(8,128)(2,1)S(1)} %copy-done.2, f32[2,256,16]{2,1,0:T(8,128)S(1)} %get-tuple-element.78.cum_ref, f32[2,16,256]{2,1,0:T(8,128)S(1)} %get-tuple-element.69.cumt_ref, ...), custom_call_target="tpu_custom_call", output_to_operand_aliasing={{}: (8, {})} | custom-call | flops 2097152000 | bytes 2621440 | tf_op jit(solution)/shard_map/pallas_call | solution.py:464
  115.1 1.8 %shard_map.121 = (f32[1024,512]{1,0:T(8,128)}, bf16[1024,512]{1,0:T(8,128)(2,1)}) custom-call(bf16[1024,256]{1,0:T(8,128)(2,1)S(1)} %shard_map.116.refs_0_, bf16[1024,256]{1,0:T(8,128)(2,1)S(1)} %collective-permute-done.17.refs_1_, bf16[1024,256]{1,0:T(8,128)(2,1)S(1)} %shard_map.117.refs_2_, bf16[1024,256]{1,0:T(8,128)(2,1)S(1)} %collective-permute-done.18.refs_3_, ...), custom_call_target="tpu_custom_call" | custom-call | flops 536870912 | bytes 5767168 | tf_op jit(solution)/shard_map/pallas_call | solution.py:535
  116.9 1.1 collective-permute-done.21.refs_6_
  118.0 1.8 %shard_map.122 = (f32[1024,512]{1,0:T(8,128)}, bf16[1024,512]{1,0:T(8,128)(2,1)}) custom-call(bf16[1024,256]{1,0:T(8,128)(2,1)S(1)} %shard_map.116.refs_0_, bf16[1024,256]{1,0:T(8,128)(2,1)S(1)} %collective-permute-done.17.refs_1_, bf16[1024,256]{1,0:T(8,128)(2,1)S(1)} %shard_map.117.refs_2_, ...), custom_call_target="tpu_custom_call", output_to_operand_aliasing={{0}: (10, {}), {1}: (11, {})} | custom-call | flops 536870912 | bytes 5767168 | tf_op jit(solution)/shard_map/pallas_call | solution.py:535
  (39 shorter events, 0.8 us)
Async XLA Ops:
  1.7 8.6 %collective-permute-start.1 = (bf16[128,1024]{1,0:T(8,128)(2,1)S(1)}, bf16[128,1024]{1,0:T(8,128)(2,1)S(1)}, u32[]{:S(2)}, u32[]{:S(2)}) collective-permute-start(bf16[128,1024]{1,0:T(8,128)(2,1)S(1)} %get-tuple-element.87), channel_id=1, source_target_pairs={{1,3},{2,0},{4,6},{7,5},{9,11},{10,8},{12,14},{15,13},{17,19},{18,... | collective-permute-start | bytes 786440 | tf_op jit(solution)/shard_map/ppermute | solution.py:637
  10.3 16.3 %collective-permute-start.2 = (f32[1024,512]{1,0:T(8,128)}, f32[1024,512]{1,0:T(8,128)S(1)}, u32[]{:S(2)}, u32[]{:S(2)}) collective-permute-start(f32[1024,512]{1,0:T(8,128)} %master_ref.1), channel_id=1, source_target_pairs={{0,1},{1,0},{2,3},{3,2},{4,5},{5,4},{6,7},{7,6},{8,9},{9,8},{10,11... | collective-permute-start | bytes 6291464 | tf_op jit(solution)/shard_map/ppermute | solution.py:642
  10.3 16.3 %collective-permute-start.3 = (s32[256,512]{1,0:T(8,128)}, s32[256,512]{1,0:T(8,128)S(1)}, u32[]{:S(2)}, u32[]{:S(2)}) collective-permute-start(s32[256,512]{1,0:T(8,128)} %now_ref.1), channel_id=1, source_target_pairs={{0,1},{1,0},{2,3},{3,2},{4,5},{5,4},{6,7},{7,6},{8,9},{9,8},{10,11... | collective-permute-start | bytes 1572872 | tf_op jit(solution)/shard_map/ppermute | solution.py:643
  10.8 17.1 %collective-permute-start.5 = (bf16[128,1024]{1,0:T(8,128)(2,1)S(1)}, bf16[128,1024]{1,0:T(8,128)(2,1)S(1)}, u32[]{:S(2)}, u32[]{:S(2)}) collective-permute-start(bf16[128,1024]{1,0:T(8,128)(2,1)S(1)} %get-tuple-element.87), channel_id=1, source_target_pairs={{0,0},{3,14},{5,4},{6,11},{8,1},{11,15},{13,5},{14,10},{16,16},{19... | collective-permute-start | bytes 786440 | tf_op jit(solution)/shard_map/ppermute | solution.py:639
  11.4 16.3 %collective-permute-start = (bf16[128,1024]{1,0:T(8,128)(2,1)S(1)}, bf16[128,1024]{1,0:T(8,128)(2,1)S(1)}, u32[]{:S(2)}, u32[]{:S(2)}) collective-permute-start(bf16[128,1024]{1,0:T(8,128)(2,1)S(1)} %get-tuple-element.88), channel_id=1, source_target_pairs={{0,0},{3,14},{5,4},{6,11},{8,1},{11,15},{13,5},{14,10},{1,7},{2,9}... | collective-permute-start | bytes 786440 | tf_op jit(solution)/shard_map/ppermute | solution.py:638
  12.1 15.8 %collective-permute-start.6 = (bf16[128,1024]{1,0:T(8,128)(2,1)S(1)}, bf16[128,1024]{1,0:T(8,128)(2,1)S(1)}, u32[]{:S(2)}, u32[]{:S(2)}) collective-permute-start(bf16[128,1024]{1,0:T(8,128)(2,1)S(1)} %collective-permute-done.1), channel_id=1, source_target_pairs={{3,7},{0,9},{6,2},{5,13},{11,6},{8,8},{14,3},{13,12},{19,23},{16,2... | collective-permute-start | bytes 786440 | tf_op jit(solution)/shard_map/ppermute | solution.py:639
  21.2 1.6 %copy-start = (f32[1024,512]{1,0:T(8,128)S(1)}, f32[1024,512]{1,0:T(8,128)}, u32[]{:S(2)}) copy-start(f32[1024,512]{1,0:T(8,128)} %master_ref.1) | copy-start | bytes 6291460
  22.8 1.0 copy-start.3
  23.9 1.0 copy-start.4
  27.8 10.9 %collective-permute-start.4 = (bf16[128,1024]{1,0:T(8,128)(2,1)S(1)}, bf16[128,1024]{1,0:T(8,128)(2,1)S(1)}, u32[]{:S(2)}, u32[]{:S(2)}) collective-permute-start(bf16[128,1024]{1,0:T(8,128)(2,1)S(1)} %collective-permute-done.refs_0_), channel_id=1, source_target_pairs={{0,2},{2,0},{1,3},{3,1},{4,6},{6,4},{5,7},{7,5},{8,10},{10,8},{9,1... | collective-permute-start | bytes 786440 | tf_op jit(solution)/shard_map/ppermute | solution.py:647
  28.6 10.5 %collective-permute-start.7 = (bf16[128,1024]{1,0:T(8,128)(2,1)S(1)}, bf16[128,1024]{1,0:T(8,128)(2,1)S(1)}, u32[]{:S(2)}, u32[]{:S(2)}) collective-permute-start(bf16[128,1024]{1,0:T(8,128)(2,1)S(1)} %get-tuple-element.51.refs_1_), channel_id=1, source_target_pairs={{0,2},{2,0},{1,3},{3,1},{4,6},{6,4},{5,7},{7,5},{8,10},{10,8},{9,1... | collective-permute-start | bytes 786440 | tf_op jit(solution)/shard_map/ppermute | solution.py:649
  30.7 23.7 %collective-permute-start.8 = (bf16[256,512]{1,0:T(8,128)(2,1)S(1)}, bf16[256,512]{1,0:T(8,128)(2,1)S(1)}, u32[]{:S(2)}, u32[]{:S(2)}) collective-permute-start(bf16[256,512]{1,0:T(8,128)(2,1)S(1)} %get-tuple-element.55), channel_id=1, source_target_pairs={{0,0},{1,9},{2,6},{3,15},{4,4},{5,13},{6,10},{7,3},{8,8},{9,1},{10... | collective-permute-start | bytes 786440 | tf_op jit(solution)/shard_map/ppermute | solution.py:651
  31.4 17.8 %copy-start.1 = (bf16[256,2048]{1,0:T(8,128)(2,1)S(1)}, bf16[256,2048]{1,0:T(8,128)(2,1)}, u32[]{:S(2)}) copy-start(bf16[256,2048]{1,0:T(8,128)(2,1)} %dy_ref.1) | copy-start | bytes 3145732
  31.4 17.8 %copy-start.2 = (bf16[256,2048]{1,0:T(8,128)(2,1)S(1)}, bf16[256,2048]{1,0:T(8,128)(2,1)}, u32[]{:S(2)}) copy-start(bf16[256,2048]{1,0:T(8,128)(2,1)} %x_ref.4) | copy-start | bytes 3145732
  31.4 17.8 %copy-start.5 = (f32[256,32]{0,1:T(8,128)S(1)}, f32[256,32]{0,1:T(8,128)}, u32[]{:S(2)}) copy-start(f32[256,32]{0,1:T(8,128)} %param.10) | copy-start | bytes 98308
  31.4 25.8 %collective-permute-start.9 = (bf16[256,512]{1,0:T(8,128)(2,1)S(1)}, bf16[256,512]{1,0:T(8,128)(2,1)S(1)}, u32[]{:S(2)}, u32[]{:S(2)}) collective-permute-start(bf16[256,512]{1,0:T(8,128)(2,1)S(1)} %get-tuple-element.56), channel_id=1, source_target_pairs={{0,1},{1,8},{2,7},{3,14},{4,5},{5,12},{6,11},{7,2},{8,9},{9,0},{10... | collective-permute-start | bytes 786440 | tf_op jit(solution)/shard_map/ppermute | solution.py:652
  39.6 24.5 %collective-permute-start.10 = (bf16[256,512]{1,0:T(8,128)(2,1)S(1)}, bf16[256,512]{1,0:T(8,128)(2,1)S(1)}, u32[]{:S(2)}, u32[]{:S(2)}) collective-permute-start(bf16[256,512]{1,0:T(8,128)(2,1)S(1)} %get-tuple-element.52), channel_id=1, source_target_pairs={{0,4},{1,13},{2,2},{3,11},{4,8},{5,1},{6,6},{7,15},{8,12},{9,5},{1... | collective-permute-start | bytes 786440 | tf_op jit(solution)/shard_map/ppermute | solution.py:657
  49.1 15.0 %collective-permute-start.11 = (bf16[256,512]{1,0:T(8,128)(2,1)S(1)}, bf16[256,512]{1,0:T(8,128)(2,1)S(1)}, u32[]{:S(2)}, u32[]{:S(2)}) collective-permute-start(bf16[256,512]{1,0:T(8,128)(2,1)S(1)} %get-tuple-element.57), channel_id=1, source_target_pairs={{0,5},{1,12},{2,3},{3,10},{4,9},{5,0},{6,7},{7,14},{8,13},{9,4},{1... | collective-permute-start | bytes 786440 | tf_op jit(solution)/shard_map/ppermute | solution.py:658
  64.5 7.3 %collective-permute-start.12 = (bf16[1,128,1024]{2,1,0:T(8,128)(2,1)S(1)}, bf16[1,128,1024]{2,1,0:T(8,128)(2,1)S(1)}, u32[]{:S(2)}, u32[]{:S(2)}) collective-permute-start(bf16[1,128,1024]{2,1,0:T(8,128)(2,1)S(1)} %get-tuple-element.64), channel_id=1, source_target_pairs={{0,4},{12,8},{1,5},{13,9},{2,6},{14,10},{3,7},{15,11},{16,20},{28,... | collective-permute-start | bytes 786440 | tf_op jit(solution)/shard_map/ppermute | solution.py:686
  67.3 14.9 %collective-permute-start.17 = (bf16[1024,256]{1,0:T(8,128)(2,1)S(1)}, bf16[1024,256]{1,0:T(8,128)(2,1)S(1)}, u32[]{:S(2)}, u32[]{:S(2)}) collective-permute-start(bf16[1024,256]{1,0:T(8,128)(2,1)S(1)} %shard_map.116.refs_0_), channel_id=1, source_target_pairs={{0,1},{1,0},{2,3},{3,2},{4,5},{5,4},{6,7},{7,6},{8,9},{9,8},{10,11... | collective-permute-start | bytes 1572872 | tf_op jit(solution)/shard_map/ppermute | solution.py:676
  67.6 14.7 %collective-permute-start.18 = (bf16[1024,256]{1,0:T(8,128)(2,1)S(1)}, bf16[1024,256]{1,0:T(8,128)(2,1)S(1)}, u32[]{:S(2)}, u32[]{:S(2)}) collective-permute-start(bf16[1024,256]{1,0:T(8,128)(2,1)S(1)} %shard_map.117.refs_2_), channel_id=1, source_target_pairs={{0,1},{1,0},{2,3},{3,2},{4,5},{5,4},{6,7},{7,6},{8,9},{9,8},{10,11... | collective-permute-start | bytes 1572872 | tf_op jit(solution)/shard_map/ppermute | solution.py:676
  71.8 8.3 %collective-permute-start.15 = (bf16[1,128,1024]{2,1,0:T(8,128)(2,1)S(1)}, bf16[1,128,1024]{2,1,0:T(8,128)(2,1)S(1)}, u32[]{:S(2)}, u32[]{:S(2)}) collective-permute-start(bf16[1,128,1024]{2,1,0:T(8,128)(2,1)S(1)} %get-tuple-element.72), channel_id=1, source_target_pairs={{0,4},{12,8},{1,5},{13,9},{2,6},{14,10},{3,7},{15,11},{16,20},{28,... | collective-permute-start | bytes 786440 | tf_op jit(solution)/shard_map/ppermute | solution.py:686
  76.3 4.5 %collective-permute-start.13 = (bf16[1,128,1024]{2,1,0:T(8,128)(2,1)S(1)}, bf16[1,128,1024]{2,1,0:T(8,128)(2,1)S(1)}, u32[]{:S(2)}, u32[]{:S(2)}) collective-permute-start(bf16[1,128,1024]{2,1,0:T(8,128)(2,1)S(1)} %shard_map.111), channel_id=1, source_target_pairs={{4,8},{8,4},{5,9},{9,5},{6,10},{10,6},{7,11},{11,7},{20,24},{24,20... | collective-permute-start | bytes 786440 | tf_op jit(solution)/shard_map/ppermute | solution.py:686
  80.1 2.1 %collective-permute-start.16 = (bf16[1,128,1024]{2,1,0:T(8,128)(2,1)S(1)}, bf16[1,128,1024]{2,1,0:T(8,128)(2,1)S(1)}, u32[]{:S(2)}, u32[]{:S(2)}) collective-permute-start(bf16[1,128,1024]{2,1,0:T(8,128)(2,1)S(1)} %shard_map.115), channel_id=1, source_target_pairs={{4,8},{8,4},{5,9},{9,5},{6,10},{10,6},{7,11},{11,7},{20,24},{24,20... | collective-permute-start | bytes 786440 | tf_op jit(solution)/shard_map/ppermute | solution.py:686
  80.9 13.9 %collective-permute-start.14 = (bf16[1,128,1024]{2,1,0:T(8,128)(2,1)S(1)}, bf16[1,128,1024]{2,1,0:T(8,128)(2,1)S(1)}, u32[]{:S(2)}, u32[]{:S(2)}) collective-permute-start(bf16[1,128,1024]{2,1,0:T(8,128)(2,1)S(1)} %shard_map.112), channel_id=1, source_target_pairs={{4,0},{8,12},{5,1},{9,13},{6,2},{10,14},{7,3},{11,15},{20,16},{24,... | collective-permute-start | bytes 786440 | tf_op jit(solution)/shard_map/ppermute | solution.py:686
  82.3 14.4 %copy-start.6 = (f32[32]{0:T(128)S(1)}, f32[32]{0:T(128)}, u32[]{:S(2)}) copy-start(f32[32]{0:T(128)} %skip_ref.3) | copy-start | bytes 388
  82.3 25.2 %collective-permute-start.19 = (bf16[1,128,1024]{2,1,0:T(8,128)(2,1)S(1)}, bf16[1,128,1024]{2,1,0:T(8,128)(2,1)S(1)}, u32[]{:S(2)}, u32[]{:S(2)}) collective-permute-start(bf16[1,128,1024]{2,1,0:T(8,128)(2,1)S(1)} %shard_map.118), channel_id=1, source_target_pairs={{4,0},{8,12},{5,1},{9,13},{6,2},{10,14},{7,3},{11,15},{20,16},{24,... | collective-permute-start | bytes 786440 | tf_op jit(solution)/shard_map/ppermute | solution.py:686
  95.4 14.1 %collective-permute-start.24 = (bf16[256,256]{1,0:T(8,128)(2,1)S(1)}, bf16[256,256]{1,0:T(8,128)(2,1)S(1)}, u32[]{:S(2)}, u32[]{:S(2)}) collective-permute-start(bf16[256,256]{1,0:T(8,128)(2,1)S(1)} %shard_map.113.refs_4_), channel_id=1, source_target_pairs={{0,8},{4,12},{8,0},{12,4},{1,9},{5,13},{9,1},{13,5},{2,10},{6,14},... | collective-permute-start | bytes 393224 | tf_op jit(solution)/shard_map/ppermute | solution.py:704
  99.6 15.5 %collective-permute-start.25 = (bf16[256,256]{1,0:T(8,128)(2,1)S(1)}, bf16[256,256]{1,0:T(8,128)(2,1)S(1)}, u32[]{:S(2)}, u32[]{:S(2)}) collective-permute-start(bf16[256,256]{1,0:T(8,128)(2,1)S(1)} %shard_map.113.refs_4_), channel_id=1, source_target_pairs={{0,4},{4,8},{8,12},{12,0},{1,5},{5,9},{9,13},{13,1},{2,6},{6,10},{... | collective-permute-start | bytes 393224 | tf_op jit(solution)/shard_map/ppermute | solution.py:704
  99.8 15.2 %collective-permute-start.23 = (bf16[256,256]{1,0:T(8,128)(2,1)S(1)}, bf16[256,256]{1,0:T(8,128)(2,1)S(1)}, u32[]{:S(2)}, u32[]{:S(2)}) collective-permute-start(bf16[256,256]{1,0:T(8,128)(2,1)S(1)} %shard_map.113.refs_4_), channel_id=1, source_target_pairs={{0,12},{4,0},{8,4},{12,8},{1,13},{5,1},{9,5},{13,9},{2,14},{6,2},{... | collective-permute-start | bytes 393224 | tf_op jit(solution)/shard_map/ppermute | solution.py:704
  108.2 8.7 %collective-permute-start.22 = (bf16[256,256]{1,0:T(8,128)(2,1)S(1)}, bf16[256,256]{1,0:T(8,128)(2,1)S(1)}, u32[]{:S(2)}, u32[]{:S(2)}) collective-permute-start(bf16[256,256]{1,0:T(8,128)(2,1)S(1)} %shard_map.119.refs_4_), channel_id=1, source_target_pairs={{0,4},{4,8},{8,12},{12,0},{1,5},{5,9},{9,13},{13,1},{2,6},{6,10},{... | collective-permute-start | bytes 393224 | tf_op jit(solution)/shard_map/ppermute | solution.py:704
  108.2 9.8 %collective-permute-start.21 = (bf16[256,256]{1,0:T(8,128)(2,1)S(1)}, bf16[256,256]{1,0:T(8,128)(2,1)S(1)}, u32[]{:S(2)}, u32[]{:S(2)}) collective-permute-start(bf16[256,256]{1,0:T(8,128)(2,1)S(1)} %shard_map.119.refs_4_), channel_id=1, source_target_pairs={{0,8},{4,12},{8,0},{12,4},{1,9},{5,13},{9,1},{13,5},{2,10},{6,14},... | collective-permute-start | bytes 393224 | tf_op jit(solution)/shard_map/ppermute | solution.py:704
  109.6 8.4 %collective-permute-start.20 = (bf16[256,256]{1,0:T(8,128)(2,1)S(1)}, bf16[256,256]{1,0:T(8,128)(2,1)S(1)}, u32[]{:S(2)}, u32[]{:S(2)}) collective-permute-start(bf16[256,256]{1,0:T(8,128)(2,1)S(1)} %shard_map.119.refs_4_), channel_id=1, source_target_pairs={{0,12},{4,0},{8,4},{12,8},{1,13},{5,1},{9,5},{13,9},{2,14},{6,2},{... | collective-permute-start | bytes 393224 | tf_op jit(solution)/shard_map/ppermute | solution.py:704
